TPU v7x, 32 devices: a whole 2x2x4 slice. The times are simulated.
32 devices in a mesh: groups: 2 (over y), rows: 4 (over x, core), cols: 4 (over z).
Axes of the slice: x: 2, y: 2, z: 4, core: 2. Of those that a mesh axis runs over, the one named last changes fastest.
Arguments:
- features: bfloat16 [4096, 256], P(('groups', 'rows', 'cols')), parts along dimension 0, may hold values from -6 to 6
- degree: int32 [4096], P(('groups', 'rows', 'cols')), parts along dimension 0, may hold values from 1 to 8
- weight: bfloat16 [256, 256], replicated, may hold values from -0.375 to 0.375
- tile_index: int32 [8, 4, 2, 8], P(('groups', 'rows'), 'cols'), parts along dimension 0, may hold values from 0 to 3, as said below
- tile_values: bfloat16 [8, 4, 8, 128, 128], P(('groups', 'rows'), 'cols'), parts along dimension 0, may hold values from -0.25 to 0.25
- tile_count: int32 [8, 4], P(('groups', 'rows'), 'cols'), parts along dimension 0, may hold values from 1 to 8, as said below
- cotangent: bfloat16 [4096, 256], P(('groups', 'rows', 'cols')), parts along dimension 0, may hold values from -6 to 6
Outputs:
- activated: bfloat16 [4096, 256], P(('groups', 'rows', 'cols')), parts along dimension 0
- input_grad: bfloat16 [4096, 256], P(('groups', 'rows', 'cols')), parts along dimension 0
- weight_grad: float32 [512, 256], P('groups'), parts along dimension 0
There are 2 independent parts, one for each index of `groups`. A program takes and returns all parts, laid end to end along the dimension named above; an argument that names none is the same for every part. Nothing has to cross between parts.
Inputs may be any that keep to these rules, and one draw needn't show every extreme that they name: `tile_index`: tile rows lie below 4 and tile columns below 4; slots at or past a block's tile_count hold no tile, whatever they contain. `tile_count`: some block uses all 8 slots.
All inputs are finite; a program needn't handle non-finite values.
Results may differ from a plain program's by a relative error of at most 0.015.
Values may be sent and summed in bfloat16 or wider, within the bound.
No kernel may reach another device: no remote copies, remote signals or barrier semaphores. Data moves between devices by JAX's collectives and lax.ppermute only.
A program may use at most 64 MiB of HBM per device.

v0:
```python
import math

import jax
import jax.numpy as jnp
from jax import lax
from jax.sharding import PartitionSpec as P


def place_tiles(values, take_idx, put_idx, used_count, source, out_tiles, transposed):
    width = source.shape[1]
    group_size = values.shape[0]
    source_tiles = source.reshape(-1, 128, width)
    picked = jnp.take(source_tiles, take_idx, axis=0)
    einsum_form = "kba,kbf->kaf" if transposed else "kab,kbf->kaf"
    products = jnp.einsum(einsum_form, values, picked, preferred_element_type=jnp.float32)
    high_part = products.astype(jnp.bfloat16)
    low_part = (products - high_part.astype(jnp.float32)).astype(jnp.bfloat16)
    live_mask = jnp.arange(group_size, dtype=jnp.int32) < used_count
    onehot = (
        (put_idx[None, :] == jnp.arange(out_tiles, dtype=jnp.int32)[:, None]) & live_mask[None, :]
    ).astype(jnp.bfloat16)
    placed_high = jnp.einsum("rk,kaf->raf", onehot, high_part, preferred_element_type=jnp.float32)
    placed_low = jnp.einsum("rk,kaf->raf", onehot, low_part, preferred_element_type=jnp.float32)
    return (placed_high + placed_low).reshape(out_tiles * 128, width)


def apply_tiles(values, take_idx, put_idx, used_count, source, out_tiles, transposed):
    return place_tiles(values, take_idx, put_idx, used_count, source, out_tiles, transposed)


def silu_parts(pre_act, cot_rows):
    sig = jax.nn.sigmoid(pre_act)
    slope_grad = (cot_rows.astype(jnp.float32) * sig * (1.0 + pre_act * (1.0 - sig))).astype(
        jnp.bfloat16
    )
    return (sig, slope_grad)


def back_rows(act_grad, weight, root_rows):
    back_pre = lax.dot_general(
        act_grad, weight, (((1,), (1,)), ((), ())), preferred_element_type=jnp.float32
    )
    return (root_rows[:, None] * back_pre).astype(jnp.bfloat16)


def shards(features, degree, weight, tile_index, tile_values, tile_count, cotangent):
    rows_dev = features.shape[0]
    row_devs = lax.axis_size("rows")
    col_devs = lax.axis_size("cols")
    coords = tile_index[0, 0]
    values = tile_values[0, 0]
    used_count = tile_count[0, 0]
    inv_root = lax.rsqrt(degree.astype(jnp.float32))
    scaled = (inv_root[:, None] * features.astype(jnp.float32)).astype(jnp.bfloat16)
    feature_panel = lax.all_gather(scaled, "rows", axis=0, tiled=True)
    row_tiles = col_devs * rows_dev // 128
    col_tiles = row_devs * rows_dev // 128
    partial_value = apply_tiles(
        values, coords[1], coords[0], used_count, feature_panel, row_tiles, False
    )
    row_sums = lax.psum_scatter(
        partial_value.astype(jnp.bfloat16), "cols", scatter_dimension=0, tiled=True
    ).astype(jnp.float32)
    own_agg = (inv_root[:, None] * row_sums).astype(jnp.bfloat16)
    own_pre = jnp.dot(own_agg, weight, preferred_element_type=jnp.float32)
    own_sig, own_grad = silu_parts(own_pre, cotangent)
    activated = (own_pre * own_sig).astype(jnp.bfloat16)
    own_spread = back_rows(own_grad, weight, inv_root)
    grad_panel = lax.all_gather(own_spread, "cols", axis=0, tiled=True)
    column_partial = apply_tiles(
        values, coords[0], coords[1], used_count, grad_panel, col_tiles, True
    )
    column_sums = lax.psum_scatter(
        column_partial.astype(jnp.bfloat16), "rows", scatter_dimension=0, tiled=True
    ).astype(jnp.float32)
    input_grad = (inv_root[:, None] * column_sums).astype(jnp.bfloat16)
    weight_term = lax.dot_general(
        own_agg, own_grad, (((0,), (0,)), ((), ())), preferred_element_type=jnp.float32
    )
    node_total = rows_dev * row_devs * col_devs
    weight_grad = lax.psum(weight_term, ("rows", "cols")) / math.sqrt(node_total)
    return (activated, input_grad, weight_grad)


def solution(mesh):
    placed = (
        P(("groups", "rows", "cols"), None),
        P(("groups", "rows", "cols")),
        P(),
        P(("groups", "rows"), "cols", None, None),
        P(("groups", "rows"), "cols", None, None, None),
        P(("groups", "rows"), "cols"),
        P(("groups", "rows", "cols"), None),
    )
    return jax.shard_map(
        shards,
        mesh=mesh,
        in_specs=placed,
        out_specs=(
            P(("groups", "rows", "cols"), None),
            P(("groups", "rows", "cols"), None),
            P("groups", None),
        ),
        check_vma=False,
    )
```

profile of v0, /device:TPU:0, one launch (start us, length us, event | category | flops | bytes accessed | tf_op | source)
XLA Modules:
  0.0 179.2 jit_solution(4962425680324988107)
XLA Ops:
  7.2 0.7 compare_and_fusion
  8.0 0.6 copy-done.5
  8.6 0.9 multiply_convert_fusion.4
  9.6 7.2 %all_gather.6 = bf16[512,256]{1,0:T(8,128)(2,1)S(1)} all-gather(bf16[128,256]{1,0:T(8,128)(2,1)S(1)} %multiply_convert_fusion.4), channel_id=1, replica_groups=mesh['groups'=2,'rows'=4,'cols'=4] {'rows'}, dimensions={0}, use_global_device_ids=true | all-gather | bytes 327680 | tf_op jit(solution)/shard_map/all_gather | solution.py:55
  16.8 0.6 gather_fusion
  17.4 0.4 subtract_convert_fusion.1
  17.8 0.4 copy.16
  18.9 0.4 copy.17
  19.9 0.7 copy.18
  20.7 21.0 %reduce-scatter.3.cloned.1.call-done = bf16[128,256]{1,0:T(8,128)(2,1)} async-done(((bf16[512,256]{1,0:T(8,128)(2,1)}), bf16[128,256]{1,0:T(8,128)(2,1)}) %reduce-scatter.3.cloned.1.call-update) | async-done | bytes 65552 | tf_op jit(solution)/shard_map/reduce_scatter | solution.py:61
  41.8 1.7 multiply_convert_fusion.2
  43.7 13.9 %all_gather.7 = bf16[512,256]{1,0:T(8,128)(2,1)S(1)} all-gather(bf16[128,256]{1,0:T(8,128)(2,1)S(1)} %fusion.2), channel_id=1, replica_groups=mesh['groups'=2,'rows'=4,'cols'=4] {'cols'}, dimensions={0}, use_global_device_ids=true | all-gather | bytes 327680 | tf_op jit(solution)/shard_map/all_gather | solution.py:69
  57.6 0.6 gather_fusion.1
  58.2 0.4 subtract_convert_fusion
  58.6 0.4 copy.20
  59.0 0.4 copy.21
  59.4 0.4 copy-done.4
  59.8 1.0 fusion.11
  61.2 0.3 fusion.1
  61.5 0.7 copy.22
  62.2 85.7 %all-reduce.2.cloned.1.call-done = f32[256,256]{1,0:T(8,128)} async-done(((f32[256,256]{1,0:T(8,128)}), f32[256,256]{1,0:T(8,128)}) %all-reduce.2.cloned.1.call-update) | async-done | bytes 262160 | tf_op jit(solution)/shard_map/psum | solution.py:81
  148.0 1.7 broadcast_multiply_fusion
  149.6 21.5 %reduce-scatter.5.cloned.1.call-done = bf16[128,256]{1,0:T(8,128)(2,1)} async-done(((bf16[512,256]{1,0:T(8,128)(2,1)}), bf16[128,256]{1,0:T(8,128)(2,1)}) %reduce-scatter.5.cloned.1.call-update) | async-done | bytes 65552 | tf_op jit(solution)/shard_map/reduce_scatter | solution.py:73
  171.1 1.6 multiply_convert_fusion
  (25 shorter events, 1.3 us)
Async XLA Ops:
  7.2 10.2 %copy-start = (bf16[1,1,8,128,128]{4,3,2,1,0:T(8,128)(2,1)S(1)}, bf16[1,1,8,128,128]{4,3,2,1,0:T(8,128)(2,1)}, u32[]{:S(2)}) copy-start(bf16[1,1,8,128,128]{4,3,2,1,0:T(8,128)(2,1)} %param.13) | copy-start | bytes 786436
  7.2 0.8 copy-start.1
  7.2 34.6 %reduce-scatter.3.cloned.1.call-start = ((), (), s32[]{:S(2)}) async-start(), calls=%async_computation.2 | async-start | bytes 327680 | tf_op jit(solution)/shard_map/reduce_scatter | solution.py:61
  8.0 0.7 copy-start.5
  20.6 21.1 %copy-start.2 = (bf16[256,256]{1,0:T(8,128)(2,1)S(1)}, bf16[256,256]{1,0:T(8,128)(2,1)}, u32[]{:S(2)}) copy-start(bf16[256,256]{1,0:T(8,128)(2,1)} %param.11) | copy-start | bytes 393220
  20.6 127.3 %all-reduce.2.cloned.1.call-start = ((), (), s32[]{:S(2)}) async-start(), calls=%async_computation.4 | async-start | bytes 524288 | tf_op jit(solution)/shard_map/psum | solution.py:81
  20.7 22.8 %copy-start.3 = (bf16[128,256]{1,0:T(8,128)(2,1)S(1)}, bf16[128,256]{1,0:T(8,128)(2,1)}, u32[]{:S(2)}) copy-start(bf16[128,256]{1,0:T(8,128)(2,1)} %param.15) | copy-start | bytes 196612
  59.0 0.8 copy-start.4
  60.8 110.3 %reduce-scatter.5.cloned.1.call-start = ((), (), s32[]{:S(2)}) async-start(), calls=%async_computation.3 | async-start | bytes 327680 | tf_op jit(solution)/shard_map/reduce_scatter | solution.py:73
Sparse Core Ops, SparseCore 0:
  20.8 20.9 reduce-scatter.2
  61.0 86.9 all-reduce.1
  150.6 20.5 reduce-scatter.4
where the time goes:
time: 180 us; the launch traced here: 179 us
  waiting for transfers between devices  128 us (71%)
  blocking collectives  21.1 us (12%)
  between operations  14.6 us (8%)
  local copies, waits for them, and re-layouts  5.31 us (3%)
  other arithmetic  4.92 us (3%)
  matrix products  4.89 us (3%)
    psum x1, waiting for transfers between devices, shards(): lax.psum(weight_term, ('rows', 'cols')) / math.sqrt(node_total)  85.7 us
    reduce_scatter x1, waiting for transfers between devices, shards(): lax.psum_scatter(column_partial.astype(jnp.bfloat16), 'rows', scatter_dim...  21.5 us
    reduce_scatter x1, waiting for transfers between devices, shards(): lax.psum_scatter(partial_value.astype(jnp.bfloat16), 'cols', scatter_dime...  21 us
    all_gather x1, blocking collectives, shards(): grad_panel = lax.all_gather(own_spread, 'cols', axis=0, tiled=True)  13.9 us
    all_gather x1, blocking collectives, shards(): feature_panel = lax.all_gather(scaled, 'rows', axis=0, tiled=True)  7.19 us
  transfers between devices with their start and end apart: 3, of which 3 were waited for; matrix products, arithmetic and copies ran while one was open for 2% of the time, Pallas kernels for 0%

commit v1 on v0

v1 whole, which is shorter than its diff:
```python
import functools
import math

import jax
import jax.numpy as jnp
from jax import lax
from jax.experimental import pallas as pl
from jax.experimental.pallas import tpu as pltpu
from jax.sharding import PartitionSpec as P

TILE = 128
DEG_ROWS = 16
BF16 = jnp.bfloat16
F32 = jnp.float32


def reverse_bits(value, bits):
    out = value & 0
    for bit in range(bits):
        out = out | (((value >> bit) & 1) << (bits - 1 - bit))
    return out


def doubling_masks(size):
    return [2 ** (step + 1) - 1 for step in range(size.bit_length() - 1)]


def slot_offsets(masks):
    offsets = [0]
    for mask in masks:
        offsets = offsets + [offset ^ mask for offset in offsets]
    return offsets


def row_scale(degree_lanes):
    spread = jnp.broadcast_to(degree_lanes.astype(F32), (TILE, TILE))
    return lax.rsqrt(spread.T)


def wide(scale, width):
    return jnp.concatenate([scale] * (width // TILE), axis=1)


def tile_loop(idx_ref, cnt_ref, body):
    tiles = idx_ref.shape[-1]
    used = cnt_ref[0, 0]
    for slot in range(tiles):
        live = slot < used
        row = jnp.where(live, idx_ref[0, 0, 0, slot], 0)
        col = jnp.where(live, idx_ref[0, 0, 1, slot], 0)
        body(slot, live, row, col)


def rows_at(block, rows=TILE):
    return pl.ds(pl.multiple_of(block * rows, rows), rows)


def scale_kernel(deg_ref, x_ref, out_ref):
    scale = row_scale(deg_ref[...].reshape(1, TILE))
    out_ref[...] = (wide(scale, x_ref.shape[1]) * x_ref[...].astype(F32)).astype(BF16)


def forward_kernel(n_rows, n_cols, idx_ref, cnt_ref, values_ref, deg_ref, cot_ref, *rest):
    blocks, (out_ref, panel, acc) = rest[:n_rows], rest[n_rows:]
    me = lax.axis_index("rows")
    for shift, block in enumerate(blocks):
        panel[lax.rem(me - shift + n_rows, n_rows)] = block[...]
    acc[...] = jnp.zeros_like(acc)

    def body(slot, live, row, col):
        tile = jnp.where(live, values_ref[0, 0, slot], jnp.zeros((TILE, TILE), BF16))
        acc[rows_at(row), :] += jnp.dot(tile, panel[col], preferred_element_type=F32)

    tile_loop(idx_ref, cnt_ref, body)
    panel_rows = n_cols * TILE
    out_ref[:panel_rows] = acc[...].astype(BF16)
    out_ref[panel_rows : panel_rows + TILE] = cot_ref[...]
    degree = deg_ref[...].reshape(1, TILE).astype(F32)
    out_ref[panel_rows + TILE :, :TILE] = jnp.broadcast_to(degree, (DEG_ROWS, TILE)).astype(BF16)


def merge_kernel(panel_rows, own_ref, got_ref, out_ref):
    out_ref[:panel_rows] = (
        own_ref[:panel_rows].astype(F32) + got_ref[:panel_rows].astype(F32)
    ).astype(BF16)
    extra = own_ref.shape[0] - panel_rows
    out_ref[panel_rows : panel_rows + extra] = own_ref[panel_rows:]
    out_ref[panel_rows + extra :] = got_ref[panel_rows:]


def middle_kernel(
    n_rows, n_cols, idx_ref, cnt_ref, values_ref, own_ref, got_ref, weight_ref,
    act_ref, keep_ref, send_ref, spread, hidden, weight_acc,
):
    width = weight_ref.shape[0]
    panel_rows = n_cols * TILE
    extra = own_ref.shape[0] - panel_rows
    per_side = extra // (TILE + DEG_ROWS)
    row, col = lax.axis_index("rows"), lax.axis_index("cols")
    odd = lax.rem(row, 2) == 1
    masks = doubling_masks(n_cols)
    even_offsets, odd_offsets = slot_offsets(masks), slot_offsets(masks[::-1])
    weight = weight_ref[...]
    weight_acc[...] = jnp.zeros_like(weight_acc)
    hidden[...] = jnp.zeros_like(hidden)
    for slot in range(n_cols):
        block = col ^ jnp.where(odd, odd_offsets[slot], even_offsets[slot])
        side = own_ref if slot < per_side else got_ref
        at = panel_rows + (slot % per_side) * (TILE + DEG_ROWS)
        here = rows_at(block)
        sums = own_ref[here, :].astype(F32) + got_ref[here, :].astype(F32)
        scale = wide(row_scale(side[at + TILE : at + TILE + 1, :TILE]), width)
        aggregated = (scale * sums).astype(BF16)
        pre_act = jnp.dot(aggregated, weight, preferred_element_type=F32)
        sig = 1.0 / (1.0 + jnp.exp(-pre_act))
        if slot == 0:
            act_ref[...] = (pre_act * sig).astype(BF16)
        grad = side[at : at + TILE, :].astype(F32) * sig * (1.0 + pre_act * (1.0 - sig))
        spread[block] = (scale * grad).astype(BF16)
        weight_acc[...] += lax.dot_general(
            aggregated, grad.astype(BF16), (((0,), (0,)), ((), ())), preferred_element_type=F32
        )

    bits = n_rows.bit_length() - 1

    def body(slot, live, tile_row, tile_col):
        tile = jnp.where(live, values_ref[0, 0, slot], jnp.zeros((TILE, TILE), BF16))
        place = reverse_bits(tile_col ^ row, bits)
        hidden[rows_at(place), :] += lax.dot_general(
            tile, spread[tile_row], (((0,), (0,)), ((), ())), preferred_element_type=F32
        )

    tile_loop(idx_ref, cnt_ref, body)
    half = n_rows * TILE // 2
    keep_ref[...] = hidden[:half]
    send_ref[:half] = hidden[half:].astype(BF16)
    send_ref[half:] = weight_acc[...].astype(BF16)


def fold_kernel(keep_ref, sent_ref, got_ref, keep_out, send_out):
    rows = keep_ref.shape[0]
    half = rows // 2
    keep_out[...] = keep_ref[:half] + got_ref[:half].astype(F32)
    send_out[:half] = (keep_ref[half:] + got_ref[half:rows].astype(F32)).astype(BF16)
    send_out[half:] = (sent_ref[rows:].astype(F32) + got_ref[rows:].astype(F32)).astype(BF16)


def last_kernel(weight_scale, deg_ref, weight_ref, keep_ref, sent_ref, got_ref, grad_ref, wgrad_ref):
    rows = keep_ref.shape[0]
    hidden = (keep_ref[...] + got_ref[:rows].astype(F32)).astype(BF16)
    back = lax.dot_general(
        hidden, weight_ref[...], (((1,), (1,)), ((), ())), preferred_element_type=F32
    )
    scale = wide(row_scale(deg_ref[...].reshape(1, TILE)), back.shape[1])
    grad_ref[...] = (scale * back).astype(BF16)
    wgrad_ref[...] = (sent_ref[rows:].astype(F32) + got_ref[rows:].astype(F32)) * weight_scale


def call(body, out_shapes, places, scratch=()):
    return pl.pallas_call(
        body,
        out_shape=out_shapes,
        in_specs=[pl.BlockSpec(memory_space=place) for place in places],
        scratch_shapes=list(scratch),
        compiler_params=pltpu.CompilerParams(vmem_limit_bytes=24 * 1024 * 1024),
    )


def shards(features, degree, weight, tile_index, tile_values, tile_count, cotangent):
    width = features.shape[1]
    n_rows = lax.axis_size("rows")
    n_cols = lax.axis_size("cols")
    shape = jax.ShapeDtypeStruct
    smem, vmem = pltpu.SMEM, pltpu.VMEM
    panel_rows = n_cols * TILE

    scaled = call(scale_kernel, shape((TILE, width), BF16), [vmem, vmem])(degree, features)
    blocks = [scaled] + [None] * (n_rows - 1)
    for shift in reversed(range(1, n_rows)):
        blocks[shift] = lax.ppermute(
            scaled, "rows", [(i, (i + shift) % n_rows) for i in range(n_rows)]
        )
    part = call(
        functools.partial(forward_kernel, n_rows, n_cols),
        shape((panel_rows + TILE + DEG_ROWS, width), BF16),
        [smem, smem] + [vmem] * (3 + n_rows),
        [vmem((n_rows, TILE, width), BF16), vmem((panel_rows, width), F32)],
    )(tile_index, tile_count, tile_values, degree, cotangent, *blocks)

    masks = doubling_masks(n_cols)
    for step in range(len(masks)):
        pairs = []
        for i in range(n_rows):
            mask = masks[::-1][step] if i % 2 else masks[step]
            pairs += [(i * n_cols + j, i * n_cols + (j ^ mask)) for j in range(n_cols)]
        got = lax.ppermute(part, ("rows", "cols"), pairs)
        if step + 1 < len(masks):
            rows = 2 * part.shape[0] - panel_rows
            part = call(
                functools.partial(merge_kernel, panel_rows), shape((rows, width), BF16), [vmem] * 2
            )(part, got)
    half = n_rows * TILE // 2
    activated, keep, send = call(
        functools.partial(middle_kernel, n_rows, n_cols),
        (
            shape((TILE, width), BF16),
            shape((half, width), F32),
            shape((half + width, width), BF16),
        ),
        [smem, smem] + [vmem] * 4,
        [
            vmem((n_cols, TILE, width), BF16),
            vmem((n_rows * TILE, width), F32),
            vmem((width, width), F32),
        ],
    )(tile_index, tile_count, tile_values, part, got, weight)
    mask = 1
    while True:
        got = lax.ppermute(send, "rows", [(i, i ^ mask) for i in range(n_rows)])
        mask *= 2
        if mask == n_rows:
            break
        half = keep.shape[0] // 2
        keep, send = call(
            fold_kernel, (shape((half, width), F32), shape((half + width, width), BF16)), [vmem] * 3
        )(keep, send, got)
    weight_scale = 1.0 / math.sqrt(TILE * n_rows * n_cols)
    input_grad, weight_grad = call(
        functools.partial(last_kernel, weight_scale),
        (shape((TILE, width), BF16), shape((width, width), F32)),
        [vmem] * 5,
    )(degree, weight, keep, send, got)
    return (activated, input_grad, weight_grad)


def solution(mesh):
    placed = (
        P(("groups", "rows", "cols"), None),
        P(("groups", "rows", "cols")),
        P(),
        P(("groups", "rows"), "cols", None, None),
        P(("groups", "rows"), "cols", None, None, None),
        P(("groups", "rows"), "cols"),
        P(("groups", "rows", "cols"), None),
    )
    return jax.shard_map(
        shards,
        mesh=mesh,
        in_specs=placed,
        out_specs=(
            P(("groups", "rows", "cols"), None),
            P(("groups", "rows", "cols"), None),
            P("groups", None),
        ),
        check_vma=False,
    )
```

time: 180 us -> 47.2 us (0.26)
  waiting for transfers between devices: 128 us -> 29.6 us
  blocking collectives: 21.1 us -> 0 us
  between operations: 14.6 us -> 1.36 us
  starting transfers between devices: 0.12 us -> 9.66 us
  other arithmetic: 4.92 us -> 0 us
  matrix products: 4.89 us -> 0 us
  Pallas kernels: 0 us -> 3.88 us
  local copies, waits for them, and re-layouts: 5.31 us -> 2.49 us
    psum x1 -> x0, waiting for transfers between devices: 85.7 us -> none  [shards(): lax.psum(weight_term, ('rows', 'cols')) / math.sqrt(node_total)]
    reduce_scatter x2 -> x0, waiting for transfers between devices: 42.5 us -> none  [the longest x1 21.5 us: shards(): lax.psum_scatter(column_partial.astype(jnp.bfloat16), 'rows', scatter_dim...]
    ppermute x0 -> x7, waiting for transfers between devices: none -> 29.6 us  [the longest x2 18.6 us: shards(): got = lax.ppermute(part, ('rows', 'cols'), pairs)]
    all_gather x2 -> x0, blocking collectives: 21.1 us -> none  [the longest x1 13.9 us: shards(): grad_panel = lax.all_gather(own_spread, 'cols', axis=0, tiled=True)]
    ppermute x0 -> x7, starting transfers between devices: none -> 9.66 us  [the longest x2 5.28 us: shards(): got = lax.ppermute(part, ('rows', 'cols'), pairs)]
    dot_general x9 -> x0, matrix products: 4.89 us -> none  [the longest x1 1.71 us: shards(): own_pre = jnp.dot(own_agg, weight, preferred_element_type=jnp.float32)]
    pallas_call x0 -> x6, Pallas kernels: none -> 3.88 us  [the longest x1 1.89 us: shards(): call(functools.partial(middle_kernel, n_rows, n_cols), (shape((TILE, widt...]
    convert_element_type x6 -> x0, local copies, waits for them, and re-layouts: 3.06 us -> none  [the longest x2 0.8 us: place_tiles(): high_part = products.astype(jnp.bfloat16)]
  transfers between devices with their start and end apart: 3 -> 7, of which waited for: 3 -> 7; matrix products, arithmetic and copies ran while one was open for 2% -> 0% of each run, Pallas kernels for 0% -> 0%
where the time goes in v1:
time: 47.2 us; the launch traced here: 46.9 us
  waiting for transfers between devices  29.6 us (63%)
  starting transfers between devices  9.66 us (20%)
  Pallas kernels  3.88 us (8%)
  local copies, waits for them, and re-layouts  2.49 us (5%)
  between operations  1.36 us (3%)
    ppermute x2, waiting for transfers between devices, shards(): got = lax.ppermute(part, ('rows', 'cols'), pairs)  18.6 us
    ppermute x2, waiting for transfers between devices, shards(): got = lax.ppermute(send, 'rows', [(i, i ^ mask) for i in range(n_rows)])  7.4 us
    ppermute x2, starting transfers between devices, shards(): got = lax.ppermute(part, ('rows', 'cols'), pairs)  5.28 us
    ppermute x3, waiting for transfers between devices, shards(): lax.ppermute(scaled, 'rows', [(i, (i + shift) % n_rows) for i in range(n_...  3.51 us
    ppermute x3, starting transfers between devices, shards(): lax.ppermute(scaled, 'rows', [(i, (i + shift) % n_rows) for i in range(n_...  3.23 us
    unnamed x14, local copies, waits for them, and re-layouts  2.49 us
    pallas_call x1, Pallas kernels, shards(): call(functools.partial(middle_kernel, n_rows, n_cols), (shape((TILE, widt...  1.89 us
    ppermute x2, starting transfers between devices, shards(): got = lax.ppermute(send, 'rows', [(i, i ^ mask) for i in range(n_rows)])  1.14 us
  transfers between devices with their start and end apart: 7, of which 7 were waited for; matrix products, arithmetic and copies ran while one was open for 0% of the time, Pallas kernels for 0%

profile of v1, /device:TPU:0, one launch (start us, length us, event | category | flops | bytes accessed | tf_op | source)
XLA Modules:
  0.0 46.9 jit_solution(7769651321882348102)
XLA Ops:
  0.6 0.9 %copy-done.3 = bf16[128,256]{1,0:T(8,128)(2,1)S(1)} copy-done((bf16[128,256]{1,0:T(8,128)(2,1)S(1)}, bf16[128,256]{1,0:T(8,128)(2,1)}, u32[]{:S(2)}) %copy-start.3) | copy-done | bytes 65560
  1.5 0.7 %copy-done.4 = s32[128]{0:T(128)S(1)} copy-done((s32[128]{0:T(128)S(1)}, s32[128]{0:T(128)}, u32[]{:S(2)}) %copy-start.4) | copy-done | bytes 536
  2.2 0.1 shard_map.94.rest_0_
  2.3 0.0 copy-start.5
  2.3 2.4 %collective-permute-start.2 = (bf16[128,256]{1,0:T(8,128)(2,1)S(1)}, bf16[128,256]{1,0:T(8,128)(2,1)S(1)}, u32[]{:S(2)}, u32[]{:S(2)}) collective-permute-start(bf16[128,256]{1,0:T(8,128)(2,1)S(1)} %shard_map.94.rest_0_), channel_id=1, source_target_pairs={{0,12},{4,0},{8,4},{12,8},{1,13},{5,1},{9,5},{13,9},{2,14},{6,2},{... | collective-permute-start | bytes 196616 | tf_op jit(solution)/shard_map/ppermute | solution.py:180
  4.7 0.6 %collective-permute-start.1 = (bf16[128,256]{1,0:T(8,128)(2,1)S(1)}, bf16[128,256]{1,0:T(8,128)(2,1)S(1)}, u32[]{:S(2)}, u32[]{:S(2)}) collective-permute-start(bf16[128,256]{1,0:T(8,128)(2,1)S(1)} %shard_map.94.rest_0_), channel_id=1, source_target_pairs={{0,8},{4,12},{8,0},{12,4},{1,9},{5,13},{9,1},{13,5},{2,10},{6,14},... | collective-permute-start | bytes 196616 | tf_op jit(solution)/shard_map/ppermute | solution.py:180
  5.4 0.2 collective-permute-start
  6.2 0.9 %collective-permute-done.2.rest_3_ = bf16[128,256]{1,0:T(8,128)(2,1)S(1)} collective-permute-done((bf16[128,256]{1,0:T(8,128)(2,1)S(1)}, bf16[128,256]{1,0:T(8,128)(2,1)S(1)}, u32[]{:S(2)}, u32[]{:S(2)}) %collective-permute-start.2) | collective-permute-done | bytes 65568 | tf_op jit(solution)/shard_map/ppermute | solution.py:180
  7.1 2.5 %collective-permute-done.1.rest_2_ = bf16[128,256]{1,0:T(8,128)(2,1)S(1)} collective-permute-done((bf16[128,256]{1,0:T(8,128)(2,1)S(1)}, bf16[128,256]{1,0:T(8,128)(2,1)S(1)}, u32[]{:S(2)}, u32[]{:S(2)}) %collective-permute-start.1) | collective-permute-done | bytes 65568 | tf_op jit(solution)/shard_map/ppermute | solution.py:180
  9.6 0.1 collective-permute-done.rest_1_
  9.7 0.0 copy-start
  9.7 0.9 %copy-done = bf16[1,1,8,128,128]{4,3,2,1,0:T(8,128)(2,1)S(1)} copy-done((bf16[1,1,8,128,128]{4,3,2,1,0:T(8,128)(2,1)S(1)}, bf16[1,1,8,128,128]{4,3,2,1,0:T(8,128)(2,1)}, u32[]{:S(2)}) %copy-start) | copy-done | bytes 262168
  10.7 0.9 %shard_map.95.own_ref = bf16[656,256]{1,0:T(8,128)(2,1)S(1)} custom-call(s32[1,1,2,8]{3,2,1,0:T(2,128)S(1)} %copy-done.6, s32[1,1]{1,0:T(1,128)S(6)} %copy.10.cnt_ref, bf16[1,1,8,128,128]{4,3,2,1,0:T(8,128)(2,1)S(1)} %copy-done, s32[128]{0:T(128)S(1)} %copy-done.5, bf16[128,256]{1,0:T(8,128)(2,1)S(1)} %copy-done.2, bf16[128,256]{1,0:T(8,128)(2,1)S(1)} %shard_map.94.rest_0_, ...), custom_call_target="tpu_custom_call" | custom-call | tf_op jit(solution)/shard_map/pallas_call | solution.py:183
  11.6 1.6 %collective-permute-start.3 = (bf16[656,256]{1,0:T(8,128)(2,1)S(1)}, bf16[656,256]{1,0:T(8,128)(2,1)S(1)}, u32[]{:S(2)}, u32[]{:S(2)}) collective-permute-start(bf16[656,256]{1,0:T(8,128)(2,1)S(1)} %shard_map.95.own_ref), channel_id=1, source_target_pairs={{0,1},{1,0},{2,3},{3,2},{4,7},{5,6},{6,5},{7,4},{8,9},{9,8},{10,11... | collective-permute-start | bytes 1007624 | tf_op jit(solution)/shard_map/ppermute | solution.py:196
  13.2 9.2 %collective-permute-done.3.got_ref = bf16[656,256]{1,0:T(8,128)(2,1)S(1)} collective-permute-done((bf16[656,256]{1,0:T(8,128)(2,1)S(1)}, bf16[656,256]{1,0:T(8,128)(2,1)S(1)}, u32[]{:S(2)}, u32[]{:S(2)}) %collective-permute-start.3) | collective-permute-done | bytes 335904 | tf_op jit(solution)/shard_map/ppermute | solution.py:196
  22.4 0.1 shard_map.96.own_ref
  22.5 3.6 %collective-permute-start.4 = (bf16[800,256]{1,0:T(8,128)(2,1)S(1)}, bf16[800,256]{1,0:T(8,128)(2,1)S(1)}, u32[]{:S(2)}, u32[]{:S(2)}) collective-permute-start(bf16[800,256]{1,0:T(8,128)(2,1)S(1)} %shard_map.96.own_ref), channel_id=1, source_target_pairs={{0,3},{1,2},{2,1},{3,0},{4,5},{5,4},{6,7},{7,6},{8,11},{9,10},{10,... | collective-permute-start | bytes 1228808 | tf_op jit(solution)/shard_map/ppermute | solution.py:196
  26.1 9.5 %collective-permute-done.4.got_ref = bf16[800,256]{1,0:T(8,128)(2,1)S(1)} collective-permute-done((bf16[800,256]{1,0:T(8,128)(2,1)S(1)}, bf16[800,256]{1,0:T(8,128)(2,1)S(1)}, u32[]{:S(2)}, u32[]{:S(2)}) %collective-permute-start.4) | collective-permute-done | bytes 409632 | tf_op jit(solution)/shard_map/ppermute | solution.py:196
  35.6 1.9 %shard_map.97 = (bf16[128,256]{1,0:T(8,128)(2,1)}, f32[256,256]{1,0:T(8,128)S(1)}, bf16[512,256]{1,0:T(8,128)(2,1)S(1)}) custom-call(s32[1,1,2,8]{3,2,1,0:T(2,128)S(1)} %copy-done.6, s32[1,1]{1,0:T(1,128)S(6)} %copy.10.cnt_ref, bf16[1,1,8,128,128]{4,3,2,1,0:T(8,128)(2,1)S(1)} %copy-done, bf16[800,256]{1,0:T(8,128)(2,1)S(1)} %shard_map.96.own_ref, ...), custom_call_target="tpu_custom_call" | custom-call | tf_op jit(solution)/shard_map/pallas_call | solution.py:203
  37.5 1.5 %collective-permute-done.5.got_ref = bf16[512,256]{1,0:T(8,128)(2,1)S(1)} collective-permute-done((bf16[512,256]{1,0:T(8,128)(2,1)S(1)}, bf16[512,256]{1,0:T(8,128)(2,1)S(1)}, u32[]{:S(2)}, u32[]{:S(2)}) %collective-permute-start.5) | collective-permute-done | bytes 262176 | tf_op jit(solution)/shard_map/ppermute | solution.py:219
  39.0 0.1 shard_map.98
  39.1 1.1 %collective-permute-start.6 = (bf16[384,256]{1,0:T(8,128)(2,1)S(1)}, bf16[384,256]{1,0:T(8,128)(2,1)S(1)}, u32[]{:S(2)}, u32[]{:S(2)}) collective-permute-start(bf16[384,256]{1,0:T(8,128)(2,1)S(1)} %get-tuple-element.14.sent_ref), channel_id=1, source_target_pairs={{0,8},{4,12},{8,0},{12,4},{1,9},{5,13},{9,1},{13,5},{2,10},{6,14},... | collective-permute-start | bytes 589832 | tf_op jit(solution)/shard_map/ppermute | solution.py:219
  40.2 5.9 %collective-permute-done.6.got_ref = bf16[384,256]{1,0:T(8,128)(2,1)S(1)} collective-permute-done((bf16[384,256]{1,0:T(8,128)(2,1)S(1)}, bf16[384,256]{1,0:T(8,128)(2,1)S(1)}, u32[]{:S(2)}, u32[]{:S(2)}) %collective-permute-start.6) | collective-permute-done | bytes 196640 | tf_op jit(solution)/shard_map/ppermute | solution.py:219
  46.1 0.9 %shard_map.99 = (bf16[128,256]{1,0:T(8,128)(2,1)}, f32[256,256]{1,0:T(8,128)}) custom-call(s32[128]{0:T(128)S(1)} %copy-done.5, bf16[256,256]{1,0:T(8,128)(2,1)S(1)} %copy-done.1, f32[128,256]{1,0:T(8,128)S(1)} %get-tuple-element.13.keep_ref, bf16[384,256]{1,0:T(8,128)(2,1)S(1)} %get-tuple-element.14.sent_ref, ...), custom_call_target="tpu_custom_call" | custom-call | tf_op jit(solution)/shard_map/pallas_call | solution.py:228
  (10 shorter events, 0.0 us)
Async XLA Ops:
  0.6 9.1 %copy-start.2 = (bf16[128,256]{1,0:T(8,128)(2,1)S(1)}, bf16[128,256]{1,0:T(8,128)(2,1)}, u32[]{:S(2)}) copy-start(bf16[128,256]{1,0:T(8,128)(2,1)} %cot_ref.1) | copy-start | bytes 196612
  0.6 0.9 %copy-start.3 = (bf16[128,256]{1,0:T(8,128)(2,1)S(1)}, bf16[128,256]{1,0:T(8,128)(2,1)}, u32[]{:S(2)}) copy-start(bf16[128,256]{1,0:T(8,128)(2,1)} %x_ref.1) | copy-start | bytes 196612
  1.5 0.7 %copy-start.4 = (s32[128]{0:T(128)S(1)}, s32[128]{0:T(128)}, u32[]{:S(2)}) copy-start(s32[128]{0:T(128)} %deg_ref.5) | copy-start | bytes 1540
  2.3 7.4 %copy-start.5 = (s32[128]{0:T(128)S(1)}, s32[128]{0:T(128)}, u32[]{:S(2)}) copy-start(s32[128]{0:T(128)} %deg_ref.5) | copy-start | bytes 1540
  2.3 7.4 %copy-start.6 = (s32[1,1,2,8]{3,2,1,0:T(2,128)S(1)}, s32[1,1,2,8]{3,2,1,0:T(2,128)}, u32[]{:S(2)}) copy-start(s32[1,1,2,8]{3,2,1,0:T(2,128)} %idx_ref.3) | copy-start | bytes 196
  2.3 4.8 %collective-permute-start.2 = (bf16[128,256]{1,0:T(8,128)(2,1)S(1)}, bf16[128,256]{1,0:T(8,128)(2,1)S(1)}, u32[]{:S(2)}, u32[]{:S(2)}) collective-permute-start(bf16[128,256]{1,0:T(8,128)(2,1)S(1)} %shard_map.94.rest_0_), channel_id=1, source_target_pairs={{0,12},{4,0},{8,4},{12,8},{1,13},{5,1},{9,5},{13,9},{2,14},{6,2},{... | collective-permute-start | bytes 196616 | tf_op jit(solution)/shard_map/ppermute | solution.py:180
  4.7 4.9 %collective-permute-start.1 = (bf16[128,256]{1,0:T(8,128)(2,1)S(1)}, bf16[128,256]{1,0:T(8,128)(2,1)S(1)}, u32[]{:S(2)}, u32[]{:S(2)}) collective-permute-start(bf16[128,256]{1,0:T(8,128)(2,1)S(1)} %shard_map.94.rest_0_), channel_id=1, source_target_pairs={{0,8},{4,12},{8,0},{12,4},{1,9},{5,13},{9,1},{13,5},{2,10},{6,14},... | collective-permute-start | bytes 196616 | tf_op jit(solution)/shard_map/ppermute | solution.py:180
  5.4 4.3 %collective-permute-start = (bf16[128,256]{1,0:T(8,128)(2,1)S(1)}, bf16[128,256]{1,0:T(8,128)(2,1)S(1)}, u32[]{:S(2)}, u32[]{:S(2)}) collective-permute-start(bf16[128,256]{1,0:T(8,128)(2,1)S(1)} %shard_map.94.rest_0_), channel_id=1, source_target_pairs={{0,4},{4,8},{8,12},{12,0},{1,5},{5,9},{9,13},{13,1},{2,6},{6,10},{... | collective-permute-start | bytes 196616 | tf_op jit(solution)/shard_map/ppermute | solution.py:180
  9.7 1.0 %copy-start = (bf16[1,1,8,128,128]{4,3,2,1,0:T(8,128)(2,1)S(1)}, bf16[1,1,8,128,128]{4,3,2,1,0:T(8,128)(2,1)}, u32[]{:S(2)}) copy-start(bf16[1,1,8,128,128]{4,3,2,1,0:T(8,128)(2,1)} %values_ref.3) | copy-start | bytes 786436
  11.6 24.0 %copy-start.1 = (bf16[256,256]{1,0:T(8,128)(2,1)S(1)}, bf16[256,256]{1,0:T(8,128)(2,1)}, u32[]{:S(2)}) copy-start(bf16[256,256]{1,0:T(8,128)(2,1)} %weight_ref.3) | copy-start | bytes 393220
  11.6 10.8 %collective-permute-start.3 = (bf16[656,256]{1,0:T(8,128)(2,1)S(1)}, bf16[656,256]{1,0:T(8,128)(2,1)S(1)}, u32[]{:S(2)}, u32[]{:S(2)}) collective-permute-start(bf16[656,256]{1,0:T(8,128)(2,1)S(1)} %shard_map.95.own_ref), channel_id=1, source_target_pairs={{0,1},{1,0},{2,3},{3,2},{4,7},{5,6},{6,5},{7,4},{8,9},{9,8},{10,11... | collective-permute-start | bytes 1007624 | tf_op jit(solution)/shard_map/ppermute | solution.py:196
  22.5 13.1 %collective-permute-start.4 = (bf16[800,256]{1,0:T(8,128)(2,1)S(1)}, bf16[800,256]{1,0:T(8,128)(2,1)S(1)}, u32[]{:S(2)}, u32[]{:S(2)}) collective-permute-start(bf16[800,256]{1,0:T(8,128)(2,1)S(1)} %shard_map.96.own_ref), channel_id=1, source_target_pairs={{0,3},{1,2},{2,1},{3,0},{4,5},{5,4},{6,7},{7,6},{8,11},{9,10},{10,... | collective-permute-start | bytes 1228808 | tf_op jit(solution)/shard_map/ppermute | solution.py:196
  37.5 1.5 %collective-permute-start.5 = (bf16[512,256]{1,0:T(8,128)(2,1)S(1)}, bf16[512,256]{1,0:T(8,128)(2,1)S(1)}, u32[]{:S(2)}, u32[]{:S(2)}) collective-permute-start(bf16[512,256]{1,0:T(8,128)(2,1)S(1)} %get-tuple-element.12.sent_ref), channel_id=1, source_target_pairs={{0,4},{4,0},{8,12},{12,8},{1,5},{5,1},{9,13},{13,9},{2,6},{6,2},{1... | collective-permute-start | bytes 786440 | tf_op jit(solution)/shard_map/ppermute | solution.py:219
  39.1 7.0 %collective-permute-start.6 = (bf16[384,256]{1,0:T(8,128)(2,1)S(1)}, bf16[384,256]{1,0:T(8,128)(2,1)S(1)}, u32[]{:S(2)}, u32[]{:S(2)}) collective-permute-start(bf16[384,256]{1,0:T(8,128)(2,1)S(1)} %get-tuple-element.14.sent_ref), channel_id=1, source_target_pairs={{0,8},{4,12},{8,0},{12,4},{1,9},{5,13},{9,1},{13,5},{2,10},{6,14},... | collective-permute-start | bytes 589832 | tf_op jit(solution)/shard_map/ppermute | solution.py:219

commit v2 on v0

v2 whole, which is shorter than its diff:
```python
import functools
import math

import jax
import jax.numpy as jnp
from jax import lax
from jax.experimental import pallas as pl
from jax.experimental.pallas import tpu as pltpu
from jax.sharding import PartitionSpec as P

TILE = 128
DEG_ROWS = 16
BF16 = jnp.bfloat16
F32 = jnp.float32


def reverse_bits(value, bits):
    out = value & 0
    for bit in range(bits):
        out = out | (((value >> bit) & 1) << (bits - 1 - bit))
    return out


def row_scale(degree_lanes):
    spread = jnp.broadcast_to(degree_lanes.astype(F32), (TILE, TILE))
    return lax.rsqrt(spread.T)


def wide(scale, width):
    return jnp.concatenate([scale] * (width // TILE), axis=1)


def tile_loop(idx_ref, row_limit, col_limit, body):
    for slot in range(idx_ref.shape[-1]):
        row = jnp.clip(idx_ref[0, 0, 0, slot], 0, row_limit - 1)
        col = jnp.clip(idx_ref[0, 0, 1, slot], 0, col_limit - 1)
        body(slot, row, col)


def rows_at(block, rows=TILE):
    return pl.ds(pl.multiple_of(block * rows, rows), rows)


def scale_kernel(deg_ref, x_ref, out_ref):
    scale = wide(row_scale(deg_ref[...].reshape(1, TILE)), x_ref.shape[1])
    out_ref[...] = (scale * x_ref[...].astype(F32)).astype(BF16)


def extra_kernel(deg_ref, cot_ref, extra_ref):
    extra_ref[:TILE] = cot_ref[...]
    degree = jnp.broadcast_to(deg_ref[...].reshape(1, TILE).astype(F32), (DEG_ROWS, TILE))
    extra_ref[TILE:] = wide(degree, cot_ref.shape[1]).astype(BF16)


def tiles_kernel(cnt_ref, values_ref, tiles_ref, flipped_ref):
    used = jnp.broadcast_to(cnt_ref[...], (TILE, TILE))
    for slot in range(values_ref.shape[2]):
        tile = jnp.where(slot < used, values_ref[0, 0, slot].astype(F32), 0.0).astype(BF16)
        tiles_ref[slot] = tile
        flipped_ref[slot] = tile.T


def forward_kernel(n_rows, n_cols, idx_ref, tiles_ref, *rest):
    blocks, outs, (panel, acc) = rest[:n_rows], rest[n_rows : n_rows + n_cols], rest[n_rows + n_cols :]
    me, col_me = lax.axis_index("rows"), lax.axis_index("cols")
    for shift, block in enumerate(blocks):
        panel[me ^ shift] = block[...]
    acc[...] = jnp.zeros_like(acc)

    def body(slot, row, col):
        acc[rows_at(row), :] += jnp.dot(
            tiles_ref[slot], panel[col], preferred_element_type=F32
        )

    tile_loop(idx_ref, n_cols, n_rows, body)
    for shift, out in enumerate(outs):
        out[...] = acc[rows_at(col_me ^ shift), :].astype(BF16)


def own_rows_kernel(deg_ref, *rest):
    blocks, out_ref = rest[:-1], rest[-1]
    sums = blocks[0][...].astype(F32)
    for block in blocks[1:]:
        sums = sums + block[...].astype(F32)
    scale = wide(row_scale(deg_ref[...].reshape(1, TILE)), sums.shape[1])
    out_ref[...] = (scale * sums).astype(BF16)


def middle_kernel(n_cols, weight_ref, *rest):
    panels, extras = rest[:n_cols], rest[n_cols : 2 * n_cols]
    act_ref, spread_ref, term_keep, term_send, term = rest[2 * n_cols :]
    width = weight_ref.shape[0]
    col = lax.axis_index("cols")
    weight = weight_ref[...]
    term[...] = jnp.zeros_like(term)
    for shift in range(n_cols):
        extra = extras[shift]
        scale = wide(row_scale(extra[TILE : TILE + 1, :TILE]), width)
        aggregated = panels[shift][...]
        pre_act = jnp.dot(aggregated, weight, preferred_element_type=F32)
        sig = 1.0 / (1.0 + jnp.exp(-pre_act))
        if shift == 0:
            act_ref[...] = (pre_act * sig).astype(BF16)
        grad = extra[:TILE, :].astype(F32) * sig * (1.0 + pre_act * (1.0 - sig))
        spread_ref[col ^ shift] = (scale * grad).astype(BF16)
        term[...] += lax.dot_general(
            aggregated, grad.astype(BF16), (((0,), (0,)), ((), ())), preferred_element_type=F32
        )
    side = lax.rem(lax.axis_index("rows"), 2)
    half = width // 2
    term_keep[...] = term[rows_at(side, half), :]
    term_send[...] = term[rows_at(1 - side, half), :].astype(BF16)


def back_kernel(n_rows, n_cols, idx_ref, flipped_ref, spread_ref, keep_ref, send_ref, hidden):
    row = lax.axis_index("rows")
    hidden[...] = jnp.zeros_like(hidden)
    bits = n_rows.bit_length() - 1

    def body(slot, tile_row, tile_col):
        place = reverse_bits(tile_col ^ row, bits)
        hidden[rows_at(place), :] += jnp.dot(
            flipped_ref[slot], spread_ref[tile_row], preferred_element_type=F32
        )

    tile_loop(idx_ref, n_cols, n_rows, body)
    half = n_rows * TILE // 2
    keep_ref[...] = hidden[:half]
    send_ref[...] = hidden[half:].astype(BF16)


def fold_kernel(keep_ref, got_ref, keep_out, send_out):
    half = keep_ref.shape[0] // 2
    keep_out[...] = keep_ref[:half] + got_ref[:half].astype(F32)
    send_out[...] = (keep_ref[half:] + got_ref[half:].astype(F32)).astype(BF16)


def add_kernel(scale, own_ref, got_ref, out_ref):
    total = own_ref[...].astype(F32) + got_ref[...].astype(F32)
    out_ref[...] = (total * scale).astype(out_ref.dtype)


def join_kernel(own_ref, got_ref, out_ref):
    half = own_ref.shape[0]
    side = lax.rem(lax.axis_index("rows"), 2)
    out_ref[rows_at(side, half), :] = own_ref[...]
    out_ref[rows_at(1 - side, half), :] = got_ref[...]


def last_kernel(deg_ref, weight_ref, keep_ref, got_ref, grad_ref):
    hidden = (keep_ref[...] + got_ref[...].astype(F32)).astype(BF16)
    back = lax.dot_general(
        hidden, weight_ref[...], (((1,), (1,)), ((), ())), preferred_element_type=F32
    )
    scale = wide(row_scale(deg_ref[...].reshape(1, TILE)), back.shape[1])
    grad_ref[...] = (scale * back).astype(BF16)


def call(body, out_shapes, places, scratch=(), cost=None):
    return pl.pallas_call(
        body,
        out_shape=out_shapes,
        in_specs=[pl.BlockSpec(memory_space=place) for place in places],
        scratch_shapes=list(scratch),
        cost_estimate=cost,
        compiler_params=pltpu.CompilerParams(vmem_limit_bytes=24 * 1024 * 1024),
    )


def shards(features, degree, weight, tile_index, tile_values, tile_count, cotangent):
    width = features.shape[1]
    n_rows = lax.axis_size("rows")
    n_cols = lax.axis_size("cols")
    shape = jax.ShapeDtypeStruct
    smem, vmem = pltpu.SMEM, pltpu.VMEM
    tiles = tile_values.shape[2]

    def shifted(block, axis, size):
        got = [block] + [None] * (size - 1)
        for shift in reversed(range(1, size)):
            source = block[shift] if isinstance(block, (list, tuple)) else block
            got[shift] = lax.ppermute(source, axis, [(i, i ^ shift) for i in range(size)])
        if isinstance(block, (list, tuple)):
            got[0] = block[0]
        return got

    block_shape = shape((TILE, width), BF16)
    square = shape((tiles, TILE, TILE), BF16)
    slow = pl.CostEstimate(flops=10**10, bytes_accessed=10**6, transcendentals=0)
    scaled = call(scale_kernel, block_shape, [vmem] * 2, cost=slow)(degree, features)
    extra = call(extra_kernel, shape((TILE + DEG_ROWS, width), BF16), [vmem] * 2)(degree, cotangent)
    live_tiles, flipped = call(tiles_kernel, (square, square), [vmem] * 2)(tile_count, tile_values)
    blocks = shifted(scaled, "rows", n_rows)
    extras = shifted(extra, "cols", n_cols)
    parts = call(
        functools.partial(forward_kernel, n_rows, n_cols),
        [block_shape] * n_cols,
        [smem] + [vmem] * (1 + n_rows),
        [vmem((n_rows, TILE, width), BF16), vmem((n_cols * TILE, width), F32)],
        pl.CostEstimate(flops=2 * 10**10, bytes_accessed=10**6, transcendentals=0),
    )(tile_index, live_tiles, *blocks)
    sums = shifted(parts, "cols", n_cols)
    sums, extras = lax.optimization_barrier((sums, extras))
    aggregated = call(own_rows_kernel, block_shape, [vmem] * (1 + n_cols))(degree, *sums)
    panels = shifted(aggregated, "cols", n_cols)
    term_shape = shape((width // 2, width), BF16)
    activated, spread, term, term_send = call(
        functools.partial(middle_kernel, n_cols),
        (
            block_shape,
            shape((n_cols, TILE, width), BF16),
            shape(term_shape.shape, F32),
            term_shape,
        ),
        [vmem] * (1 + 2 * n_cols),
        [vmem((width, width), F32)],
    )(weight, *panels, *extras)
    half = n_rows * TILE // 2
    keep, send = call(
        functools.partial(back_kernel, n_rows, n_cols),
        (shape((half, width), F32), shape((half, width), BF16)),
        [smem] + [vmem] * 2,
        [vmem((n_rows * TILE, width), F32)],
    )(tile_index, flipped, spread)

    def partner(block, mask):
        return lax.ppermute(block, "rows", [(i, i ^ mask) for i in range(n_rows)])

    def add(dtype, scale, own, got):
        return call(
            functools.partial(add_kernel, scale), shape(own.shape, dtype), [vmem] * 2
        )(own, got)

    node_scale = 1.0 / math.sqrt(TILE * n_rows * n_cols)
    mask = 1
    while mask < n_rows:
        term_got, got = partner(term_send, mask), partner(send, mask)
        mask *= 2
        if mask == n_rows:
            term_got, got = lax.optimization_barrier((term_got, got))
        else:
            term = term_send = add(BF16, 1.0, term, term_got)
            rows = keep.shape[0] // 2
            keep, send = call(
                fold_kernel, (shape((rows, width), F32), shape((rows, width), BF16)), [vmem] * 2
            )(keep, got)
    term = add(F32, node_scale, term, term_got)
    weight_grad = call(join_kernel, shape((width, width), F32), [vmem] * 2)(
        term, partner(term, 1)
    )
    input_grad = call(last_kernel, block_shape, [vmem] * 4)(degree, weight, keep, got)
    return (activated, input_grad, weight_grad)


def solution(mesh):
    placed = (
        P(("groups", "rows", "cols"), None),
        P(("groups", "rows", "cols")),
        P(),
        P(("groups", "rows"), "cols", None, None),
        P(("groups", "rows"), "cols", None, None, None),
        P(("groups", "rows"), "cols"),
        P(("groups", "rows", "cols"), None),
    )
    return jax.shard_map(
        shards,
        mesh=mesh,
        in_specs=placed,
        out_specs=(
            P(("groups", "rows", "cols"), None),
            P(("groups", "rows", "cols"), None),
            P("groups", None),
        ),
        check_vma=False,
    )
```

time: 180 us -> 41.8 us (0.23)
  waiting for transfers between devices: 128 us -> 14.3 us
  blocking collectives: 21.1 us -> 0 us
  starting transfers between devices: 0.12 us -> 19.5 us
  between operations: 14.6 us -> 1.41 us
  other arithmetic: 4.92 us -> 0 us
  matrix products: 4.89 us -> 0 us
  Pallas kernels: 0 us -> 4.85 us
  local copies, waits for them, and re-layouts: 5.31 us -> 1.54 us
    psum x1 -> x0, waiting for transfers between devices: 85.7 us -> none  [shards(): lax.psum(weight_term, ('rows', 'cols')) / math.sqrt(node_total)]
    reduce_scatter x2 -> x0, waiting for transfers between devices: 42.5 us -> none  [the longest x1 21.5 us: shards(): lax.psum_scatter(column_partial.astype(jnp.bfloat16), 'rows', scatter_dim...]
    all_gather x2 -> x0, blocking collectives: 21.1 us -> none  [the longest x1 13.9 us: shards(): grad_panel = lax.all_gather(own_spread, 'cols', axis=0, tiled=True)]
    ppermute x0 -> x17, starting transfers between devices: none -> 19.5 us  [the longest x12 16.7 us: shifted(): lax.ppermute(source, axis, [(i, i ^ shift) for i in range(size)])]
    ppermute x0 -> x17, waiting for transfers between devices: none -> 14.3 us  [the longest x12 9.15 us: shifted(): lax.ppermute(source, axis, [(i, i ^ shift) for i in range(size)])]
    dot_general x9 -> x0, matrix products: 4.89 us -> none  [the longest x1 1.71 us: shards(): own_pre = jnp.dot(own_agg, weight, preferred_element_type=jnp.float32)]
    pallas_call x0 -> x12, Pallas kernels: none -> 4.85 us  [the longest x1 1.03 us: shards(): call(functools.partial(middle_kernel, n_cols), (block_shape, shape((n_col...]
    convert_element_type x6 -> x0, local copies, waits for them, and re-layouts: 3.06 us -> none  [the longest x2 0.8 us: place_tiles(): high_part = products.astype(jnp.bfloat16)]
  transfers between devices with their start and end apart: 3 -> 17, of which waited for: 3 -> 10; matrix products, arithmetic and copies ran while one was open for 2% -> 0% of each run, Pallas kernels for 0% -> 5%
where the time goes in v2:
time: 41.8 us; the launch traced here: 41.6 us
  starting transfers between devices  19.5 us (47%)
  waiting for transfers between devices  14.3 us (34%)
  Pallas kernels  4.85 us (12%)
  local copies, waits for them, and re-layouts  1.54 us (4%)
  between operations  1.41 us (3%)
    ppermute x12, starting transfers between devices, shifted(): lax.ppermute(source, axis, [(i, i ^ shift) for i in range(size)])  16.7 us
    ppermute x12, waiting for transfers between devices, shifted(): lax.ppermute(source, axis, [(i, i ^ shift) for i in range(size)])  9.15 us
    ppermute x5, waiting for transfers between devices, partner(): return lax.ppermute(block, 'rows', [(i, i ^ mask) for i in range(n_rows)])  5.15 us
    ppermute x5, starting transfers between devices, partner(): return lax.ppermute(block, 'rows', [(i, i ^ mask) for i in range(n_rows)])  2.8 us
    unnamed x14, local copies, waits for them, and re-layouts  1.54 us
    pallas_call x1, Pallas kernels, shards(): call(functools.partial(middle_kernel, n_cols), (block_shape, shape((n_col...  1.03 us
    pallas_call x1, Pallas kernels, shards(): call(functools.partial(forward_kernel, n_rows, n_cols), [block_shape] * n...  0.9 us
    pallas_call x1, Pallas kernels, shards(): call(functools.partial(back_kernel, n_rows, n_cols), (shape((half, width)...  0.88 us
  transfers between devices with their start and end apart: 17, of which 10 were waited for; matrix products, arithmetic and copies ran while one was open for 0% of the time, Pallas kernels for 5%

profile of v2, /device:TPU:0, one launch (start us, length us, event | category | flops | bytes accessed | tf_op | source)
XLA Modules:
  0.0 41.6 jit_solution(16360701404063590903)
XLA Ops:
  0.7 0.7 %copy-done.3 = s32[128]{0:T(128)S(1)} copy-done((s32[128]{0:T(128)S(1)}, s32[128]{0:T(128)}, u32[]{:S(2)}) %copy-start.3) | copy-done | bytes 536
  1.3 0.8 %copy-done.6 = bf16[128,256]{1,0:T(8,128)(2,1)S(1)} copy-done((bf16[128,256]{1,0:T(8,128)(2,1)S(1)}, bf16[128,256]{1,0:T(8,128)(2,1)}, u32[]{:S(2)}) %copy-start.6) | copy-done | bytes 65560
  2.3 2.4 %collective-permute-start.2 = (bf16[128,256]{1,0:T(8,128)(2,1)S(1)}, bf16[128,256]{1,0:T(8,128)(2,1)S(1)}, u32[]{:S(2)}, u32[]{:S(2)}) collective-permute-start(bf16[128,256]{1,0:T(8,128)(2,1)S(1)} %shard_map.95.rest_0_), channel_id=1, source_target_pairs={{0,12},{4,8},{8,4},{12,0},{1,13},{5,9},{9,5},{13,1},{2,14},{6,10},... | collective-permute-start | bytes 196616 | tf_op jit(solution)/shard_map/ppermute | solution.py:182
  5.4 3.9 %collective-permute-start.8 = (bf16[144,256]{1,0:T(8,128)(2,1)S(1)}, bf16[144,256]{1,0:T(8,128)(2,1)S(1)}, u32[]{:S(2)}, u32[]{:S(2)}) collective-permute-start(bf16[144,256]{1,0:T(8,128)(2,1)S(1)} %shard_map.97.rest_4_), channel_id=1, source_target_pairs={{0,3},{1,2},{2,1},{3,0},{4,7},{5,6},{6,5},{7,4},{8,11},{9,10},{10,... | collective-permute-start | bytes 221192 | tf_op jit(solution)/shard_map/ppermute | solution.py:182
  10.2 0.7 %collective-permute-start.6 = (bf16[144,256]{1,0:T(8,128)(2,1)S(1)}, bf16[144,256]{1,0:T(8,128)(2,1)S(1)}, u32[]{:S(2)}, u32[]{:S(2)}) collective-permute-start(bf16[144,256]{1,0:T(8,128)(2,1)S(1)} %shard_map.97.rest_4_), channel_id=1, source_target_pairs={{0,1},{1,0},{2,3},{3,2},{4,5},{5,4},{6,7},{7,6},{8,9},{9,8},{10,11... | collective-permute-start | bytes 221192 | tf_op jit(solution)/shard_map/ppermute | solution.py:182
  10.9 0.9 %shard_map.96 = (bf16[128,256]{1,0:T(8,128)(2,1)S(1)}, bf16[128,256]{1,0:T(8,128)(2,1)S(1)}, bf16[128,256]{1,0:T(8,128)(2,1)S(1)}, bf16[128,256]{1,0:T(8,128)(2,1)S(1)}) custom-call(s32[1,1,2,8]{3,2,1,0:T(2,128)S(1)} %copy-done.5, bf16[8,128,128]{2,1,0:T(8,128)(2,1)S(1)} %get-tuple-element.27.tiles_ref, bf16[128,256]{1,0:T(8,128)(2,1)S(1)} %shard_map.95.rest_0_, ...), custom_call_target="tpu_custom_call" | custom-call | flops 20000000000 | bytes 1000000 | tf_op jit(solution)/shard_map/pallas_call | solution.py:195
  11.8 1.5 %collective-permute-start.3 = (bf16[128,256]{1,0:T(8,128)(2,1)S(1)}, bf16[128,256]{1,0:T(8,128)(2,1)S(1)}, u32[]{:S(2)}, u32[]{:S(2)}) collective-permute-start(bf16[128,256]{1,0:T(8,128)(2,1)S(1)} %get-tuple-element.29), channel_id=1, source_target_pairs={{0,1},{1,0},{2,3},{3,2},{4,5},{5,4},{6,7},{7,6},{8,9},{9,8},{10,11... | collective-permute-start | bytes 196616 | tf_op jit(solution)/shard_map/ppermute | solution.py:182
  13.3 2.9 %collective-permute-start.4 = (bf16[128,256]{1,0:T(8,128)(2,1)S(1)}, bf16[128,256]{1,0:T(8,128)(2,1)S(1)}, u32[]{:S(2)}, u32[]{:S(2)}) collective-permute-start(bf16[128,256]{1,0:T(8,128)(2,1)S(1)} %get-tuple-element.30), channel_id=1, source_target_pairs={{0,2},{1,3},{2,0},{3,1},{4,6},{5,7},{6,4},{7,5},{8,10},{9,11},{10,... | collective-permute-start | bytes 196616 | tf_op jit(solution)/shard_map/ppermute | solution.py:182
  16.3 1.0 %collective-permute-done.6.rest_5_ = bf16[144,256]{1,0:T(8,128)(2,1)S(1)} collective-permute-done((bf16[144,256]{1,0:T(8,128)(2,1)S(1)}, bf16[144,256]{1,0:T(8,128)(2,1)S(1)}, u32[]{:S(2)}, u32[]{:S(2)}) %collective-permute-start.6) | collective-permute-done | bytes 73760 | tf_op jit(solution)/shard_map/ppermute | solution.py:182
  17.4 1.1 %collective-permute-done.3.rest_1_ = bf16[128,256]{1,0:T(8,128)(2,1)S(1)} collective-permute-done((bf16[128,256]{1,0:T(8,128)(2,1)S(1)}, bf16[128,256]{1,0:T(8,128)(2,1)S(1)}, u32[]{:S(2)}, u32[]{:S(2)}) %collective-permute-start.3) | collective-permute-done | bytes 65568 | tf_op jit(solution)/shard_map/ppermute | solution.py:182
  18.4 2.8 %collective-permute-done.4.rest_2_ = bf16[128,256]{1,0:T(8,128)(2,1)S(1)} collective-permute-done((bf16[128,256]{1,0:T(8,128)(2,1)S(1)}, bf16[128,256]{1,0:T(8,128)(2,1)S(1)}, u32[]{:S(2)}, u32[]{:S(2)}) %collective-permute-start.4) | collective-permute-done | bytes 65568 | tf_op jit(solution)/shard_map/ppermute | solution.py:182
  21.2 1.2 %collective-permute-done.5.rest_3_ = bf16[128,256]{1,0:T(8,128)(2,1)S(1)} collective-permute-done((bf16[128,256]{1,0:T(8,128)(2,1)S(1)}, bf16[128,256]{1,0:T(8,128)(2,1)S(1)}, u32[]{:S(2)}, u32[]{:S(2)}) %collective-permute-start.5) | collective-permute-done | bytes 65568 | tf_op jit(solution)/shard_map/ppermute | solution.py:182
  22.5 1.7 %collective-permute-start.11 = (bf16[128,256]{1,0:T(8,128)(2,1)S(1)}, bf16[128,256]{1,0:T(8,128)(2,1)S(1)}, u32[]{:S(2)}, u32[]{:S(2)}) collective-permute-start(bf16[128,256]{1,0:T(8,128)(2,1)S(1)} %shard_map.98.rest_0_), channel_id=1, source_target_pairs={{0,3},{1,2},{2,1},{3,0},{4,7},{5,6},{6,5},{7,4},{8,11},{9,10},{10,... | collective-permute-start | bytes 196616 | tf_op jit(solution)/shard_map/ppermute | solution.py:182
  24.8 2.1 %collective-permute-start.9 = (bf16[128,256]{1,0:T(8,128)(2,1)S(1)}, bf16[128,256]{1,0:T(8,128)(2,1)S(1)}, u32[]{:S(2)}, u32[]{:S(2)}) collective-permute-start(bf16[128,256]{1,0:T(8,128)(2,1)S(1)} %shard_map.98.rest_0_), channel_id=1, source_target_pairs={{0,1},{1,0},{2,3},{3,2},{4,5},{5,4},{6,7},{7,6},{8,9},{9,8},{10,11... | collective-permute-start | bytes 196616 | tf_op jit(solution)/shard_map/ppermute | solution.py:182
  27.0 1.7 %collective-permute-done.11.rest_3_ = bf16[128,256]{1,0:T(8,128)(2,1)S(1)} collective-permute-done((bf16[128,256]{1,0:T(8,128)(2,1)S(1)}, bf16[128,256]{1,0:T(8,128)(2,1)S(1)}, u32[]{:S(2)}, u32[]{:S(2)}) %collective-permute-start.11) | collective-permute-done | bytes 65568 | tf_op jit(solution)/shard_map/ppermute | solution.py:182
  28.7 1.4 %collective-permute-done.10.rest_2_ = bf16[128,256]{1,0:T(8,128)(2,1)S(1)} collective-permute-done((bf16[128,256]{1,0:T(8,128)(2,1)S(1)}, bf16[128,256]{1,0:T(8,128)(2,1)S(1)}, u32[]{:S(2)}, u32[]{:S(2)}) %collective-permute-start.10) | collective-permute-done | bytes 65568 | tf_op jit(solution)/shard_map/ppermute | solution.py:182
  30.1 1.0 %shard_map.99 = (bf16[128,256]{1,0:T(8,128)(2,1)}, bf16[4,128,256]{2,1,0:T(8,128)(2,1)S(1)}, f32[128,256]{1,0:T(8,128)S(1)}, bf16[128,256]{1,0:T(8,128)(2,1)S(1)}) custom-call(bf16[256,256]{1,0:T(8,128)(2,1)S(1)} %copy-done, bf16[128,256]{1,0:T(8,128)(2,1)S(1)} %shard_map.98.rest_0_, bf16[128,256]{1,0:T(8,128)(2,1)S(1)} %collective-permute-done.9.rest_1_, ...), custom_call_target="tpu_custom_call" | custom-call | tf_op jit(solution)/shard_map/pallas_call | solution.py:207
  31.1 0.9 %shard_map.100 = (f32[256,256]{1,0:T(8,128)S(1)}, bf16[256,256]{1,0:T(8,128)(2,1)S(1)}) custom-call(s32[1,1,2,8]{3,2,1,0:T(2,128)S(1)} %copy-done.5, bf16[8,128,128]{2,1,0:T(8,128)(2,1)S(1)} %get-tuple-element.41.flipped_ref, bf16[4,128,256]{2,1,0:T(8,128)(2,1)S(1)} %get-tuple-element.42.spread_ref), custom_call_target="tpu_custom_call" | custom-call | tf_op jit(solution)/shard_map/pallas_call | solution.py:219
  32.6 0.9 %collective-permute-done.13.got_ref = bf16[128,256]{1,0:T(8,128)(2,1)S(1)} collective-permute-done((bf16[128,256]{1,0:T(8,128)(2,1)S(1)}, bf16[128,256]{1,0:T(8,128)(2,1)S(1)}, u32[]{:S(2)}, u32[]{:S(2)}) %collective-permute-start.13) | collective-permute-done | bytes 65568 | tf_op jit(solution)/shard_map/ppermute | solution.py:227
  33.5 1.6 %collective-permute-start.14 = (bf16[128,256]{1,0:T(8,128)(2,1)S(1)}, bf16[128,256]{1,0:T(8,128)(2,1)S(1)}, u32[]{:S(2)}, u32[]{:S(2)}) collective-permute-start(bf16[128,256]{1,0:T(8,128)(2,1)S(1)} %shard_map.102.own_ref), channel_id=1, source_target_pairs={{0,8},{4,12},{8,0},{12,4},{1,9},{5,13},{9,1},{13,5},{2,10},{6,14},... | collective-permute-start | bytes 196616 | tf_op jit(solution)/shard_map/ppermute | solution.py:227
  35.7 2.3 %collective-permute-done.14.got_ref = bf16[128,256]{1,0:T(8,128)(2,1)S(1)} collective-permute-done((bf16[128,256]{1,0:T(8,128)(2,1)S(1)}, bf16[128,256]{1,0:T(8,128)(2,1)S(1)}, u32[]{:S(2)}, u32[]{:S(2)}) %collective-permute-start.14) | collective-permute-done | bytes 65568 | tf_op jit(solution)/shard_map/ppermute | solution.py:227
  38.0 1.4 %collective-permute-done.15.got_ref = bf16[128,256]{1,0:T(8,128)(2,1)S(1)} collective-permute-done((bf16[128,256]{1,0:T(8,128)(2,1)S(1)}, bf16[128,256]{1,0:T(8,128)(2,1)S(1)}, u32[]{:S(2)}, u32[]{:S(2)}) %collective-permute-start.15) | collective-permute-done | bytes 65568 | tf_op jit(solution)/shard_map/ppermute | solution.py:227
  39.5 0.8 %shard_map.103 = bf16[128,256]{1,0:T(8,128)(2,1)} custom-call(s32[128]{0:T(128)S(1)} %copy-done.4, bf16[256,256]{1,0:T(8,128)(2,1)S(1)} %copy-done, f32[128,256]{1,0:T(8,128)S(1)} %get-tuple-element.45.keep_ref, bf16[128,256]{1,0:T(8,128)(2,1)S(1)} %collective-permute-done.15.got_ref), custom_call_target="tpu_custom_call" | custom-call | tf_op jit(solution)/shard_map/pallas_call | solution.py:251
  40.9 0.7 %shard_map.105 = f32[256,256]{1,0:T(8,128)} custom-call(f32[128,256]{1,0:T(8,128)S(1)} %shard_map.104.own_ref, f32[128,256]{1,0:T(8,128)S(1)} %collective-permute-done.16.got_ref), custom_call_target="tpu_custom_call" | custom-call | tf_op jit(solution)/shard_map/pallas_call | solution.py:248
  (36 shorter events, 3.7 us)
Async XLA Ops:
  0.6 4.8 %copy-start.2 = (bf16[128,256]{1,0:T(8,128)(2,1)S(1)}, bf16[128,256]{1,0:T(8,128)(2,1)}, u32[]{:S(2)}) copy-start(bf16[128,256]{1,0:T(8,128)(2,1)} %cot_ref.1) | copy-start | bytes 196612
  0.6 0.7 %copy-start.3 = (s32[128]{0:T(128)S(1)}, s32[128]{0:T(128)}, u32[]{:S(2)}) copy-start(s32[128]{0:T(128)} %deg_ref.7) | copy-start | bytes 1540
  1.3 0.8 %copy-start.6 = (bf16[128,256]{1,0:T(8,128)(2,1)S(1)}, bf16[128,256]{1,0:T(8,128)(2,1)}, u32[]{:S(2)}) copy-start(bf16[128,256]{1,0:T(8,128)(2,1)} %x_ref.1) | copy-start | bytes 196612
  2.2 7.8 %copy-start.1 = (bf16[1,1,8,128,128]{4,3,2,1,0:T(8,128)(2,1)S(1)}, bf16[1,1,8,128,128]{4,3,2,1,0:T(8,128)(2,1)}, u32[]{:S(2)}) copy-start(bf16[1,1,8,128,128]{4,3,2,1,0:T(8,128)(2,1)} %values_ref.1) | copy-start | bytes 786436
  2.3 7.9 %collective-permute-start.2 = (bf16[128,256]{1,0:T(8,128)(2,1)S(1)}, bf16[128,256]{1,0:T(8,128)(2,1)S(1)}, u32[]{:S(2)}, u32[]{:S(2)}) collective-permute-start(bf16[128,256]{1,0:T(8,128)(2,1)S(1)} %shard_map.95.rest_0_), channel_id=1, source_target_pairs={{0,12},{4,8},{8,4},{12,0},{1,13},{5,9},{9,5},{13,1},{2,14},{6,10},... | collective-permute-start | bytes 196616 | tf_op jit(solution)/shard_map/ppermute | solution.py:182
  4.7 6.2 %collective-permute-start.1 = (bf16[128,256]{1,0:T(8,128)(2,1)S(1)}, bf16[128,256]{1,0:T(8,128)(2,1)S(1)}, u32[]{:S(2)}, u32[]{:S(2)}) collective-permute-start(bf16[128,256]{1,0:T(8,128)(2,1)S(1)} %shard_map.95.rest_0_), channel_id=1, source_target_pairs={{0,8},{4,12},{8,0},{12,4},{1,9},{5,13},{9,1},{13,5},{2,10},{6,14},... | collective-permute-start | bytes 196616 | tf_op jit(solution)/shard_map/ppermute | solution.py:182
  5.4 5.6 %collective-permute-start = (bf16[128,256]{1,0:T(8,128)(2,1)S(1)}, bf16[128,256]{1,0:T(8,128)(2,1)S(1)}, u32[]{:S(2)}, u32[]{:S(2)}) collective-permute-start(bf16[128,256]{1,0:T(8,128)(2,1)S(1)} %shard_map.95.rest_0_), channel_id=1, source_target_pairs={{0,4},{4,0},{8,12},{12,8},{1,5},{5,1},{9,13},{13,9},{2,6},{6,2},{1... | collective-permute-start | bytes 196616 | tf_op jit(solution)/shard_map/ppermute | solution.py:182
  5.4 10.8 %collective-permute-start.8 = (bf16[144,256]{1,0:T(8,128)(2,1)S(1)}, bf16[144,256]{1,0:T(8,128)(2,1)S(1)}, u32[]{:S(2)}, u32[]{:S(2)}) collective-permute-start(bf16[144,256]{1,0:T(8,128)(2,1)S(1)} %shard_map.97.rest_4_), channel_id=1, source_target_pairs={{0,3},{1,2},{2,1},{3,0},{4,7},{5,6},{6,5},{7,4},{8,11},{9,10},{10,... | collective-permute-start | bytes 221192 | tf_op jit(solution)/shard_map/ppermute | solution.py:182
  9.3 7.0 %collective-permute-start.7 = (bf16[144,256]{1,0:T(8,128)(2,1)S(1)}, bf16[144,256]{1,0:T(8,128)(2,1)S(1)}, u32[]{:S(2)}, u32[]{:S(2)}) collective-permute-start(bf16[144,256]{1,0:T(8,128)(2,1)S(1)} %shard_map.97.rest_4_), channel_id=1, source_target_pairs={{0,2},{1,3},{2,0},{3,1},{4,6},{5,7},{6,4},{7,5},{8,10},{9,11},{10,... | collective-permute-start | bytes 221192 | tf_op jit(solution)/shard_map/ppermute | solution.py:182
  10.2 0.7 %copy-start.5 = (s32[1,1,2,8]{3,2,1,0:T(2,128)S(1)}, s32[1,1,2,8]{3,2,1,0:T(2,128)}, u32[]{:S(2)}) copy-start(s32[1,1,2,8]{3,2,1,0:T(2,128)} %idx_ref.3) | copy-start | bytes 196
  10.2 7.1 %collective-permute-start.6 = (bf16[144,256]{1,0:T(8,128)(2,1)S(1)}, bf16[144,256]{1,0:T(8,128)(2,1)S(1)}, u32[]{:S(2)}, u32[]{:S(2)}) collective-permute-start(bf16[144,256]{1,0:T(8,128)(2,1)S(1)} %shard_map.97.rest_4_), channel_id=1, source_target_pairs={{0,1},{1,0},{2,3},{3,2},{4,5},{5,4},{6,7},{7,6},{8,9},{9,8},{10,11... | collective-permute-start | bytes 221192 | tf_op jit(solution)/shard_map/ppermute | solution.py:182
  11.8 6.6 %collective-permute-start.3 = (bf16[128,256]{1,0:T(8,128)(2,1)S(1)}, bf16[128,256]{1,0:T(8,128)(2,1)S(1)}, u32[]{:S(2)}, u32[]{:S(2)}) collective-permute-start(bf16[128,256]{1,0:T(8,128)(2,1)S(1)} %get-tuple-element.29), channel_id=1, source_target_pairs={{0,1},{1,0},{2,3},{3,2},{4,5},{5,4},{6,7},{7,6},{8,9},{9,8},{10,11... | collective-permute-start | bytes 196616 | tf_op jit(solution)/shard_map/ppermute | solution.py:182
  13.3 7.9 %collective-permute-start.4 = (bf16[128,256]{1,0:T(8,128)(2,1)S(1)}, bf16[128,256]{1,0:T(8,128)(2,1)S(1)}, u32[]{:S(2)}, u32[]{:S(2)}) collective-permute-start(bf16[128,256]{1,0:T(8,128)(2,1)S(1)} %get-tuple-element.30), channel_id=1, source_target_pairs={{0,2},{1,3},{2,0},{3,1},{4,6},{5,7},{6,4},{7,5},{8,10},{9,11},{10,... | collective-permute-start | bytes 196616 | tf_op jit(solution)/shard_map/ppermute | solution.py:182
  16.2 6.2 %copy-start.4 = (s32[128]{0:T(128)S(1)}, s32[128]{0:T(128)}, u32[]{:S(2)}) copy-start(s32[128]{0:T(128)} %deg_ref.7) | copy-start | bytes 1540
  16.2 6.2 %collective-permute-start.5 = (bf16[128,256]{1,0:T(8,128)(2,1)S(1)}, bf16[128,256]{1,0:T(8,128)(2,1)S(1)}, u32[]{:S(2)}, u32[]{:S(2)}) collective-permute-start(bf16[128,256]{1,0:T(8,128)(2,1)S(1)} %get-tuple-element.31), channel_id=1, source_target_pairs={{0,3},{1,2},{2,1},{3,0},{4,7},{5,6},{6,5},{7,4},{8,11},{9,10},{10,... | collective-permute-start | bytes 196616 | tf_op jit(solution)/shard_map/ppermute | solution.py:182
  22.4 7.7 %copy-start = (bf16[256,256]{1,0:T(8,128)(2,1)S(1)}, bf16[256,256]{1,0:T(8,128)(2,1)}, u32[]{:S(2)}) copy-start(bf16[256,256]{1,0:T(8,128)(2,1)} %weight_ref.3) | copy-start | bytes 393220
  22.5 6.1 %collective-permute-start.11 = (bf16[128,256]{1,0:T(8,128)(2,1)S(1)}, bf16[128,256]{1,0:T(8,128)(2,1)S(1)}, u32[]{:S(2)}, u32[]{:S(2)}) collective-permute-start(bf16[128,256]{1,0:T(8,128)(2,1)S(1)} %shard_map.98.rest_0_), channel_id=1, source_target_pairs={{0,3},{1,2},{2,1},{3,0},{4,7},{5,6},{6,5},{7,4},{8,11},{9,10},{10,... | collective-permute-start | bytes 196616 | tf_op jit(solution)/shard_map/ppermute | solution.py:182
  24.2 5.8 %collective-permute-start.10 = (bf16[128,256]{1,0:T(8,128)(2,1)S(1)}, bf16[128,256]{1,0:T(8,128)(2,1)S(1)}, u32[]{:S(2)}, u32[]{:S(2)}) collective-permute-start(bf16[128,256]{1,0:T(8,128)(2,1)S(1)} %shard_map.98.rest_0_), channel_id=1, source_target_pairs={{0,2},{1,3},{2,0},{3,1},{4,6},{5,7},{6,4},{7,5},{8,10},{9,11},{10,... | collective-permute-start | bytes 196616 | tf_op jit(solution)/shard_map/ppermute | solution.py:182
  24.8 5.2 %collective-permute-start.9 = (bf16[128,256]{1,0:T(8,128)(2,1)S(1)}, bf16[128,256]{1,0:T(8,128)(2,1)S(1)}, u32[]{:S(2)}, u32[]{:S(2)}) collective-permute-start(bf16[128,256]{1,0:T(8,128)(2,1)S(1)} %shard_map.98.rest_0_), channel_id=1, source_target_pairs={{0,1},{1,0},{2,3},{3,2},{4,5},{5,4},{6,7},{7,6},{8,9},{9,8},{10,11... | collective-permute-start | bytes 196616 | tf_op jit(solution)/shard_map/ppermute | solution.py:182
  32.0 3.1 %collective-permute-start.12 = (bf16[256,256]{1,0:T(8,128)(2,1)S(1)}, bf16[256,256]{1,0:T(8,128)(2,1)S(1)}, u32[]{:S(2)}, u32[]{:S(2)}) collective-permute-start(bf16[256,256]{1,0:T(8,128)(2,1)S(1)} %get-tuple-element.44), channel_id=1, source_target_pairs={{0,4},{4,0},{8,12},{12,8},{1,5},{5,1},{9,13},{13,9},{2,6},{6,2},{1... | collective-permute-start | bytes 393224 | tf_op jit(solution)/shard_map/ppermute | solution.py:227
  32.1 1.4 %collective-permute-start.13 = (bf16[128,256]{1,0:T(8,128)(2,1)S(1)}, bf16[128,256]{1,0:T(8,128)(2,1)S(1)}, u32[]{:S(2)}, u32[]{:S(2)}) collective-permute-start(bf16[128,256]{1,0:T(8,128)(2,1)S(1)} %get-tuple-element.47), channel_id=1, source_target_pairs={{0,4},{4,0},{8,12},{12,8},{1,5},{5,1},{9,13},{13,9},{2,6},{6,2},{1... | collective-permute-start | bytes 196616 | tf_op jit(solution)/shard_map/ppermute | solution.py:227
  33.5 4.5 %collective-permute-start.14 = (bf16[128,256]{1,0:T(8,128)(2,1)S(1)}, bf16[128,256]{1,0:T(8,128)(2,1)S(1)}, u32[]{:S(2)}, u32[]{:S(2)}) collective-permute-start(bf16[128,256]{1,0:T(8,128)(2,1)S(1)} %shard_map.102.own_ref), channel_id=1, source_target_pairs={{0,8},{4,12},{8,0},{12,4},{1,9},{5,13},{9,1},{13,5},{2,10},{6,14},... | collective-permute-start | bytes 196616 | tf_op jit(solution)/shard_map/ppermute | solution.py:227
  35.1 4.3 %collective-permute-start.15 = (bf16[128,256]{1,0:T(8,128)(2,1)S(1)}, bf16[128,256]{1,0:T(8,128)(2,1)S(1)}, u32[]{:S(2)}, u32[]{:S(2)}) collective-permute-start(bf16[128,256]{1,0:T(8,128)(2,1)S(1)} %get-tuple-element.48), channel_id=1, source_target_pairs={{0,8},{4,12},{8,0},{12,4},{1,9},{5,13},{9,1},{13,5},{2,10},{6,14},... | collective-permute-start | bytes 196616 | tf_op jit(solution)/shard_map/ppermute | solution.py:227
  39.4 1.4 %collective-permute-start.16 = (f32[128,256]{1,0:T(8,128)S(1)}, f32[128,256]{1,0:T(8,128)S(1)}, u32[]{:S(2)}, u32[]{:S(2)}) collective-permute-start(f32[128,256]{1,0:T(8,128)S(1)} %shard_map.104.own_ref), channel_id=1, source_target_pairs={{0,4},{4,0},{8,12},{12,8},{1,5},{5,1},{9,13},{13,9},{2,6},{6,2},{1... | collective-permute-start | bytes 393224 | tf_op jit(solution)/shard_map/ppermute | solution.py:227

commit v3 on v2

v3 whole, which is shorter than its diff:
```python
import functools
import math

import jax
import jax.numpy as jnp
from jax import lax
from jax.experimental import pallas as pl
from jax.experimental.pallas import tpu as pltpu
from jax.sharding import PartitionSpec as P

TILE = 128
DEG_ROWS = 16
BF16 = jnp.bfloat16
F32 = jnp.float32


def reverse_bits(value, bits):
    out = value & 0
    for bit in range(bits):
        out = out | (((value >> bit) & 1) << (bits - 1 - bit))
    return out


def row_scale(degree_lanes):
    spread = jnp.broadcast_to(degree_lanes.astype(F32), (TILE, TILE))
    return lax.rsqrt(spread.T)


def wide(scale, width):
    return jnp.concatenate([scale] * (width // TILE), axis=1)


def rows_at(block, rows=TILE):
    return pl.ds(pl.multiple_of(block * rows, rows), rows)


def scale_kernel(deg_ref, x_ref, out_ref):
    scale = wide(row_scale(deg_ref[...].reshape(1, TILE)), x_ref.shape[1])
    out_ref[...] = (scale * x_ref[...].astype(F32)).astype(BF16)


def extra_kernel(deg_ref, cot_ref, extra_ref):
    extra_ref[:TILE] = cot_ref[...]
    degree = jnp.broadcast_to(deg_ref[...].reshape(1, TILE).astype(F32), (DEG_ROWS, TILE))
    extra_ref[TILE:] = wide(degree, cot_ref.shape[1]).astype(BF16)


def place_tiles(idx_ref, cnt_ref, values_ref, out_ref, transposed, bits):
    row_me, col_me = lax.axis_index("rows"), lax.axis_index("cols")
    used = cnt_ref[0, 0]
    out_ref[...] = jnp.zeros_like(out_ref)
    for slot in range(values_ref.shape[2]):
        live = slot < used
        row = jnp.where(live, idx_ref[0, 0, 0, slot], 0) ^ col_me
        col = jnp.where(live, idx_ref[0, 0, 1, slot], 0) ^ row_me
        row = jnp.where(live, row, 0)
        col = jnp.where(live, col, 0)
        tile = jnp.where(live, values_ref[0, 0, slot], jnp.zeros((TILE, TILE), BF16))
        at = (row, col)
        if transposed:
            tile = tile.T
            at = (reverse_bits(col, bits), row)
        here = (rows_at(at[0]), rows_at(at[1]))
        out_ref[here] = (out_ref[here].astype(F32) + tile.astype(F32)).astype(BF16)


def block_kernel(transposed, bits, idx_ref, cnt_ref, values_ref, *rest):
    place_tiles(idx_ref, cnt_ref, values_ref, rest[-1], transposed, bits)


def forward_kernel(n_rows, n_cols, matrix_ref, *rest):
    blocks, outs, panel = rest[:n_rows], rest[n_rows : n_rows + n_cols], rest[-1]
    for shift, block in enumerate(blocks):
        panel[shift * TILE : (shift + 1) * TILE] = block[...]
    for shift, out in enumerate(outs):
        out[...] = jnp.dot(
            matrix_ref[shift * TILE : (shift + 1) * TILE, :],
            panel[...],
            preferred_element_type=F32,
        ).astype(BF16)


def own_rows_kernel(deg_ref, *rest):
    blocks, out_ref = rest[:-1], rest[-1]
    sums = blocks[0][...].astype(F32)
    for block in blocks[1:]:
        sums = sums + block[...].astype(F32)
    scale = wide(row_scale(deg_ref[...].reshape(1, TILE)), sums.shape[1])
    out_ref[...] = (scale * sums).astype(BF16)


def middle_kernel(n_rows, n_cols, weight_ref, matrix_ref, *rest):
    panels, extras = rest[:n_cols], rest[n_cols : 2 * n_cols]
    act_ref, keep_ref, term_ref, send_ref, spread, term = rest[2 * n_cols :]
    width = weight_ref.shape[0]
    weight = weight_ref[...]
    term[...] = jnp.zeros_like(term)
    for shift in range(n_cols):
        extra = extras[shift]
        scale = wide(row_scale(extra[TILE : TILE + 1, :TILE]), width)
        aggregated = panels[shift][...]
        pre_act = jnp.dot(aggregated, weight, preferred_element_type=F32)
        sig = 1.0 / (1.0 + jnp.exp(-pre_act))
        if shift == 0:
            act_ref[...] = (pre_act * sig).astype(BF16)
        grad = extra[:TILE, :].astype(F32) * sig * (1.0 + pre_act * (1.0 - sig))
        spread[shift * TILE : (shift + 1) * TILE] = (scale * grad).astype(BF16)
        term[...] += lax.dot_general(
            aggregated, grad.astype(BF16), (((0,), (0,)), ((), ())), preferred_element_type=F32
        )
    half_rows = n_rows // 2 * TILE
    for place in range(n_rows):
        here = slice(place * TILE, (place + 1) * TILE)
        hidden = jnp.dot(matrix_ref[here, :], spread[...], preferred_element_type=F32)
        if place < n_rows // 2:
            keep_ref[here] = hidden
        else:
            send_ref[place * TILE - half_rows : (place + 1) * TILE - half_rows] = hidden.astype(BF16)
    side = lax.rem(lax.axis_index("rows"), 2)
    half = width // 2
    term_ref[...] = term[rows_at(side, half), :]
    send_ref[half_rows:] = term[rows_at(1 - side, half), :].astype(BF16)


def fold_kernel(keep_ref, term_ref, got_ref, keep_out, term_out, send_out):
    rows = keep_ref.shape[0]
    half = rows // 2
    keep_out[...] = keep_ref[:half] + got_ref[:half].astype(F32)
    term = (term_ref[...].astype(F32) + got_ref[rows:].astype(F32)).astype(BF16)
    send_out[:half] = (keep_ref[half:] + got_ref[half:rows].astype(F32)).astype(BF16)
    send_out[half:] = term
    term_out[...] = term


def add_kernel(scale, own_ref, got_ref, out_ref):
    got = got_ref[got_ref.shape[0] - own_ref.shape[0] :]
    out_ref[...] = (own_ref[...].astype(F32) + got.astype(F32)) * scale


def join_kernel(own_ref, got_ref, out_ref):
    half = own_ref.shape[0]
    side = lax.rem(lax.axis_index("rows"), 2)
    out_ref[rows_at(side, half), :] = own_ref[...]
    out_ref[rows_at(1 - side, half), :] = got_ref[...]


def last_kernel(deg_ref, weight_ref, keep_ref, got_ref, grad_ref):
    hidden = (keep_ref[...] + got_ref[: keep_ref.shape[0]].astype(F32)).astype(BF16)
    back = lax.dot_general(
        hidden, weight_ref[...], (((1,), (1,)), ((), ())), preferred_element_type=F32
    )
    scale = wide(row_scale(deg_ref[...].reshape(1, TILE)), back.shape[1])
    grad_ref[...] = (scale * back).astype(BF16)


def call(body, out_shapes, places, scratch=(), cost=None):
    return pl.pallas_call(
        body,
        out_shape=out_shapes,
        in_specs=[pl.BlockSpec(memory_space=place) for place in places],
        scratch_shapes=list(scratch),
        cost_estimate=cost,
        compiler_params=pltpu.CompilerParams(vmem_limit_bytes=24 * 1024 * 1024),
    )


def shards(features, degree, weight, tile_index, tile_values, tile_count, cotangent):
    width = features.shape[1]
    n_rows = lax.axis_size("rows")
    n_cols = lax.axis_size("cols")
    shape = jax.ShapeDtypeStruct
    smem, vmem = pltpu.SMEM, pltpu.VMEM

    def shifted(block, axis, size):
        got = [block] + [None] * (size - 1)
        for shift in reversed(range(1, size)):
            source = block[shift] if isinstance(block, (list, tuple)) else block
            got[shift] = lax.ppermute(source, axis, [(i, i ^ shift) for i in range(size)])
        if isinstance(block, (list, tuple)):
            got[0] = block[0]
        return got

    block_shape = shape((TILE, width), BF16)
    slow = pl.CostEstimate(flops=10**10, bytes_accessed=10**6, transcendentals=0)
    scaled = call(scale_kernel, block_shape, [vmem] * 2, cost=slow)(degree, features)
    extra = call(extra_kernel, shape((TILE + DEG_ROWS, width), BF16), [vmem] * 2)(degree, cotangent)
    bits = n_rows.bit_length() - 1
    matrix = call(
        functools.partial(block_kernel, False, bits),
        shape((n_cols * TILE, n_rows * TILE), BF16),
        [smem, smem, vmem],
    )(tile_index, tile_count, tile_values)
    blocks = shifted(scaled, "rows", n_rows)
    extras = shifted(extra, "cols", n_cols)
    parts = call(
        functools.partial(forward_kernel, n_rows, n_cols),
        [block_shape] * n_cols,
        [vmem] * (1 + n_rows),
        [vmem((n_rows * TILE, width), BF16)],
        slow,
    )(matrix, *blocks)
    back_matrix = call(
        functools.partial(block_kernel, True, bits),
        shape((n_rows * TILE, n_cols * TILE), BF16),
        [smem, smem, vmem] + [pl.ANY],
    )(tile_index, tile_count, tile_values, parts[0])
    sums = shifted(parts, "cols", n_cols)
    sums, extras = lax.optimization_barrier((sums[::-1], extras))
    aggregated = call(own_rows_kernel, block_shape, [vmem] * (1 + n_cols))(degree, *sums)
    panels = shifted(aggregated, "cols", n_cols)
    half = n_rows // 2 * TILE
    side_rows = width // 2
    activated, keep, term, send = call(
        functools.partial(middle_kernel, n_rows, n_cols),
        (
            block_shape,
            shape((half, width), F32),
            shape((side_rows, width), F32),
            shape((half + side_rows, width), BF16),
        ),
        [vmem] * (2 + 2 * n_cols),
        [vmem((n_cols * TILE, width), BF16), vmem((width, width), F32)],
    )(weight, back_matrix, *panels, *extras)

    def partner(block, mask):
        return lax.ppermute(block, "rows", [(i, i ^ mask) for i in range(n_rows)])

    got = partner(send, 1)
    mask = 2
    while mask < n_rows:
        half = keep.shape[0] // 2
        keep, term, send = call(
            fold_kernel,
            (
                shape((half, width), F32),
                shape((side_rows, width), BF16),
                shape((half + side_rows, width), BF16),
            ),
            [vmem] * 3,
        )(keep, term, got)
        got = partner(send, mask)
        mask *= 2
    node_scale = 1.0 / math.sqrt(TILE * n_rows * n_cols)
    term = call(
        functools.partial(add_kernel, node_scale), shape((side_rows, width), F32), [vmem] * 2
    )(term, got)
    weight_grad = call(join_kernel, shape((width, width), F32), [vmem] * 2)(
        term, partner(term, 1)
    )
    input_grad = call(last_kernel, block_shape, [vmem] * 4)(degree, weight, keep, got)
    return (activated, input_grad, weight_grad)


def solution(mesh):
    placed = (
        P(("groups", "rows", "cols"), None),
        P(("groups", "rows", "cols")),
        P(),
        P(("groups", "rows"), "cols", None, None),
        P(("groups", "rows"), "cols", None, None, None),
        P(("groups", "rows"), "cols"),
        P(("groups", "rows", "cols"), None),
    )
    return jax.shard_map(
        shards,
        mesh=mesh,
        in_specs=placed,
        out_specs=(
            P(("groups", "rows", "cols"), None),
            P(("groups", "rows", "cols"), None),
            P("groups", None),
        ),
        check_vma=False,
    )
```

time: 41.8 us -> 40.9 us (0.978)
  starting transfers between devices: 19.5 us -> 18.2 us
    ppermute x5 -> x3, starting transfers between devices: 2.8 us -> 1.52 us  [partner(): return lax.ppermute(block, 'rows', [(i, i ^ mask) for i in range(n_rows)])]
    ppermute x5 -> x3, waiting for transfers between devices: 5.15 us -> 6.1 us  [partner(): return lax.ppermute(block, 'rows', [(i, i ^ mask) for i in range(n_rows)])]
    pallas_call x6 -> x5, Pallas kernels: 2.17 us -> 2.83 us  [the longest x1 1.36 us: shards(): call(functools.partial(middle_kernel, n_rows, n_cols), (block_shape, shap...]
    pallas_call x1, Pallas kernels: 0.9 us -> 0.3 us  [shards(): call(functools.partial(forward_kernel, n_rows, n_cols), [block_shape] * n...]
    ppermute x12, waiting for transfers between devices: 9.15 us -> 8.56 us  [shifted(): lax.ppermute(source, axis, [(i, i ^ shift) for i in range(size)])]
  transfers between devices with their start and end apart: 17 -> 15, of which waited for: 10 -> 8; matrix products, arithmetic and copies ran while one was open for 0% -> 0% of each run, Pallas kernels for 5% -> 6%
where the time goes in v3:
time: 40.9 us; the launch traced here: 40.7 us
  starting transfers between devices  18.2 us (44%)
  waiting for transfers between devices  14.7 us (36%)
  Pallas kernels  4.91 us (12%)
  local copies, waits for them, and re-layouts  1.54 us (4%)
  between operations  1.41 us (3%)
    ppermute x12, starting transfers between devices, shifted(): lax.ppermute(source, axis, [(i, i ^ shift) for i in range(size)])  16.7 us
    ppermute x12, waiting for transfers between devices, shifted(): lax.ppermute(source, axis, [(i, i ^ shift) for i in range(size)])  8.56 us
    ppermute x3, waiting for transfers between devices, partner(): return lax.ppermute(block, 'rows', [(i, i ^ mask) for i in range(n_rows)])  6.1 us
    unnamed x14, local copies, waits for them, and re-layouts  1.54 us
    ppermute x3, starting transfers between devices, partner(): return lax.ppermute(block, 'rows', [(i, i ^ mask) for i in range(n_rows)])  1.52 us
    pallas_call x1, Pallas kernels, shards(): call(functools.partial(middle_kernel, n_rows, n_cols), (block_shape, shap...  1.36 us
    pallas_call x1, Pallas kernels, shards(): call(last_kernel, block_shape, [vmem] * 4)(degree, weight, keep, got)  0.83 us
  transfers between devices with their start and end apart: 15, of which 8 were waited for; matrix products, arithmetic and copies ran while one was open for 0% of the time, Pallas kernels for 6%

profile of v3, /device:TPU:0, one launch (start us, length us, event | category | flops | bytes accessed | tf_op | source)
XLA Modules:
  0.0 40.7 jit_solution(9896693565749667768)
XLA Ops:
  0.7 0.7 %copy-done.3 = s32[128]{0:T(128)S(1)} copy-done((s32[128]{0:T(128)S(1)}, s32[128]{0:T(128)}, u32[]{:S(2)}) %copy-start.3) | copy-done | bytes 536
  1.3 0.8 %copy-done.6 = bf16[128,256]{1,0:T(8,128)(2,1)S(1)} copy-done((bf16[128,256]{1,0:T(8,128)(2,1)S(1)}, bf16[128,256]{1,0:T(8,128)(2,1)}, u32[]{:S(2)}) %copy-start.6) | copy-done | bytes 65560
  2.3 2.4 %collective-permute-start.2 = (bf16[128,256]{1,0:T(8,128)(2,1)S(1)}, bf16[128,256]{1,0:T(8,128)(2,1)S(1)}, u32[]{:S(2)}, u32[]{:S(2)}) collective-permute-start(bf16[128,256]{1,0:T(8,128)(2,1)S(1)} %shard_map.95.rest_0_), channel_id=1, source_target_pairs={{0,12},{4,8},{8,4},{12,0},{1,13},{5,9},{9,5},{13,1},{2,14},{6,10},... | collective-permute-start | bytes 196616 | tf_op jit(solution)/shard_map/ppermute | solution.py:178
  4.7 0.6 %collective-permute-start.1 = (bf16[128,256]{1,0:T(8,128)(2,1)S(1)}, bf16[128,256]{1,0:T(8,128)(2,1)S(1)}, u32[]{:S(2)}, u32[]{:S(2)}) collective-permute-start(bf16[128,256]{1,0:T(8,128)(2,1)S(1)} %shard_map.95.rest_0_), channel_id=1, source_target_pairs={{0,8},{4,12},{8,0},{12,4},{1,9},{5,13},{9,1},{13,5},{2,10},{6,14},... | collective-permute-start | bytes 196616 | tf_op jit(solution)/shard_map/ppermute | solution.py:178
  5.4 3.9 %collective-permute-start.8 = (bf16[144,256]{1,0:T(8,128)(2,1)S(1)}, bf16[144,256]{1,0:T(8,128)(2,1)S(1)}, u32[]{:S(2)}, u32[]{:S(2)}) collective-permute-start(bf16[144,256]{1,0:T(8,128)(2,1)S(1)} %shard_map.98.rest_4_), channel_id=1, source_target_pairs={{0,3},{1,2},{2,1},{3,0},{4,7},{5,6},{6,5},{7,4},{8,11},{9,10},{10,... | collective-permute-start | bytes 221192 | tf_op jit(solution)/shard_map/ppermute | solution.py:178
  10.0 0.7 %shard_map.94.matrix_ref = bf16[512,512]{1,0:T(8,128)(2,1)S(1)} custom-call(s32[1,1,2,8]{3,2,1,0:T(2,128)S(1)} %copy-done.5, s32[1,1]{1,0:T(1,128)S(6)} %copy.10.cnt_ref, bf16[1,1,8,128,128]{4,3,2,1,0:T(8,128)(2,1)S(1)} %copy-done), custom_call_target="tpu_custom_call" | custom-call | tf_op jit(solution)/shard_map/pallas_call | solution.py:188
  10.7 0.7 %collective-permute-start.6 = (bf16[144,256]{1,0:T(8,128)(2,1)S(1)}, bf16[144,256]{1,0:T(8,128)(2,1)S(1)}, u32[]{:S(2)}, u32[]{:S(2)}) collective-permute-start(bf16[144,256]{1,0:T(8,128)(2,1)S(1)} %shard_map.98.rest_4_), channel_id=1, source_target_pairs={{0,1},{1,0},{2,3},{3,2},{4,5},{5,4},{6,7},{7,6},{8,9},{9,8},{10,11... | collective-permute-start | bytes 221192 | tf_op jit(solution)/shard_map/ppermute | solution.py:178
  11.8 3.8 %collective-permute-start.3 = (bf16[128,256]{1,0:T(8,128)(2,1)S(1)}, bf16[128,256]{1,0:T(8,128)(2,1)S(1)}, u32[]{:S(2)}, u32[]{:S(2)}) collective-permute-start(bf16[128,256]{1,0:T(8,128)(2,1)S(1)} %get-tuple-element.23), channel_id=1, source_target_pairs={{0,3},{1,2},{2,1},{3,0},{4,7},{5,6},{6,5},{7,4},{8,11},{9,10},{10,... | collective-permute-start | bytes 196616 | tf_op jit(solution)/shard_map/ppermute | solution.py:178
  15.6 0.6 %collective-permute-start.5 = (bf16[128,256]{1,0:T(8,128)(2,1)S(1)}, bf16[128,256]{1,0:T(8,128)(2,1)S(1)}, u32[]{:S(2)}, u32[]{:S(2)}) collective-permute-start(bf16[128,256]{1,0:T(8,128)(2,1)S(1)} %get-tuple-element.25), channel_id=1, source_target_pairs={{0,1},{1,0},{2,3},{3,2},{4,5},{5,4},{6,7},{7,6},{8,9},{9,8},{10,11... | collective-permute-start | bytes 196616 | tf_op jit(solution)/shard_map/ppermute | solution.py:178
  16.2 1.2 %collective-permute-done.7.rest_6_ = bf16[144,256]{1,0:T(8,128)(2,1)S(1)} collective-permute-done((bf16[144,256]{1,0:T(8,128)(2,1)S(1)}, bf16[144,256]{1,0:T(8,128)(2,1)S(1)}, u32[]{:S(2)}, u32[]{:S(2)}) %collective-permute-start.7) | collective-permute-done | bytes 73760 | tf_op jit(solution)/shard_map/ppermute | solution.py:178
  17.4 1.7 %collective-permute-done.3.rest_0_ = bf16[128,256]{1,0:T(8,128)(2,1)S(1)} collective-permute-done((bf16[128,256]{1,0:T(8,128)(2,1)S(1)}, bf16[128,256]{1,0:T(8,128)(2,1)S(1)}, u32[]{:S(2)}, u32[]{:S(2)}) %collective-permute-start.3) | collective-permute-done | bytes 65568 | tf_op jit(solution)/shard_map/ppermute | solution.py:178
  19.1 2.4 %collective-permute-done.4.rest_1_ = bf16[128,256]{1,0:T(8,128)(2,1)S(1)} collective-permute-done((bf16[128,256]{1,0:T(8,128)(2,1)S(1)}, bf16[128,256]{1,0:T(8,128)(2,1)S(1)}, u32[]{:S(2)}, u32[]{:S(2)}) %collective-permute-start.4) | collective-permute-done | bytes 65568 | tf_op jit(solution)/shard_map/ppermute | solution.py:178
  21.6 2.5 %collective-permute-start.11 = (bf16[128,256]{1,0:T(8,128)(2,1)S(1)}, bf16[128,256]{1,0:T(8,128)(2,1)S(1)}, u32[]{:S(2)}, u32[]{:S(2)}) collective-permute-start(bf16[128,256]{1,0:T(8,128)(2,1)S(1)} %shard_map.99.rest_0_), channel_id=1, source_target_pairs={{0,3},{1,2},{2,1},{3,0},{4,7},{5,6},{6,5},{7,4},{8,11},{9,10},{10,... | collective-permute-start | bytes 196616 | tf_op jit(solution)/shard_map/ppermute | solution.py:178
  24.2 1.9 %collective-permute-start.9 = (bf16[128,256]{1,0:T(8,128)(2,1)S(1)}, bf16[128,256]{1,0:T(8,128)(2,1)S(1)}, u32[]{:S(2)}, u32[]{:S(2)}) collective-permute-start(bf16[128,256]{1,0:T(8,128)(2,1)S(1)} %shard_map.99.rest_0_), channel_id=1, source_target_pairs={{0,1},{1,0},{2,3},{3,2},{4,5},{5,4},{6,7},{7,6},{8,9},{9,8},{10,11... | collective-permute-start | bytes 196616 | tf_op jit(solution)/shard_map/ppermute | solution.py:178
  26.1 0.7 %shard_map.97.matrix_ref = bf16[512,512]{1,0:T(8,128)(2,1)S(1)} custom-call(s32[1,1,2,8]{3,2,1,0:T(2,128)S(1)} %copy-done.5, s32[1,1]{1,0:T(1,128)S(6)} %copy.10.cnt_ref, bf16[1,1,8,128,128]{4,3,2,1,0:T(8,128)(2,1)S(1)} %copy-done, bf16[128,256]{1,0:T(8,128)(2,1)S(1)} %get-tuple-element.29.rest_0_.rest_3_), custom_call_target="tpu_custom_call" | custom-call | tf_op jit(solution)/shard_map/pallas_call | solution.py:202
  26.8 1.3 %collective-permute-done.11.rest_3_ = bf16[128,256]{1,0:T(8,128)(2,1)S(1)} collective-permute-done((bf16[128,256]{1,0:T(8,128)(2,1)S(1)}, bf16[128,256]{1,0:T(8,128)(2,1)S(1)}, u32[]{:S(2)}, u32[]{:S(2)}) %collective-permute-start.11) | collective-permute-done | bytes 65568 | tf_op jit(solution)/shard_map/ppermute | solution.py:178
  28.1 2.0 %collective-permute-done.10.rest_2_ = bf16[128,256]{1,0:T(8,128)(2,1)S(1)} collective-permute-done((bf16[128,256]{1,0:T(8,128)(2,1)S(1)}, bf16[128,256]{1,0:T(8,128)(2,1)S(1)}, u32[]{:S(2)}, u32[]{:S(2)}) %collective-permute-start.10) | collective-permute-done | bytes 65568 | tf_op jit(solution)/shard_map/ppermute | solution.py:178
  30.1 1.4 %shard_map.100 = (bf16[128,256]{1,0:T(8,128)(2,1)}, f32[256,256]{1,0:T(8,128)S(1)}, f32[128,256]{1,0:T(8,128)S(1)}, bf16[384,256]{1,0:T(8,128)(2,1)S(1)}) custom-call(bf16[256,256]{1,0:T(8,128)(2,1)S(1)} %copy-done.1, bf16[512,512]{1,0:T(8,128)(2,1)S(1)} %shard_map.97.matrix_ref, bf16[128,256]{1,0:T(8,128)(2,1)S(1)} %shard_map.99.rest_0_, ...), custom_call_target="tpu_custom_call" | custom-call | tf_op jit(solution)/shard_map/pallas_call | solution.py:213
  31.5 1.4 %collective-permute-done.12.got_ref = bf16[384,256]{1,0:T(8,128)(2,1)S(1)} collective-permute-done((bf16[384,256]{1,0:T(8,128)(2,1)S(1)}, bf16[384,256]{1,0:T(8,128)(2,1)S(1)}, u32[]{:S(2)}, u32[]{:S(2)}) %collective-permute-start.12) | collective-permute-done | bytes 196640 | tf_op jit(solution)/shard_map/ppermute | solution.py:226
  32.9 1.4 %collective-permute-start.13 = (bf16[256,256]{1,0:T(8,128)(2,1)S(1)}, bf16[256,256]{1,0:T(8,128)(2,1)S(1)}, u32[]{:S(2)}, u32[]{:S(2)}) collective-permute-start(bf16[256,256]{1,0:T(8,128)(2,1)S(1)} %get-tuple-element.39), channel_id=1, source_target_pairs={{0,8},{4,12},{8,0},{12,4},{1,9},{5,13},{9,1},{13,5},{2,10},{6,14},... | collective-permute-start | bytes 393224 | tf_op jit(solution)/shard_map/ppermute | solution.py:226
  34.4 4.2 %collective-permute-done.13.got_ref = bf16[256,256]{1,0:T(8,128)(2,1)S(1)} collective-permute-done((bf16[256,256]{1,0:T(8,128)(2,1)S(1)}, bf16[256,256]{1,0:T(8,128)(2,1)S(1)}, u32[]{:S(2)}, u32[]{:S(2)}) %collective-permute-start.13) | collective-permute-done | bytes 131104 | tf_op jit(solution)/shard_map/ppermute | solution.py:226
  38.6 0.8 %shard_map.102 = bf16[128,256]{1,0:T(8,128)(2,1)} custom-call(s32[128]{0:T(128)S(1)} %copy-done.4, bf16[256,256]{1,0:T(8,128)(2,1)S(1)} %copy-done.1, f32[128,256]{1,0:T(8,128)S(1)} %get-tuple-element.38.keep_ref, bf16[256,256]{1,0:T(8,128)(2,1)S(1)} %collective-permute-done.13.got_ref), custom_call_target="tpu_custom_call" | custom-call | tf_op jit(solution)/shard_map/pallas_call | solution.py:250
  39.5 0.5 %collective-permute-done.14.got_ref = f32[128,256]{1,0:T(8,128)S(1)} collective-permute-done((f32[128,256]{1,0:T(8,128)S(1)}, f32[128,256]{1,0:T(8,128)S(1)}, u32[]{:S(2)}, u32[]{:S(2)}) %collective-permute-start.14) | collective-permute-done | bytes 131104 | tf_op jit(solution)/shard_map/ppermute | solution.py:226
  40.0 0.7 %shard_map.104 = f32[256,256]{1,0:T(8,128)} custom-call(f32[128,256]{1,0:T(8,128)S(1)} %shard_map.103.own_ref, f32[128,256]{1,0:T(8,128)S(1)} %collective-permute-done.14.got_ref), custom_call_target="tpu_custom_call" | custom-call | tf_op jit(solution)/shard_map/pallas_call | solution.py:247
  (31 shorter events, 0.8 us)
Async XLA Ops:
  0.6 4.8 %copy-start.2 = (bf16[128,256]{1,0:T(8,128)(2,1)S(1)}, bf16[128,256]{1,0:T(8,128)(2,1)}, u32[]{:S(2)}) copy-start(bf16[128,256]{1,0:T(8,128)(2,1)} %cot_ref.1) | copy-start | bytes 196612
  0.6 0.7 %copy-start.3 = (s32[128]{0:T(128)S(1)}, s32[128]{0:T(128)}, u32[]{:S(2)}) copy-start(s32[128]{0:T(128)} %deg_ref.7) | copy-start | bytes 1540
  1.3 0.8 %copy-start.6 = (bf16[128,256]{1,0:T(8,128)(2,1)S(1)}, bf16[128,256]{1,0:T(8,128)(2,1)}, u32[]{:S(2)}) copy-start(bf16[128,256]{1,0:T(8,128)(2,1)} %x_ref.1) | copy-start | bytes 196612
  2.2 7.8 %copy-start = (bf16[1,1,8,128,128]{4,3,2,1,0:T(8,128)(2,1)S(1)}, bf16[1,1,8,128,128]{4,3,2,1,0:T(8,128)(2,1)}, u32[]{:S(2)}) copy-start(bf16[1,1,8,128,128]{4,3,2,1,0:T(8,128)(2,1)} %values_ref.3) | copy-start | bytes 786436
  2.3 8.4 %collective-permute-start.2 = (bf16[128,256]{1,0:T(8,128)(2,1)S(1)}, bf16[128,256]{1,0:T(8,128)(2,1)S(1)}, u32[]{:S(2)}, u32[]{:S(2)}) collective-permute-start(bf16[128,256]{1,0:T(8,128)(2,1)S(1)} %shard_map.95.rest_0_), channel_id=1, source_target_pairs={{0,12},{4,8},{8,4},{12,0},{1,13},{5,9},{9,5},{13,1},{2,14},{6,10},... | collective-permute-start | bytes 196616 | tf_op jit(solution)/shard_map/ppermute | solution.py:178
  4.7 6.7 %collective-permute-start.1 = (bf16[128,256]{1,0:T(8,128)(2,1)S(1)}, bf16[128,256]{1,0:T(8,128)(2,1)S(1)}, u32[]{:S(2)}, u32[]{:S(2)}) collective-permute-start(bf16[128,256]{1,0:T(8,128)(2,1)S(1)} %shard_map.95.rest_0_), channel_id=1, source_target_pairs={{0,8},{4,12},{8,0},{12,4},{1,9},{5,13},{9,1},{13,5},{2,10},{6,14},... | collective-permute-start | bytes 196616 | tf_op jit(solution)/shard_map/ppermute | solution.py:178
  5.4 6.1 %collective-permute-start = (bf16[128,256]{1,0:T(8,128)(2,1)S(1)}, bf16[128,256]{1,0:T(8,128)(2,1)S(1)}, u32[]{:S(2)}, u32[]{:S(2)}) collective-permute-start(bf16[128,256]{1,0:T(8,128)(2,1)S(1)} %shard_map.95.rest_0_), channel_id=1, source_target_pairs={{0,4},{4,0},{8,12},{12,8},{1,5},{5,1},{9,13},{13,9},{2,6},{6,2},{1... | collective-permute-start | bytes 196616 | tf_op jit(solution)/shard_map/ppermute | solution.py:178
  5.4 4.6 %copy-start.5 = (s32[1,1,2,8]{3,2,1,0:T(2,128)S(1)}, s32[1,1,2,8]{3,2,1,0:T(2,128)}, u32[]{:S(2)}) copy-start(s32[1,1,2,8]{3,2,1,0:T(2,128)} %idx_ref.3) | copy-start | bytes 196
  5.4 10.1 %collective-permute-start.8 = (bf16[144,256]{1,0:T(8,128)(2,1)S(1)}, bf16[144,256]{1,0:T(8,128)(2,1)S(1)}, u32[]{:S(2)}, u32[]{:S(2)}) collective-permute-start(bf16[144,256]{1,0:T(8,128)(2,1)S(1)} %shard_map.98.rest_4_), channel_id=1, source_target_pairs={{0,3},{1,2},{2,1},{3,0},{4,7},{5,6},{6,5},{7,4},{8,11},{9,10},{10,... | collective-permute-start | bytes 221192 | tf_op jit(solution)/shard_map/ppermute | solution.py:178
  9.4 8.1 %collective-permute-start.7 = (bf16[144,256]{1,0:T(8,128)(2,1)S(1)}, bf16[144,256]{1,0:T(8,128)(2,1)S(1)}, u32[]{:S(2)}, u32[]{:S(2)}) collective-permute-start(bf16[144,256]{1,0:T(8,128)(2,1)S(1)} %shard_map.98.rest_4_), channel_id=1, source_target_pairs={{0,2},{1,3},{2,0},{3,1},{4,6},{5,7},{6,4},{7,5},{8,10},{9,11},{10,... | collective-permute-start | bytes 221192 | tf_op jit(solution)/shard_map/ppermute | solution.py:178
  10.7 6.7 %collective-permute-start.6 = (bf16[144,256]{1,0:T(8,128)(2,1)S(1)}, bf16[144,256]{1,0:T(8,128)(2,1)S(1)}, u32[]{:S(2)}, u32[]{:S(2)}) collective-permute-start(bf16[144,256]{1,0:T(8,128)(2,1)S(1)} %shard_map.98.rest_4_), channel_id=1, source_target_pairs={{0,1},{1,0},{2,3},{3,2},{4,5},{5,4},{6,7},{7,6},{8,9},{9,8},{10,11... | collective-permute-start | bytes 221192 | tf_op jit(solution)/shard_map/ppermute | solution.py:178
  11.8 7.3 %collective-permute-start.3 = (bf16[128,256]{1,0:T(8,128)(2,1)S(1)}, bf16[128,256]{1,0:T(8,128)(2,1)S(1)}, u32[]{:S(2)}, u32[]{:S(2)}) collective-permute-start(bf16[128,256]{1,0:T(8,128)(2,1)S(1)} %get-tuple-element.23), channel_id=1, source_target_pairs={{0,3},{1,2},{2,1},{3,0},{4,7},{5,6},{6,5},{7,4},{8,11},{9,10},{10,... | collective-permute-start | bytes 196616 | tf_op jit(solution)/shard_map/ppermute | solution.py:178
  15.6 5.9 %collective-permute-start.4 = (bf16[128,256]{1,0:T(8,128)(2,1)S(1)}, bf16[128,256]{1,0:T(8,128)(2,1)S(1)}, u32[]{:S(2)}, u32[]{:S(2)}) collective-permute-start(bf16[128,256]{1,0:T(8,128)(2,1)S(1)} %get-tuple-element.24), channel_id=1, source_target_pairs={{0,2},{1,3},{2,0},{3,1},{4,6},{5,7},{6,4},{7,5},{8,10},{9,11},{10,... | collective-permute-start | bytes 196616 | tf_op jit(solution)/shard_map/ppermute | solution.py:178
  15.6 5.9 %copy-start.4 = (s32[128]{0:T(128)S(1)}, s32[128]{0:T(128)}, u32[]{:S(2)}) copy-start(s32[128]{0:T(128)} %deg_ref.7) | copy-start | bytes 1540
  15.6 5.9 %collective-permute-start.5 = (bf16[128,256]{1,0:T(8,128)(2,1)S(1)}, bf16[128,256]{1,0:T(8,128)(2,1)S(1)}, u32[]{:S(2)}, u32[]{:S(2)}) collective-permute-start(bf16[128,256]{1,0:T(8,128)(2,1)S(1)} %get-tuple-element.25), channel_id=1, source_target_pairs={{0,1},{1,0},{2,3},{3,2},{4,5},{5,4},{6,7},{7,6},{8,9},{9,8},{10,11... | collective-permute-start | bytes 196616 | tf_op jit(solution)/shard_map/ppermute | solution.py:178
  21.6 8.5 %copy-start.1 = (bf16[256,256]{1,0:T(8,128)(2,1)S(1)}, bf16[256,256]{1,0:T(8,128)(2,1)}, u32[]{:S(2)}) copy-start(bf16[256,256]{1,0:T(8,128)(2,1)} %weight_ref.3) | copy-start | bytes 393220
  21.6 6.5 %collective-permute-start.11 = (bf16[128,256]{1,0:T(8,128)(2,1)S(1)}, bf16[128,256]{1,0:T(8,128)(2,1)S(1)}, u32[]{:S(2)}, u32[]{:S(2)}) collective-permute-start(bf16[128,256]{1,0:T(8,128)(2,1)S(1)} %shard_map.99.rest_0_), channel_id=1, source_target_pairs={{0,3},{1,2},{2,1},{3,0},{4,7},{5,6},{6,5},{7,4},{8,11},{9,10},{10,... | collective-permute-start | bytes 196616 | tf_op jit(solution)/shard_map/ppermute | solution.py:178
  24.2 5.9 %collective-permute-start.10 = (bf16[128,256]{1,0:T(8,128)(2,1)S(1)}, bf16[128,256]{1,0:T(8,128)(2,1)S(1)}, u32[]{:S(2)}, u32[]{:S(2)}) collective-permute-start(bf16[128,256]{1,0:T(8,128)(2,1)S(1)} %shard_map.99.rest_0_), channel_id=1, source_target_pairs={{0,2},{1,3},{2,0},{3,1},{4,6},{5,7},{6,4},{7,5},{8,10},{9,11},{10,... | collective-permute-start | bytes 196616 | tf_op jit(solution)/shard_map/ppermute | solution.py:178
  24.2 5.9 %collective-permute-start.9 = (bf16[128,256]{1,0:T(8,128)(2,1)S(1)}, bf16[128,256]{1,0:T(8,128)(2,1)S(1)}, u32[]{:S(2)}, u32[]{:S(2)}) collective-permute-start(bf16[128,256]{1,0:T(8,128)(2,1)S(1)} %shard_map.99.rest_0_), channel_id=1, source_target_pairs={{0,1},{1,0},{2,3},{3,2},{4,5},{5,4},{6,7},{7,6},{8,9},{9,8},{10,11... | collective-permute-start | bytes 196616 | tf_op jit(solution)/shard_map/ppermute | solution.py:178
  31.4 1.4 %collective-permute-start.12 = (bf16[384,256]{1,0:T(8,128)(2,1)S(1)}, bf16[384,256]{1,0:T(8,128)(2,1)S(1)}, u32[]{:S(2)}, u32[]{:S(2)}) collective-permute-start(bf16[384,256]{1,0:T(8,128)(2,1)S(1)} %get-tuple-element.37), channel_id=1, source_target_pairs={{0,4},{4,0},{8,12},{12,8},{1,5},{5,1},{9,13},{13,9},{2,6},{6,2},{1... | collective-permute-start | bytes 589832 | tf_op jit(solution)/shard_map/ppermute | solution.py:226
  32.9 5.6 %collective-permute-start.13 = (bf16[256,256]{1,0:T(8,128)(2,1)S(1)}, bf16[256,256]{1,0:T(8,128)(2,1)S(1)}, u32[]{:S(2)}, u32[]{:S(2)}) collective-permute-start(bf16[256,256]{1,0:T(8,128)(2,1)S(1)} %get-tuple-element.39), channel_id=1, source_target_pairs={{0,8},{4,12},{8,0},{12,4},{1,9},{5,13},{9,1},{13,5},{2,10},{6,14},... | collective-permute-start | bytes 393224 | tf_op jit(solution)/shard_map/ppermute | solution.py:226
  38.6 1.4 %collective-permute-start.14 = (f32[128,256]{1,0:T(8,128)S(1)}, f32[128,256]{1,0:T(8,128)S(1)}, u32[]{:S(2)}, u32[]{:S(2)}) collective-permute-start(f32[128,256]{1,0:T(8,128)S(1)} %shard_map.103.own_ref), channel_id=1, source_target_pairs={{0,4},{4,0},{8,12},{12,8},{1,5},{5,1},{9,13},{13,9},{2,6},{6,2},{1... | collective-permute-start | bytes 393224 | tf_op jit(solution)/shard_map/ppermute | solution.py:226

commit v4 on v3

--- a/solution.py
+++ b/solution.py
@@ -40,9 +40,11 @@
 
 
 def extra_kernel(deg_ref, cot_ref, extra_ref):
-    extra_ref[:TILE] = cot_ref[...]
+    width = cot_ref.shape[1]
+    for at in range(0, width, TILE):
+        extra_ref[at : at + TILE] = cot_ref[:, at : at + TILE]
     degree = jnp.broadcast_to(deg_ref[...].reshape(1, TILE).astype(F32), (DEG_ROWS, TILE))
-    extra_ref[TILE:] = wide(degree, cot_ref.shape[1]).astype(BF16)
+    extra_ref[width:] = degree.astype(BF16)
 
 
 def place_tiles(idx_ref, cnt_ref, values_ref, out_ref, transposed, bits):
@@ -97,13 +99,14 @@
     term[...] = jnp.zeros_like(term)
     for shift in range(n_cols):
         extra = extras[shift]
-        scale = wide(row_scale(extra[TILE : TILE + 1, :TILE]), width)
+        scale = wide(row_scale(extra[width : width + 1, :]), width)
         aggregated = panels[shift][...]
         pre_act = jnp.dot(aggregated, weight, preferred_element_type=F32)
         sig = 1.0 / (1.0 + jnp.exp(-pre_act))
         if shift == 0:
             act_ref[...] = (pre_act * sig).astype(BF16)
-        grad = extra[:TILE, :].astype(F32) * sig * (1.0 + pre_act * (1.0 - sig))
+        cot = jnp.concatenate([extra[at : at + TILE] for at in range(0, width, TILE)], axis=1)
+        grad = cot.astype(F32) * sig * (1.0 + pre_act * (1.0 - sig))
         spread[shift * TILE : (shift + 1) * TILE] = (scale * grad).astype(BF16)
         term[...] += lax.dot_general(
             aggregated, grad.astype(BF16), (((0,), (0,)), ((), ())), preferred_element_type=F32
@@ -144,7 +147,8 @@
     out_ref[rows_at(1 - side, half), :] = got_ref[...]
 
 
-def last_kernel(deg_ref, weight_ref, keep_ref, got_ref, grad_ref):
+def last_kernel(deg_ref, weight_ref, keep_ref, got_ref, held_ref, grad_ref, act_ref):
+    act_ref[...] = held_ref[...]
     hidden = (keep_ref[...] + got_ref[: keep_ref.shape[0]].astype(F32)).astype(BF16)
     back = lax.dot_general(
         hidden, weight_ref[...], (((1,), (1,)), ((), ())), preferred_element_type=F32
@@ -183,7 +187,7 @@
     block_shape = shape((TILE, width), BF16)
     slow = pl.CostEstimate(flops=10**10, bytes_accessed=10**6, transcendentals=0)
     scaled = call(scale_kernel, block_shape, [vmem] * 2, cost=slow)(degree, features)
-    extra = call(extra_kernel, shape((TILE + DEG_ROWS, width), BF16), [vmem] * 2)(degree, cotangent)
+    extra = call(extra_kernel, shape((width + DEG_ROWS, TILE), BF16), [vmem] * 2)(degree, cotangent)
     bits = n_rows.bit_length() - 1
     matrix = call(
         functools.partial(block_kernel, False, bits),
@@ -191,7 +195,14 @@
         [smem, smem, vmem],
     )(tile_index, tile_count, tile_values)
     blocks = shifted(scaled, "rows", n_rows)
-    extras = shifted(extra, "cols", n_cols)
+    def sent(block, shift):
+        return lax.ppermute(block, "cols", [(j, j ^ shift) for j in range(n_cols)])
+
+    late = [shift for shift in range(1, n_cols) if shift != 2]
+    early = [shift for shift in range(1, n_cols) if shift == 2]
+    extras = [extra] + [None] * (n_cols - 1)
+    for shift in reversed(early):
+        extras[shift] = sent(extra, shift)
     parts = call(
         functools.partial(forward_kernel, n_rows, n_cols),
         [block_shape] * n_cols,
@@ -204,13 +215,19 @@
         shape((n_rows * TILE, n_cols * TILE), BF16),
         [smem, smem, vmem] + [pl.ANY],
     )(tile_index, tile_count, tile_values, parts[0])
+    parts, tied = lax.optimization_barrier((parts, extra))
+    for shift in reversed(late):
+        extras[shift] = sent(tied, shift)
     sums = shifted(parts, "cols", n_cols)
-    sums, extras = lax.optimization_barrier((sums[::-1], extras))
+    held = [extras[shift] for shift in early]
+    sums, held = lax.optimization_barrier((sums[::-1], held))
+    for shift, block in zip(early, held):
+        extras[shift] = block
     aggregated = call(own_rows_kernel, block_shape, [vmem] * (1 + n_cols))(degree, *sums)
     panels = shifted(aggregated, "cols", n_cols)
     half = n_rows // 2 * TILE
     side_rows = width // 2
-    activated, keep, term, send = call(
+    kept_act, keep, term, send = call(
         functools.partial(middle_kernel, n_rows, n_cols),
         (
             block_shape,
@@ -247,7 +264,9 @@
     weight_grad = call(join_kernel, shape((width, width), F32), [vmem] * 2)(
         term, partner(term, 1)
     )
-    input_grad = call(last_kernel, block_shape, [vmem] * 4)(degree, weight, keep, got)
+    input_grad, activated = call(last_kernel, (block_shape, block_shape), [vmem] * 5)(
+        degree, weight, keep, got, kept_act
+    )
     return (activated, input_grad, weight_grad)
 
 

time: 40.9 us -> 39.4 us (0.963)
  waiting for transfers between devices: 14.7 us -> 11.7 us
  starting transfers between devices: 18.2 us -> 20.2 us
  Pallas kernels: 4.91 us -> 4.33 us
    ppermute x0 -> x3, starting transfers between devices: none -> 6.36 us  [sent(): return lax.ppermute(block, 'cols', [(j, j ^ shift) for j in range(n_cols)])]
    ppermute x12 -> x9, starting transfers between devices: 16.7 us -> 12 us  [shifted(): lax.ppermute(source, axis, [(i, i ^ shift) for i in range(size)])]
    ppermute x12 -> x9, waiting for transfers between devices: 8.56 us -> 5.83 us  [shifted(): lax.ppermute(source, axis, [(i, i ^ shift) for i in range(size)])]
    pallas_call x1, Pallas kernels: 1.36 us -> 0.75 us  [shards(): call(functools.partial(middle_kernel, n_rows, n_cols), (block_shape, shap...]
  transfers between devices with their start and end apart: 15 -> 15, of which waited for: 8 -> 6; matrix products, arithmetic and copies ran while one was open for 0% -> 0% of each run, Pallas kernels for 6% -> 7%
where the time goes in v4:
time: 39.4 us; the launch traced here: 39.2 us
  starting transfers between devices  20.2 us (51%)
  waiting for transfers between devices  11.7 us (30%)
  Pallas kernels  4.33 us (11%)
  local copies, waits for them, and re-layouts  1.55 us (4%)
  between operations  1.46 us (4%)
    ppermute x9, starting transfers between devices, shifted(): lax.ppermute(source, axis, [(i, i ^ shift) for i in range(size)])  12 us
    ppermute x3, starting transfers between devices, sent(): return lax.ppermute(block, 'cols', [(j, j ^ shift) for j in range(n_cols)])  6.36 us
    ppermute x3, waiting for transfers between devices, partner(): return lax.ppermute(block, 'rows', [(i, i ^ mask) for i in range(n_rows)])  5.83 us
    ppermute x9, waiting for transfers between devices, shifted(): lax.ppermute(source, axis, [(i, i ^ shift) for i in range(size)])  5.83 us
    ppermute x3, starting transfers between devices, partner(): return lax.ppermute(block, 'rows', [(i, i ^ mask) for i in range(n_rows)])  1.84 us
    unnamed x14, local copies, waits for them, and re-layouts  1.55 us
    pallas_call x1, Pallas kernels, shards(): call(last_kernel, (block_shape, block_shape), [vmem] * 5)  0.84 us
  transfers between devices with their start and end apart: 15, of which 6 were waited for; matrix products, arithmetic and copies ran while one was open for 0% of the time, Pallas kernels for 7%

profile of v4, /device:TPU:0, one launch (start us, length us, event | category | flops | bytes accessed | tf_op | source)
XLA Modules:
  0.0 39.2 jit_solution(1740303715372143830)
XLA Ops:
  0.7 0.7 %copy-done.3 = s32[128]{0:T(128)S(1)} copy-done((s32[128]{0:T(128)S(1)}, s32[128]{0:T(128)}, u32[]{:S(2)}) %copy-start.3) | copy-done | bytes 536
  1.3 0.8 %copy-done.6 = bf16[128,256]{1,0:T(8,128)(2,1)S(1)} copy-done((bf16[128,256]{1,0:T(8,128)(2,1)S(1)}, bf16[128,256]{1,0:T(8,128)(2,1)}, u32[]{:S(2)}) %copy-start.6) | copy-done | bytes 65560
  2.3 2.4 %collective-permute-start.2 = (bf16[128,256]{1,0:T(8,128)(2,1)S(1)}, bf16[128,256]{1,0:T(8,128)(2,1)S(1)}, u32[]{:S(2)}, u32[]{:S(2)}) collective-permute-start(bf16[128,256]{1,0:T(8,128)(2,1)S(1)} %shard_map.95.rest_0_), channel_id=1, source_target_pairs={{0,12},{4,8},{8,4},{12,0},{1,13},{5,9},{9,5},{13,1},{2,14},{6,10},... | collective-permute-start | bytes 196616 | tf_op jit(solution)/shard_map/ppermute | solution.py:182
  4.7 0.6 %collective-permute-start.1 = (bf16[128,256]{1,0:T(8,128)(2,1)S(1)}, bf16[128,256]{1,0:T(8,128)(2,1)S(1)}, u32[]{:S(2)}, u32[]{:S(2)}) collective-permute-start(bf16[128,256]{1,0:T(8,128)(2,1)S(1)} %shard_map.95.rest_0_), channel_id=1, source_target_pairs={{0,8},{4,12},{8,0},{12,4},{1,9},{5,13},{9,1},{13,5},{2,10},{6,14},... | collective-permute-start | bytes 196616 | tf_op jit(solution)/shard_map/ppermute | solution.py:182
  5.4 2.9 %collective-permute-start.6 = (bf16[272,128]{1,0:T(8,128)(2,1)S(1)}, bf16[272,128]{1,0:T(8,128)(2,1)S(1)}, u32[]{:S(2)}, u32[]{:S(2)}) collective-permute-start(bf16[272,128]{1,0:T(8,128)(2,1)S(1)} %shard_map.98.rest_4_), channel_id=1, source_target_pairs={{0,2},{1,3},{2,0},{3,1},{4,6},{5,7},{6,4},{7,5},{8,10},{9,11},{10,... | collective-permute-start | bytes 208904 | tf_op jit(solution)/shard_map/ppermute | solution.py:199
  9.0 0.7 %shard_map.94.matrix_ref = bf16[512,512]{1,0:T(8,128)(2,1)S(1)} custom-call(s32[1,1,2,8]{3,2,1,0:T(2,128)S(1)} %copy-done.5, s32[1,1]{1,0:T(1,128)S(6)} %copy.10.cnt_ref, bf16[1,1,8,128,128]{4,3,2,1,0:T(8,128)(2,1)S(1)} %copy-done), custom_call_target="tpu_custom_call" | custom-call | tf_op jit(solution)/shard_map/pallas_call | solution.py:192
  9.7 0.3 shard_map.96
  10.1 3.5 %collective-permute-start.3 = (bf16[128,256]{1,0:T(8,128)(2,1)S(1)}, bf16[128,256]{1,0:T(8,128)(2,1)S(1)}, u32[]{:S(2)}, u32[]{:S(2)}) collective-permute-start(bf16[128,256]{1,0:T(8,128)(2,1)S(1)} %get-tuple-element.30), channel_id=1, source_target_pairs={{0,3},{1,2},{2,1},{3,0},{4,7},{5,6},{6,5},{7,4},{8,11},{9,10},{10,... | collective-permute-start | bytes 196616 | tf_op jit(solution)/shard_map/ppermute | solution.py:182
  13.6 0.9 %collective-permute-start.5 = (bf16[128,256]{1,0:T(8,128)(2,1)S(1)}, bf16[128,256]{1,0:T(8,128)(2,1)S(1)}, u32[]{:S(2)}, u32[]{:S(2)}) collective-permute-start(bf16[128,256]{1,0:T(8,128)(2,1)S(1)} %get-tuple-element.32), channel_id=1, source_target_pairs={{0,1},{1,0},{2,3},{3,2},{4,5},{5,4},{6,7},{7,6},{8,9},{9,8},{10,11... | collective-permute-start | bytes 196616 | tf_op jit(solution)/shard_map/ppermute | solution.py:182
  14.5 3.5 %collective-permute-start.11 = (bf16[272,128]{1,0:T(8,128)(2,1)S(1)}, bf16[272,128]{1,0:T(8,128)(2,1)S(1)}, u32[]{:S(2)}, u32[]{:S(2)}) collective-permute-start(bf16[272,128]{1,0:T(8,128)(2,1)S(1)} %shard_map.98.rest_4_), channel_id=1, source_target_pairs={{0,3},{1,2},{2,1},{3,0},{4,7},{5,6},{6,5},{7,4},{8,11},{9,10},{10,... | collective-permute-start | bytes 208904 | tf_op jit(solution)/shard_map/ppermute | solution.py:199
  18.0 2.4 %collective-permute-done.4.rest_1_ = bf16[128,256]{1,0:T(8,128)(2,1)S(1)} collective-permute-done((bf16[128,256]{1,0:T(8,128)(2,1)S(1)}, bf16[128,256]{1,0:T(8,128)(2,1)S(1)}, u32[]{:S(2)}, u32[]{:S(2)}) %collective-permute-start.4) | collective-permute-done | bytes 65568 | tf_op jit(solution)/shard_map/ppermute | solution.py:182
  20.4 0.1 shard_map.99.rest_0_
  20.5 3.0 %collective-permute-start.9 = (bf16[128,256]{1,0:T(8,128)(2,1)S(1)}, bf16[128,256]{1,0:T(8,128)(2,1)S(1)}, u32[]{:S(2)}, u32[]{:S(2)}) collective-permute-start(bf16[128,256]{1,0:T(8,128)(2,1)S(1)} %shard_map.99.rest_0_), channel_id=1, source_target_pairs={{0,3},{1,2},{2,1},{3,0},{4,7},{5,6},{6,5},{7,4},{8,11},{9,10},{10,... | collective-permute-start | bytes 196616 | tf_op jit(solution)/shard_map/ppermute | solution.py:182
  23.5 1.4 %collective-permute-start.7 = (bf16[128,256]{1,0:T(8,128)(2,1)S(1)}, bf16[128,256]{1,0:T(8,128)(2,1)S(1)}, u32[]{:S(2)}, u32[]{:S(2)}) collective-permute-start(bf16[128,256]{1,0:T(8,128)(2,1)S(1)} %shard_map.99.rest_0_), channel_id=1, source_target_pairs={{0,1},{1,0},{2,3},{3,2},{4,5},{5,4},{6,7},{7,6},{8,9},{9,8},{10,11... | collective-permute-start | bytes 196616 | tf_op jit(solution)/shard_map/ppermute | solution.py:182
  25.0 0.7 %shard_map.97.matrix_ref = bf16[512,512]{1,0:T(8,128)(2,1)S(1)} custom-call(s32[1,1,2,8]{3,2,1,0:T(2,128)S(1)} %copy-done.5, s32[1,1]{1,0:T(1,128)S(6)} %copy.10.cnt_ref, bf16[1,1,8,128,128]{4,3,2,1,0:T(8,128)(2,1)S(1)} %copy-done, bf16[128,256]{1,0:T(8,128)(2,1)S(1)} %get-tuple-element.37.rest_0_.rest_3_), custom_call_target="tpu_custom_call" | custom-call | tf_op jit(solution)/shard_map/pallas_call | solution.py:213
  25.7 1.7 %collective-permute-done.9.rest_3_ = bf16[128,256]{1,0:T(8,128)(2,1)S(1)} collective-permute-done((bf16[128,256]{1,0:T(8,128)(2,1)S(1)}, bf16[128,256]{1,0:T(8,128)(2,1)S(1)}, u32[]{:S(2)}, u32[]{:S(2)}) %collective-permute-start.9) | collective-permute-done | bytes 65568 | tf_op jit(solution)/shard_map/ppermute | solution.py:182
  27.4 1.7 %collective-permute-done.8.rest_2_ = bf16[128,256]{1,0:T(8,128)(2,1)S(1)} collective-permute-done((bf16[128,256]{1,0:T(8,128)(2,1)S(1)}, bf16[128,256]{1,0:T(8,128)(2,1)S(1)}, u32[]{:S(2)}, u32[]{:S(2)}) %collective-permute-start.8) | collective-permute-done | bytes 65568 | tf_op jit(solution)/shard_map/ppermute | solution.py:182
  29.2 0.8 %shard_map.100 = (bf16[128,256]{1,0:T(8,128)(2,1)S(1)}, f32[256,256]{1,0:T(8,128)S(1)}, f32[128,256]{1,0:T(8,128)S(1)}, bf16[384,256]{1,0:T(8,128)(2,1)S(1)}) custom-call(bf16[256,256]{1,0:T(8,128)(2,1)S(1)} %copy-done.1, bf16[512,512]{1,0:T(8,128)(2,1)S(1)} %shard_map.97.matrix_ref, bf16[128,256]{1,0:T(8,128)(2,1)S(1)} %shard_map.99.rest_0_, ...), custom_call_target="tpu_custom_call" | custom-call | tf_op jit(solution)/shard_map/pallas_call | solution.py:230
  30.0 1.4 %collective-permute-done.12.got_ref = bf16[384,256]{1,0:T(8,128)(2,1)S(1)} collective-permute-done((bf16[384,256]{1,0:T(8,128)(2,1)S(1)}, bf16[384,256]{1,0:T(8,128)(2,1)S(1)}, u32[]{:S(2)}, u32[]{:S(2)}) %collective-permute-start.12) | collective-permute-done | bytes 196640 | tf_op jit(solution)/shard_map/ppermute | solution.py:243
  31.5 1.7 %collective-permute-start.13 = (bf16[256,256]{1,0:T(8,128)(2,1)S(1)}, bf16[256,256]{1,0:T(8,128)(2,1)S(1)}, u32[]{:S(2)}, u32[]{:S(2)}) collective-permute-start(bf16[256,256]{1,0:T(8,128)(2,1)S(1)} %get-tuple-element.44), channel_id=1, source_target_pairs={{0,8},{4,12},{8,0},{12,4},{1,9},{5,13},{9,1},{13,5},{2,10},{6,14},... | collective-permute-start | bytes 393224 | tf_op jit(solution)/shard_map/ppermute | solution.py:243
  33.2 3.9 %collective-permute-done.13.got_ref = bf16[256,256]{1,0:T(8,128)(2,1)S(1)} collective-permute-done((bf16[256,256]{1,0:T(8,128)(2,1)S(1)}, bf16[256,256]{1,0:T(8,128)(2,1)S(1)}, u32[]{:S(2)}, u32[]{:S(2)}) %collective-permute-start.13) | collective-permute-done | bytes 131104 | tf_op jit(solution)/shard_map/ppermute | solution.py:243
  37.2 0.8 %shard_map.102 = (bf16[128,256]{1,0:T(8,128)(2,1)}, bf16[128,256]{1,0:T(8,128)(2,1)}) custom-call(s32[128]{0:T(128)S(1)} %copy-done.4, bf16[256,256]{1,0:T(8,128)(2,1)S(1)} %copy-done.1, f32[128,256]{1,0:T(8,128)S(1)} %get-tuple-element.43.keep_ref, bf16[256,256]{1,0:T(8,128)(2,1)S(1)} %collective-permute-done.13.got_ref, ...), custom_call_target="tpu_custom_call" | custom-call | tf_op jit(solution)/shard_map/pallas_call | solution.py:267
  38.0 0.5 %collective-permute-done.14.got_ref = f32[128,256]{1,0:T(8,128)S(1)} collective-permute-done((f32[128,256]{1,0:T(8,128)S(1)}, f32[128,256]{1,0:T(8,128)S(1)}, u32[]{:S(2)}, u32[]{:S(2)}) %collective-permute-start.14) | collective-permute-done | bytes 131104 | tf_op jit(solution)/shard_map/ppermute | solution.py:243
  38.5 0.7 %shard_map.104 = f32[256,256]{1,0:T(8,128)} custom-call(f32[128,256]{1,0:T(8,128)S(1)} %shard_map.103.own_ref, f32[128,256]{1,0:T(8,128)S(1)} %collective-permute-done.14.got_ref), custom_call_target="tpu_custom_call" | custom-call | tf_op jit(solution)/shard_map/pallas_call | solution.py:264
  (31 shorter events, 0.4 us)
Async XLA Ops:
  0.6 4.8 %copy-start.2 = (bf16[128,256]{1,0:T(8,128)(2,1)S(1)}, bf16[128,256]{1,0:T(8,128)(2,1)}, u32[]{:S(2)}) copy-start(bf16[128,256]{1,0:T(8,128)(2,1)} %cot_ref.1) | copy-start | bytes 196612
  0.6 0.7 %copy-start.3 = (s32[128]{0:T(128)S(1)}, s32[128]{0:T(128)}, u32[]{:S(2)}) copy-start(s32[128]{0:T(128)} %deg_ref.7) | copy-start | bytes 1540
  1.3 0.8 %copy-start.6 = (bf16[128,256]{1,0:T(8,128)(2,1)S(1)}, bf16[128,256]{1,0:T(8,128)(2,1)}, u32[]{:S(2)}) copy-start(bf16[128,256]{1,0:T(8,128)(2,1)} %x_ref.1) | copy-start | bytes 196612
  2.2 6.8 %copy-start = (bf16[1,1,8,128,128]{4,3,2,1,0:T(8,128)(2,1)S(1)}, bf16[1,1,8,128,128]{4,3,2,1,0:T(8,128)(2,1)}, u32[]{:S(2)}) copy-start(bf16[1,1,8,128,128]{4,3,2,1,0:T(8,128)(2,1)} %values_ref.3) | copy-start | bytes 786436
  2.3 7.4 %collective-permute-start.2 = (bf16[128,256]{1,0:T(8,128)(2,1)S(1)}, bf16[128,256]{1,0:T(8,128)(2,1)S(1)}, u32[]{:S(2)}, u32[]{:S(2)}) collective-permute-start(bf16[128,256]{1,0:T(8,128)(2,1)S(1)} %shard_map.95.rest_0_), channel_id=1, source_target_pairs={{0,12},{4,8},{8,4},{12,0},{1,13},{5,9},{9,5},{13,1},{2,14},{6,10},... | collective-permute-start | bytes 196616 | tf_op jit(solution)/shard_map/ppermute | solution.py:182
  4.7 5.0 %collective-permute-start.1 = (bf16[128,256]{1,0:T(8,128)(2,1)S(1)}, bf16[128,256]{1,0:T(8,128)(2,1)S(1)}, u32[]{:S(2)}, u32[]{:S(2)}) collective-permute-start(bf16[128,256]{1,0:T(8,128)(2,1)S(1)} %shard_map.95.rest_0_), channel_id=1, source_target_pairs={{0,8},{4,12},{8,0},{12,4},{1,9},{5,13},{9,1},{13,5},{2,10},{6,14},... | collective-permute-start | bytes 196616 | tf_op jit(solution)/shard_map/ppermute | solution.py:182
  5.4 4.4 %collective-permute-start = (bf16[128,256]{1,0:T(8,128)(2,1)S(1)}, bf16[128,256]{1,0:T(8,128)(2,1)S(1)}, u32[]{:S(2)}, u32[]{:S(2)}) collective-permute-start(bf16[128,256]{1,0:T(8,128)(2,1)S(1)} %shard_map.95.rest_0_), channel_id=1, source_target_pairs={{0,4},{4,0},{8,12},{12,8},{1,5},{5,1},{9,13},{13,9},{2,6},{6,2},{1... | collective-permute-start | bytes 196616 | tf_op jit(solution)/shard_map/ppermute | solution.py:182
  5.4 3.6 %copy-start.5 = (s32[1,1,2,8]{3,2,1,0:T(2,128)S(1)}, s32[1,1,2,8]{3,2,1,0:T(2,128)}, u32[]{:S(2)}) copy-start(s32[1,1,2,8]{3,2,1,0:T(2,128)} %idx_ref.3) | copy-start | bytes 196
  5.4 12.5 %collective-permute-start.6 = (bf16[272,128]{1,0:T(8,128)(2,1)S(1)}, bf16[272,128]{1,0:T(8,128)(2,1)S(1)}, u32[]{:S(2)}, u32[]{:S(2)}) collective-permute-start(bf16[272,128]{1,0:T(8,128)(2,1)S(1)} %shard_map.98.rest_4_), channel_id=1, source_target_pairs={{0,2},{1,3},{2,0},{3,1},{4,6},{5,7},{6,4},{7,5},{8,10},{9,11},{10,... | collective-permute-start | bytes 208904 | tf_op jit(solution)/shard_map/ppermute | solution.py:199
  10.1 10.3 %copy-start.4 = (s32[128]{0:T(128)S(1)}, s32[128]{0:T(128)}, u32[]{:S(2)}) copy-start(s32[128]{0:T(128)} %deg_ref.7) | copy-start | bytes 1540
  10.1 7.9 %collective-permute-start.3 = (bf16[128,256]{1,0:T(8,128)(2,1)S(1)}, bf16[128,256]{1,0:T(8,128)(2,1)S(1)}, u32[]{:S(2)}, u32[]{:S(2)}) collective-permute-start(bf16[128,256]{1,0:T(8,128)(2,1)S(1)} %get-tuple-element.30), channel_id=1, source_target_pairs={{0,3},{1,2},{2,1},{3,0},{4,7},{5,6},{6,5},{7,4},{8,11},{9,10},{10,... | collective-permute-start | bytes 196616 | tf_op jit(solution)/shard_map/ppermute | solution.py:182
  13.6 6.8 %collective-permute-start.4 = (bf16[128,256]{1,0:T(8,128)(2,1)S(1)}, bf16[128,256]{1,0:T(8,128)(2,1)S(1)}, u32[]{:S(2)}, u32[]{:S(2)}) collective-permute-start(bf16[128,256]{1,0:T(8,128)(2,1)S(1)} %get-tuple-element.31), channel_id=1, source_target_pairs={{0,2},{1,3},{2,0},{3,1},{4,6},{5,7},{6,4},{7,5},{8,10},{9,11},{10,... | collective-permute-start | bytes 196616 | tf_op jit(solution)/shard_map/ppermute | solution.py:182
  13.6 6.8 %collective-permute-start.5 = (bf16[128,256]{1,0:T(8,128)(2,1)S(1)}, bf16[128,256]{1,0:T(8,128)(2,1)S(1)}, u32[]{:S(2)}, u32[]{:S(2)}) collective-permute-start(bf16[128,256]{1,0:T(8,128)(2,1)S(1)} %get-tuple-element.32), channel_id=1, source_target_pairs={{0,1},{1,0},{2,3},{3,2},{4,5},{5,4},{6,7},{7,6},{8,9},{9,8},{10,11... | collective-permute-start | bytes 196616 | tf_op jit(solution)/shard_map/ppermute | solution.py:182
  14.5 11.2 %collective-permute-start.11 = (bf16[272,128]{1,0:T(8,128)(2,1)S(1)}, bf16[272,128]{1,0:T(8,128)(2,1)S(1)}, u32[]{:S(2)}, u32[]{:S(2)}) collective-permute-start(bf16[272,128]{1,0:T(8,128)(2,1)S(1)} %shard_map.98.rest_4_), channel_id=1, source_target_pairs={{0,3},{1,2},{2,1},{3,0},{4,7},{5,6},{6,5},{7,4},{8,11},{9,10},{10,... | collective-permute-start | bytes 208904 | tf_op jit(solution)/shard_map/ppermute | solution.py:199
  18.0 7.7 %collective-permute-start.10 = (bf16[272,128]{1,0:T(8,128)(2,1)S(1)}, bf16[272,128]{1,0:T(8,128)(2,1)S(1)}, u32[]{:S(2)}, u32[]{:S(2)}) collective-permute-start(bf16[272,128]{1,0:T(8,128)(2,1)S(1)} %shard_map.98.rest_4_), channel_id=1, source_target_pairs={{0,1},{1,0},{2,3},{3,2},{4,5},{5,4},{6,7},{7,6},{8,9},{9,8},{10,11... | collective-permute-start | bytes 208904 | tf_op jit(solution)/shard_map/ppermute | solution.py:199
  20.5 8.6 %copy-start.1 = (bf16[256,256]{1,0:T(8,128)(2,1)S(1)}, bf16[256,256]{1,0:T(8,128)(2,1)}, u32[]{:S(2)}) copy-start(bf16[256,256]{1,0:T(8,128)(2,1)} %weight_ref.3) | copy-start | bytes 393220
  20.5 6.9 %collective-permute-start.9 = (bf16[128,256]{1,0:T(8,128)(2,1)S(1)}, bf16[128,256]{1,0:T(8,128)(2,1)S(1)}, u32[]{:S(2)}, u32[]{:S(2)}) collective-permute-start(bf16[128,256]{1,0:T(8,128)(2,1)S(1)} %shard_map.99.rest_0_), channel_id=1, source_target_pairs={{0,3},{1,2},{2,1},{3,0},{4,7},{5,6},{6,5},{7,4},{8,11},{9,10},{10,... | collective-permute-start | bytes 196616 | tf_op jit(solution)/shard_map/ppermute | solution.py:182
  23.5 5.6 %collective-permute-start.8 = (bf16[128,256]{1,0:T(8,128)(2,1)S(1)}, bf16[128,256]{1,0:T(8,128)(2,1)S(1)}, u32[]{:S(2)}, u32[]{:S(2)}) collective-permute-start(bf16[128,256]{1,0:T(8,128)(2,1)S(1)} %shard_map.99.rest_0_), channel_id=1, source_target_pairs={{0,2},{1,3},{2,0},{3,1},{4,6},{5,7},{6,4},{7,5},{8,10},{9,11},{10,... | collective-permute-start | bytes 196616 | tf_op jit(solution)/shard_map/ppermute | solution.py:182
  23.5 5.6 %collective-permute-start.7 = (bf16[128,256]{1,0:T(8,128)(2,1)S(1)}, bf16[128,256]{1,0:T(8,128)(2,1)S(1)}, u32[]{:S(2)}, u32[]{:S(2)}) collective-permute-start(bf16[128,256]{1,0:T(8,128)(2,1)S(1)} %shard_map.99.rest_0_), channel_id=1, source_target_pairs={{0,1},{1,0},{2,3},{3,2},{4,5},{5,4},{6,7},{7,6},{8,9},{9,8},{10,11... | collective-permute-start | bytes 196616 | tf_op jit(solution)/shard_map/ppermute | solution.py:182
  29.9 1.5 %collective-permute-start.12 = (bf16[384,256]{1,0:T(8,128)(2,1)S(1)}, bf16[384,256]{1,0:T(8,128)(2,1)S(1)}, u32[]{:S(2)}, u32[]{:S(2)}) collective-permute-start(bf16[384,256]{1,0:T(8,128)(2,1)S(1)} %get-tuple-element.42), channel_id=1, source_target_pairs={{0,4},{4,0},{8,12},{12,8},{1,5},{5,1},{9,13},{13,9},{2,6},{6,2},{1... | collective-permute-start | bytes 589832 | tf_op jit(solution)/shard_map/ppermute | solution.py:243
  31.5 5.6 %collective-permute-start.13 = (bf16[256,256]{1,0:T(8,128)(2,1)S(1)}, bf16[256,256]{1,0:T(8,128)(2,1)S(1)}, u32[]{:S(2)}, u32[]{:S(2)}) collective-permute-start(bf16[256,256]{1,0:T(8,128)(2,1)S(1)} %get-tuple-element.44), channel_id=1, source_target_pairs={{0,8},{4,12},{8,0},{12,4},{1,9},{5,13},{9,1},{13,5},{2,10},{6,14},... | collective-permute-start | bytes 393224 | tf_op jit(solution)/shard_map/ppermute | solution.py:243
  37.1 1.4 %collective-permute-start.14 = (f32[128,256]{1,0:T(8,128)S(1)}, f32[128,256]{1,0:T(8,128)S(1)}, u32[]{:S(2)}, u32[]{:S(2)}) collective-permute-start(f32[128,256]{1,0:T(8,128)S(1)} %shard_map.103.own_ref), channel_id=1, source_target_pairs={{0,4},{4,0},{8,12},{12,8},{1,5},{5,1},{9,13},{13,9},{2,6},{6,2},{1... | collective-permute-start | bytes 393224 | tf_op jit(solution)/shard_map/ppermute | solution.py:243

commit v5 on v4

--- a/solution.py
+++ b/solution.py
@@ -125,29 +125,23 @@
     send_ref[half_rows:] = term[rows_at(1 - side, half), :].astype(BF16)
 
 
-def fold_kernel(keep_ref, term_ref, got_ref, keep_out, term_out, send_out):
+def fold_kernel(keep_ref, term_ref, got_ref, term_got_ref, keep_out, term_out, send_out):
     rows = keep_ref.shape[0]
     half = rows // 2
+    term_got = term_got_ref[term_got_ref.shape[0] - term_ref.shape[0] :]
     keep_out[...] = keep_ref[:half] + got_ref[:half].astype(F32)
-    term = (term_ref[...].astype(F32) + got_ref[rows:].astype(F32)).astype(BF16)
-    send_out[:half] = (keep_ref[half:] + got_ref[half:rows].astype(F32)).astype(BF16)
-    send_out[half:] = term
-    term_out[...] = term
+    term_out[...] = (term_ref[...].astype(F32) + term_got.astype(F32)).astype(BF16)
+    send_out[...] = (keep_ref[half:] + got_ref[half:rows].astype(F32)).astype(BF16)
 
 
 def add_kernel(scale, own_ref, got_ref, out_ref):
     got = got_ref[got_ref.shape[0] - own_ref.shape[0] :]
-    out_ref[...] = (own_ref[...].astype(F32) + got.astype(F32)) * scale
-
-
-def join_kernel(own_ref, got_ref, out_ref):
-    half = own_ref.shape[0]
-    side = lax.rem(lax.axis_index("rows"), 2)
-    out_ref[rows_at(side, half), :] = own_ref[...]
-    out_ref[rows_at(1 - side, half), :] = got_ref[...]
-
-
-def last_kernel(deg_ref, weight_ref, keep_ref, got_ref, held_ref, grad_ref, act_ref):
+    out_ref[...] = ((own_ref[...].astype(F32) + got.astype(F32)) * scale).astype(out_ref.dtype)
+
+
+def last_kernel(
+    deg_ref, weight_ref, keep_ref, got_ref, held_ref, own_ref, other_ref, grad_ref, act_ref, wgrad_ref
+):
     act_ref[...] = held_ref[...]
     hidden = (keep_ref[...] + got_ref[: keep_ref.shape[0]].astype(F32)).astype(BF16)
     back = lax.dot_general(
@@ -155,6 +149,10 @@
     )
     scale = wide(row_scale(deg_ref[...].reshape(1, TILE)), back.shape[1])
     grad_ref[...] = (scale * back).astype(BF16)
+    half = own_ref.shape[0]
+    side = lax.rem(lax.axis_index("rows"), 2)
+    wgrad_ref[rows_at(side, half), :] = own_ref[...].astype(F32)
+    wgrad_ref[rows_at(1 - side, half), :] = other_ref[...].astype(F32)
 
 
 def call(body, out_shapes, places, scratch=(), cost=None):
@@ -242,7 +240,7 @@
     def partner(block, mask):
         return lax.ppermute(block, "rows", [(i, i ^ mask) for i in range(n_rows)])
 
-    got = partner(send, 1)
+    got = term_got = partner(send, 1)
     mask = 2
     while mask < n_rows:
         half = keep.shape[0] // 2
@@ -251,22 +249,22 @@
             (
                 shape((half, width), F32),
                 shape((side_rows, width), BF16),
-                shape((half + side_rows, width), BF16),
+                shape((half, width), BF16),
             ),
-            [vmem] * 3,
-        )(keep, term, got)
-        got = partner(send, mask)
+            [vmem] * 4,
+        )(keep, term, got, term_got)
+        term_got, got = partner(term, mask), partner(send, mask)
         mask *= 2
     node_scale = 1.0 / math.sqrt(TILE * n_rows * n_cols)
     term = call(
-        functools.partial(add_kernel, node_scale), shape((side_rows, width), F32), [vmem] * 2
-    )(term, got)
-    weight_grad = call(join_kernel, shape((width, width), F32), [vmem] * 2)(
-        term, partner(term, 1)
-    )
-    input_grad, activated = call(last_kernel, (block_shape, block_shape), [vmem] * 5)(
-        degree, weight, keep, got, kept_act
-    )
+        functools.partial(add_kernel, node_scale),
+        shape((side_rows, width), BF16),
+        [vmem] * 2,
+        cost=slow,
+    )(term, term_got)
+    input_grad, activated, weight_grad = call(
+        last_kernel, (block_shape, block_shape, shape((width, width), F32)), [vmem] * 7
+    )(degree, weight, keep, got, kept_act, term, partner(term, 1))
     return (activated, input_grad, weight_grad)
 
 

time: 39.4 us -> 38.5 us (0.977)
  Pallas kernels: 4.33 us -> 3.6 us
  waiting for transfers between devices: 11.7 us -> 11 us
  starting transfers between devices: 20.2 us -> 20.6 us
    pallas_call x2 -> x1, Pallas kernels: 1.57 us -> 0.85 us  [shards(): call(last_kernel, (block_shape, block_shape, shape((width, width), F32)),...]
    ppermute x3 -> x4, waiting for transfers between devices: 5.83 us -> 5.2 us  [partner(): return lax.ppermute(block, 'rows', [(i, i ^ mask) for i in range(n_rows)])]
    ppermute x3 -> x4, starting transfers between devices: 1.84 us -> 2.23 us  [partner(): return lax.ppermute(block, 'rows', [(i, i ^ mask) for i in range(n_rows)])]
  transfers between devices with their start and end apart: 15 -> 16, of which waited for: 6 -> 6; matrix products, arithmetic and copies ran while one was open for 0% -> 0% of each run, Pallas kernels for 7% -> 5%
where the time goes in v5:
time: 38.5 us; the launch traced here: 38.3 us
  starting transfers between devices  20.6 us (54%)
  waiting for transfers between devices  11 us (29%)
  Pallas kernels  3.6 us (9%)
  local copies, waits for them, and re-layouts  1.55 us (4%)
  between operations  1.46 us (4%)
    ppermute x9, starting transfers between devices, shifted(): lax.ppermute(source, axis, [(i, i ^ shift) for i in range(size)])  12 us
    ppermute x3, starting transfers between devices, sent(): return lax.ppermute(block, 'cols', [(j, j ^ shift) for j in range(n_cols)])  6.36 us
    ppermute x9, waiting for transfers between devices, shifted(): lax.ppermute(source, axis, [(i, i ^ shift) for i in range(size)])  5.83 us
    ppermute x4, waiting for transfers between devices, partner(): return lax.ppermute(block, 'rows', [(i, i ^ mask) for i in range(n_rows)])  5.2 us
    ppermute x4, starting transfers between devices, partner(): return lax.ppermute(block, 'rows', [(i, i ^ mask) for i in range(n_rows)])  2.23 us
    unnamed x14, local copies, waits for them, and re-layouts  1.55 us
    pallas_call x1, Pallas kernels, shards(): call(last_kernel, (block_shape, block_shape, shape((width, width), F32)),...  0.85 us
  transfers between devices with their start and end apart: 16, of which 6 were waited for; matrix products, arithmetic and copies ran while one was open for 0% of the time, Pallas kernels for 5%

profile of v5, /device:TPU:0, one launch (start us, length us, event | category | flops | bytes accessed | tf_op | source)
XLA Modules:
  0.0 38.3 jit_solution(4111881975826679739)
XLA Ops:
  0.7 0.7 %copy-done.3 = s32[128]{0:T(128)S(1)} copy-done((s32[128]{0:T(128)S(1)}, s32[128]{0:T(128)}, u32[]{:S(2)}) %copy-start.3) | copy-done | bytes 536
  1.3 0.8 %copy-done.6 = bf16[128,256]{1,0:T(8,128)(2,1)S(1)} copy-done((bf16[128,256]{1,0:T(8,128)(2,1)S(1)}, bf16[128,256]{1,0:T(8,128)(2,1)}, u32[]{:S(2)}) %copy-start.6) | copy-done | bytes 65560
  2.3 2.4 %collective-permute-start.2 = (bf16[128,256]{1,0:T(8,128)(2,1)S(1)}, bf16[128,256]{1,0:T(8,128)(2,1)S(1)}, u32[]{:S(2)}, u32[]{:S(2)}) collective-permute-start(bf16[128,256]{1,0:T(8,128)(2,1)S(1)} %shard_map.95.rest_0_), channel_id=1, source_target_pairs={{0,12},{4,8},{8,4},{12,0},{1,13},{5,9},{9,5},{13,1},{2,14},{6,10},... | collective-permute-start | bytes 196616 | tf_op jit(solution)/shard_map/ppermute | solution.py:180
  4.7 0.6 %collective-permute-start.1 = (bf16[128,256]{1,0:T(8,128)(2,1)S(1)}, bf16[128,256]{1,0:T(8,128)(2,1)S(1)}, u32[]{:S(2)}, u32[]{:S(2)}) collective-permute-start(bf16[128,256]{1,0:T(8,128)(2,1)S(1)} %shard_map.95.rest_0_), channel_id=1, source_target_pairs={{0,8},{4,12},{8,0},{12,4},{1,9},{5,13},{9,1},{13,5},{2,10},{6,14},... | collective-permute-start | bytes 196616 | tf_op jit(solution)/shard_map/ppermute | solution.py:180
  5.4 2.9 %collective-permute-start.6 = (bf16[272,128]{1,0:T(8,128)(2,1)S(1)}, bf16[272,128]{1,0:T(8,128)(2,1)S(1)}, u32[]{:S(2)}, u32[]{:S(2)}) collective-permute-start(bf16[272,128]{1,0:T(8,128)(2,1)S(1)} %shard_map.98.rest_4_), channel_id=1, source_target_pairs={{0,2},{1,3},{2,0},{3,1},{4,6},{5,7},{6,4},{7,5},{8,10},{9,11},{10,... | collective-permute-start | bytes 208904 | tf_op jit(solution)/shard_map/ppermute | solution.py:197
  9.0 0.7 %shard_map.94.matrix_ref = bf16[512,512]{1,0:T(8,128)(2,1)S(1)} custom-call(s32[1,1,2,8]{3,2,1,0:T(2,128)S(1)} %copy-done.5, s32[1,1]{1,0:T(1,128)S(6)} %copy.10.cnt_ref, bf16[1,1,8,128,128]{4,3,2,1,0:T(8,128)(2,1)S(1)} %copy-done), custom_call_target="tpu_custom_call" | custom-call | tf_op jit(solution)/shard_map/pallas_call | solution.py:190
  9.7 0.3 shard_map.96
  10.1 3.5 %collective-permute-start.3 = (bf16[128,256]{1,0:T(8,128)(2,1)S(1)}, bf16[128,256]{1,0:T(8,128)(2,1)S(1)}, u32[]{:S(2)}, u32[]{:S(2)}) collective-permute-start(bf16[128,256]{1,0:T(8,128)(2,1)S(1)} %get-tuple-element.31), channel_id=1, source_target_pairs={{0,3},{1,2},{2,1},{3,0},{4,7},{5,6},{6,5},{7,4},{8,11},{9,10},{10,... | collective-permute-start | bytes 196616 | tf_op jit(solution)/shard_map/ppermute | solution.py:180
  13.6 0.9 %collective-permute-start.5 = (bf16[128,256]{1,0:T(8,128)(2,1)S(1)}, bf16[128,256]{1,0:T(8,128)(2,1)S(1)}, u32[]{:S(2)}, u32[]{:S(2)}) collective-permute-start(bf16[128,256]{1,0:T(8,128)(2,1)S(1)} %get-tuple-element.33), channel_id=1, source_target_pairs={{0,1},{1,0},{2,3},{3,2},{4,5},{5,4},{6,7},{7,6},{8,9},{9,8},{10,11... | collective-permute-start | bytes 196616 | tf_op jit(solution)/shard_map/ppermute | solution.py:180
  14.5 3.5 %collective-permute-start.11 = (bf16[272,128]{1,0:T(8,128)(2,1)S(1)}, bf16[272,128]{1,0:T(8,128)(2,1)S(1)}, u32[]{:S(2)}, u32[]{:S(2)}) collective-permute-start(bf16[272,128]{1,0:T(8,128)(2,1)S(1)} %shard_map.98.rest_4_), channel_id=1, source_target_pairs={{0,3},{1,2},{2,1},{3,0},{4,7},{5,6},{6,5},{7,4},{8,11},{9,10},{10,... | collective-permute-start | bytes 208904 | tf_op jit(solution)/shard_map/ppermute | solution.py:197
  18.0 2.4 %collective-permute-done.4.rest_1_ = bf16[128,256]{1,0:T(8,128)(2,1)S(1)} collective-permute-done((bf16[128,256]{1,0:T(8,128)(2,1)S(1)}, bf16[128,256]{1,0:T(8,128)(2,1)S(1)}, u32[]{:S(2)}, u32[]{:S(2)}) %collective-permute-start.4) | collective-permute-done | bytes 65568 | tf_op jit(solution)/shard_map/ppermute | solution.py:180
  20.4 0.1 shard_map.99.rest_0_
  20.5 3.0 %collective-permute-start.9 = (bf16[128,256]{1,0:T(8,128)(2,1)S(1)}, bf16[128,256]{1,0:T(8,128)(2,1)S(1)}, u32[]{:S(2)}, u32[]{:S(2)}) collective-permute-start(bf16[128,256]{1,0:T(8,128)(2,1)S(1)} %shard_map.99.rest_0_), channel_id=1, source_target_pairs={{0,3},{1,2},{2,1},{3,0},{4,7},{5,6},{6,5},{7,4},{8,11},{9,10},{10,... | collective-permute-start | bytes 196616 | tf_op jit(solution)/shard_map/ppermute | solution.py:180
  23.5 1.4 %collective-permute-start.7 = (bf16[128,256]{1,0:T(8,128)(2,1)S(1)}, bf16[128,256]{1,0:T(8,128)(2,1)S(1)}, u32[]{:S(2)}, u32[]{:S(2)}) collective-permute-start(bf16[128,256]{1,0:T(8,128)(2,1)S(1)} %shard_map.99.rest_0_), channel_id=1, source_target_pairs={{0,1},{1,0},{2,3},{3,2},{4,5},{5,4},{6,7},{7,6},{8,9},{9,8},{10,11... | collective-permute-start | bytes 196616 | tf_op jit(solution)/shard_map/ppermute | solution.py:180
  25.0 0.7 %shard_map.97.matrix_ref = bf16[512,512]{1,0:T(8,128)(2,1)S(1)} custom-call(s32[1,1,2,8]{3,2,1,0:T(2,128)S(1)} %copy-done.5, s32[1,1]{1,0:T(1,128)S(6)} %copy.10.cnt_ref, bf16[1,1,8,128,128]{4,3,2,1,0:T(8,128)(2,1)S(1)} %copy-done, bf16[128,256]{1,0:T(8,128)(2,1)S(1)} %get-tuple-element.38.rest_0_.rest_3_), custom_call_target="tpu_custom_call" | custom-call | tf_op jit(solution)/shard_map/pallas_call | solution.py:211
  25.7 1.7 %collective-permute-done.9.rest_3_ = bf16[128,256]{1,0:T(8,128)(2,1)S(1)} collective-permute-done((bf16[128,256]{1,0:T(8,128)(2,1)S(1)}, bf16[128,256]{1,0:T(8,128)(2,1)S(1)}, u32[]{:S(2)}, u32[]{:S(2)}) %collective-permute-start.9) | collective-permute-done | bytes 65568 | tf_op jit(solution)/shard_map/ppermute | solution.py:180
  27.4 1.7 %collective-permute-done.8.rest_2_ = bf16[128,256]{1,0:T(8,128)(2,1)S(1)} collective-permute-done((bf16[128,256]{1,0:T(8,128)(2,1)S(1)}, bf16[128,256]{1,0:T(8,128)(2,1)S(1)}, u32[]{:S(2)}, u32[]{:S(2)}) %collective-permute-start.8) | collective-permute-done | bytes 65568 | tf_op jit(solution)/shard_map/ppermute | solution.py:180
  29.1 0.7 %shard_map.100 = (bf16[128,256]{1,0:T(8,128)(2,1)S(1)}, f32[256,256]{1,0:T(8,128)S(1)}, f32[128,256]{1,0:T(8,128)S(1)}, bf16[384,256]{1,0:T(8,128)(2,1)S(1)}) custom-call(bf16[256,256]{1,0:T(8,128)(2,1)S(1)} %copy-done.1, bf16[512,512]{1,0:T(8,128)(2,1)S(1)} %shard_map.97.matrix_ref, bf16[128,256]{1,0:T(8,128)(2,1)S(1)} %shard_map.99.rest_0_, ...), custom_call_target="tpu_custom_call" | custom-call | tf_op jit(solution)/shard_map/pallas_call | solution.py:228
  30.0 1.4 %collective-permute-done.12.got_ref.term_got_ref = bf16[384,256]{1,0:T(8,128)(2,1)S(1)} collective-permute-done((bf16[384,256]{1,0:T(8,128)(2,1)S(1)}, bf16[384,256]{1,0:T(8,128)(2,1)S(1)}, u32[]{:S(2)}, u32[]{:S(2)}) %collective-permute-start.12) | collective-permute-done | bytes 196640 | tf_op jit(solution)/shard_map/ppermute | solution.py:241
  31.4 1.7 %collective-permute-start.14 = (bf16[128,256]{1,0:T(8,128)(2,1)S(1)}, bf16[128,256]{1,0:T(8,128)(2,1)S(1)}, u32[]{:S(2)}, u32[]{:S(2)}) collective-permute-start(bf16[128,256]{1,0:T(8,128)(2,1)S(1)} %get-tuple-element.47.own_ref), channel_id=1, source_target_pairs={{0,8},{4,12},{8,0},{12,4},{1,9},{5,13},{9,1},{13,5},{2,10},{6,14},... | collective-permute-start | bytes 196616 | tf_op jit(solution)/shard_map/ppermute | solution.py:241
  33.1 0.4 %collective-permute-start.13 = (bf16[128,256]{1,0:T(8,128)(2,1)S(1)}, bf16[128,256]{1,0:T(8,128)(2,1)S(1)}, u32[]{:S(2)}, u32[]{:S(2)}) collective-permute-start(bf16[128,256]{1,0:T(8,128)(2,1)S(1)} %get-tuple-element.45), channel_id=1, source_target_pairs={{0,8},{4,12},{8,0},{12,4},{1,9},{5,13},{9,1},{13,5},{2,10},{6,14},... | collective-permute-start | bytes 196616 | tf_op jit(solution)/shard_map/ppermute | solution.py:241
  33.5 2.5 %collective-permute-done.14.got_ref = bf16[128,256]{1,0:T(8,128)(2,1)S(1)} collective-permute-done((bf16[128,256]{1,0:T(8,128)(2,1)S(1)}, bf16[128,256]{1,0:T(8,128)(2,1)S(1)}, u32[]{:S(2)}, u32[]{:S(2)}) %collective-permute-start.14) | collective-permute-done | bytes 65568 | tf_op jit(solution)/shard_map/ppermute | solution.py:241
  36.1 1.3 %collective-permute-done.13.got_ref = bf16[128,256]{1,0:T(8,128)(2,1)S(1)} collective-permute-done((bf16[128,256]{1,0:T(8,128)(2,1)S(1)}, bf16[128,256]{1,0:T(8,128)(2,1)S(1)}, u32[]{:S(2)}, u32[]{:S(2)}) %collective-permute-start.13) | collective-permute-done | bytes 65568 | tf_op jit(solution)/shard_map/ppermute | solution.py:241
  37.4 0.8 %shard_map.103 = (bf16[128,256]{1,0:T(8,128)(2,1)}, bf16[128,256]{1,0:T(8,128)(2,1)}, f32[256,256]{1,0:T(8,128)}) custom-call(s32[128]{0:T(128)S(1)} %copy-done.4, bf16[256,256]{1,0:T(8,128)(2,1)S(1)} %copy-done.1, f32[128,256]{1,0:T(8,128)S(1)} %get-tuple-element.44.keep_ref, bf16[128,256]{1,0:T(8,128)(2,1)S(1)} %collective-permute-done.13.got_ref, ...), custom_call_target="tpu_custom_call" | custom-call | tf_op jit(solution)/shard_map/pallas_call | solution.py:265
  (32 shorter events, 0.4 us)
Async XLA Ops:
  0.6 4.8 %copy-start.2 = (bf16[128,256]{1,0:T(8,128)(2,1)S(1)}, bf16[128,256]{1,0:T(8,128)(2,1)}, u32[]{:S(2)}) copy-start(bf16[128,256]{1,0:T(8,128)(2,1)} %cot_ref.1) | copy-start | bytes 196612
  0.6 0.7 %copy-start.3 = (s32[128]{0:T(128)S(1)}, s32[128]{0:T(128)}, u32[]{:S(2)}) copy-start(s32[128]{0:T(128)} %deg_ref.7) | copy-start | bytes 1540
  1.3 0.8 %copy-start.6 = (bf16[128,256]{1,0:T(8,128)(2,1)S(1)}, bf16[128,256]{1,0:T(8,128)(2,1)}, u32[]{:S(2)}) copy-start(bf16[128,256]{1,0:T(8,128)(2,1)} %x_ref.1) | copy-start | bytes 196612
  2.2 6.8 %copy-start = (bf16[1,1,8,128,128]{4,3,2,1,0:T(8,128)(2,1)S(1)}, bf16[1,1,8,128,128]{4,3,2,1,0:T(8,128)(2,1)}, u32[]{:S(2)}) copy-start(bf16[1,1,8,128,128]{4,3,2,1,0:T(8,128)(2,1)} %values_ref.3) | copy-start | bytes 786436
  2.3 7.4 %collective-permute-start.2 = (bf16[128,256]{1,0:T(8,128)(2,1)S(1)}, bf16[128,256]{1,0:T(8,128)(2,1)S(1)}, u32[]{:S(2)}, u32[]{:S(2)}) collective-permute-start(bf16[128,256]{1,0:T(8,128)(2,1)S(1)} %shard_map.95.rest_0_), channel_id=1, source_target_pairs={{0,12},{4,8},{8,4},{12,0},{1,13},{5,9},{9,5},{13,1},{2,14},{6,10},... | collective-permute-start | bytes 196616 | tf_op jit(solution)/shard_map/ppermute | solution.py:180
  4.7 5.0 %collective-permute-start.1 = (bf16[128,256]{1,0:T(8,128)(2,1)S(1)}, bf16[128,256]{1,0:T(8,128)(2,1)S(1)}, u32[]{:S(2)}, u32[]{:S(2)}) collective-permute-start(bf16[128,256]{1,0:T(8,128)(2,1)S(1)} %shard_map.95.rest_0_), channel_id=1, source_target_pairs={{0,8},{4,12},{8,0},{12,4},{1,9},{5,13},{9,1},{13,5},{2,10},{6,14},... | collective-permute-start | bytes 196616 | tf_op jit(solution)/shard_map/ppermute | solution.py:180
  5.4 4.4 %collective-permute-start = (bf16[128,256]{1,0:T(8,128)(2,1)S(1)}, bf16[128,256]{1,0:T(8,128)(2,1)S(1)}, u32[]{:S(2)}, u32[]{:S(2)}) collective-permute-start(bf16[128,256]{1,0:T(8,128)(2,1)S(1)} %shard_map.95.rest_0_), channel_id=1, source_target_pairs={{0,4},{4,0},{8,12},{12,8},{1,5},{5,1},{9,13},{13,9},{2,6},{6,2},{1... | collective-permute-start | bytes 196616 | tf_op jit(solution)/shard_map/ppermute | solution.py:180
  5.4 3.6 %copy-start.5 = (s32[1,1,2,8]{3,2,1,0:T(2,128)S(1)}, s32[1,1,2,8]{3,2,1,0:T(2,128)}, u32[]{:S(2)}) copy-start(s32[1,1,2,8]{3,2,1,0:T(2,128)} %idx_ref.3) | copy-start | bytes 196
  5.4 12.5 %collective-permute-start.6 = (bf16[272,128]{1,0:T(8,128)(2,1)S(1)}, bf16[272,128]{1,0:T(8,128)(2,1)S(1)}, u32[]{:S(2)}, u32[]{:S(2)}) collective-permute-start(bf16[272,128]{1,0:T(8,128)(2,1)S(1)} %shard_map.98.rest_4_), channel_id=1, source_target_pairs={{0,2},{1,3},{2,0},{3,1},{4,6},{5,7},{6,4},{7,5},{8,10},{9,11},{10,... | collective-permute-start | bytes 208904 | tf_op jit(solution)/shard_map/ppermute | solution.py:197
  10.1 10.3 %copy-start.4 = (s32[128]{0:T(128)S(1)}, s32[128]{0:T(128)}, u32[]{:S(2)}) copy-start(s32[128]{0:T(128)} %deg_ref.7) | copy-start | bytes 1540
  10.1 7.9 %collective-permute-start.3 = (bf16[128,256]{1,0:T(8,128)(2,1)S(1)}, bf16[128,256]{1,0:T(8,128)(2,1)S(1)}, u32[]{:S(2)}, u32[]{:S(2)}) collective-permute-start(bf16[128,256]{1,0:T(8,128)(2,1)S(1)} %get-tuple-element.31), channel_id=1, source_target_pairs={{0,3},{1,2},{2,1},{3,0},{4,7},{5,6},{6,5},{7,4},{8,11},{9,10},{10,... | collective-permute-start | bytes 196616 | tf_op jit(solution)/shard_map/ppermute | solution.py:180
  13.6 6.8 %collective-permute-start.4 = (bf16[128,256]{1,0:T(8,128)(2,1)S(1)}, bf16[128,256]{1,0:T(8,128)(2,1)S(1)}, u32[]{:S(2)}, u32[]{:S(2)}) collective-permute-start(bf16[128,256]{1,0:T(8,128)(2,1)S(1)} %get-tuple-element.32), channel_id=1, source_target_pairs={{0,2},{1,3},{2,0},{3,1},{4,6},{5,7},{6,4},{7,5},{8,10},{9,11},{10,... | collective-permute-start | bytes 196616 | tf_op jit(solution)/shard_map/ppermute | solution.py:180
  13.6 6.8 %collective-permute-start.5 = (bf16[128,256]{1,0:T(8,128)(2,1)S(1)}, bf16[128,256]{1,0:T(8,128)(2,1)S(1)}, u32[]{:S(2)}, u32[]{:S(2)}) collective-permute-start(bf16[128,256]{1,0:T(8,128)(2,1)S(1)} %get-tuple-element.33), channel_id=1, source_target_pairs={{0,1},{1,0},{2,3},{3,2},{4,5},{5,4},{6,7},{7,6},{8,9},{9,8},{10,11... | collective-permute-start | bytes 196616 | tf_op jit(solution)/shard_map/ppermute | solution.py:180
  14.5 11.2 %collective-permute-start.11 = (bf16[272,128]{1,0:T(8,128)(2,1)S(1)}, bf16[272,128]{1,0:T(8,128)(2,1)S(1)}, u32[]{:S(2)}, u32[]{:S(2)}) collective-permute-start(bf16[272,128]{1,0:T(8,128)(2,1)S(1)} %shard_map.98.rest_4_), channel_id=1, source_target_pairs={{0,3},{1,2},{2,1},{3,0},{4,7},{5,6},{6,5},{7,4},{8,11},{9,10},{10,... | collective-permute-start | bytes 208904 | tf_op jit(solution)/shard_map/ppermute | solution.py:197
  18.0 7.7 %collective-permute-start.10 = (bf16[272,128]{1,0:T(8,128)(2,1)S(1)}, bf16[272,128]{1,0:T(8,128)(2,1)S(1)}, u32[]{:S(2)}, u32[]{:S(2)}) collective-permute-start(bf16[272,128]{1,0:T(8,128)(2,1)S(1)} %shard_map.98.rest_4_), channel_id=1, source_target_pairs={{0,1},{1,0},{2,3},{3,2},{4,5},{5,4},{6,7},{7,6},{8,9},{9,8},{10,11... | collective-permute-start | bytes 208904 | tf_op jit(solution)/shard_map/ppermute | solution.py:197
  20.5 8.6 %copy-start.1 = (bf16[256,256]{1,0:T(8,128)(2,1)S(1)}, bf16[256,256]{1,0:T(8,128)(2,1)}, u32[]{:S(2)}) copy-start(bf16[256,256]{1,0:T(8,128)(2,1)} %weight_ref.3) | copy-start | bytes 393220
  20.5 6.9 %collective-permute-start.9 = (bf16[128,256]{1,0:T(8,128)(2,1)S(1)}, bf16[128,256]{1,0:T(8,128)(2,1)S(1)}, u32[]{:S(2)}, u32[]{:S(2)}) collective-permute-start(bf16[128,256]{1,0:T(8,128)(2,1)S(1)} %shard_map.99.rest_0_), channel_id=1, source_target_pairs={{0,3},{1,2},{2,1},{3,0},{4,7},{5,6},{6,5},{7,4},{8,11},{9,10},{10,... | collective-permute-start | bytes 196616 | tf_op jit(solution)/shard_map/ppermute | solution.py:180
  23.5 5.6 %collective-permute-start.8 = (bf16[128,256]{1,0:T(8,128)(2,1)S(1)}, bf16[128,256]{1,0:T(8,128)(2,1)S(1)}, u32[]{:S(2)}, u32[]{:S(2)}) collective-permute-start(bf16[128,256]{1,0:T(8,128)(2,1)S(1)} %shard_map.99.rest_0_), channel_id=1, source_target_pairs={{0,2},{1,3},{2,0},{3,1},{4,6},{5,7},{6,4},{7,5},{8,10},{9,11},{10,... | collective-permute-start | bytes 196616 | tf_op jit(solution)/shard_map/ppermute | solution.py:180
  23.5 5.6 %collective-permute-start.7 = (bf16[128,256]{1,0:T(8,128)(2,1)S(1)}, bf16[128,256]{1,0:T(8,128)(2,1)S(1)}, u32[]{:S(2)}, u32[]{:S(2)}) collective-permute-start(bf16[128,256]{1,0:T(8,128)(2,1)S(1)} %shard_map.99.rest_0_), channel_id=1, source_target_pairs={{0,1},{1,0},{2,3},{3,2},{4,5},{5,4},{6,7},{7,6},{8,9},{9,8},{10,11... | collective-permute-start | bytes 196616 | tf_op jit(solution)/shard_map/ppermute | solution.py:180
  29.9 1.5 %collective-permute-start.12 = (bf16[384,256]{1,0:T(8,128)(2,1)S(1)}, bf16[384,256]{1,0:T(8,128)(2,1)S(1)}, u32[]{:S(2)}, u32[]{:S(2)}) collective-permute-start(bf16[384,256]{1,0:T(8,128)(2,1)S(1)} %get-tuple-element.43), channel_id=1, source_target_pairs={{0,4},{4,0},{8,12},{12,8},{1,5},{5,1},{9,13},{13,9},{2,6},{6,2},{1... | collective-permute-start | bytes 589832 | tf_op jit(solution)/shard_map/ppermute | solution.py:241
  31.4 4.6 %collective-permute-start.14 = (bf16[128,256]{1,0:T(8,128)(2,1)S(1)}, bf16[128,256]{1,0:T(8,128)(2,1)S(1)}, u32[]{:S(2)}, u32[]{:S(2)}) collective-permute-start(bf16[128,256]{1,0:T(8,128)(2,1)S(1)} %get-tuple-element.47.own_ref), channel_id=1, source_target_pairs={{0,8},{4,12},{8,0},{12,4},{1,9},{5,13},{9,1},{13,5},{2,10},{6,14},... | collective-permute-start | bytes 196616 | tf_op jit(solution)/shard_map/ppermute | solution.py:241
  33.1 4.3 %collective-permute-start.13 = (bf16[128,256]{1,0:T(8,128)(2,1)S(1)}, bf16[128,256]{1,0:T(8,128)(2,1)S(1)}, u32[]{:S(2)}, u32[]{:S(2)}) collective-permute-start(bf16[128,256]{1,0:T(8,128)(2,1)S(1)} %get-tuple-element.45), channel_id=1, source_target_pairs={{0,8},{4,12},{8,0},{12,4},{1,9},{5,13},{9,1},{13,5},{2,10},{6,14},... | collective-permute-start | bytes 196616 | tf_op jit(solution)/shard_map/ppermute | solution.py:241
  36.0 1.4 %collective-permute-start.15 = (bf16[128,256]{1,0:T(8,128)(2,1)S(1)}, bf16[128,256]{1,0:T(8,128)(2,1)S(1)}, u32[]{:S(2)}, u32[]{:S(2)}) collective-permute-start(bf16[128,256]{1,0:T(8,128)(2,1)S(1)} %shard_map.102.own_ref), channel_id=1, source_target_pairs={{0,4},{4,0},{8,12},{12,8},{1,5},{5,1},{9,13},{13,9},{2,6},{6,2},{1... | collective-permute-start | bytes 196616 | tf_op jit(solution)/shard_map/ppermute | solution.py:241

commit v6 on v5

--- a/solution.py
+++ b/solution.py
@@ -34,9 +34,14 @@
     return pl.ds(pl.multiple_of(block * rows, rows), rows)
 
 
-def scale_kernel(deg_ref, x_ref, out_ref):
+def zero_kernel(out_ref):
+    out_ref[...] = jnp.zeros_like(out_ref)
+
+
+def scale_kernel(cnt_ref, zero_ref, deg_ref, x_ref, out_ref, used_ref):
     scale = wide(row_scale(deg_ref[...].reshape(1, TILE)), x_ref.shape[1])
     out_ref[...] = (scale * x_ref[...].astype(F32)).astype(BF16)
+    used_ref[...] = zero_ref[...] + cnt_ref[0, 0]
 
 
 def extra_kernel(deg_ref, cot_ref, extra_ref):
@@ -47,27 +52,22 @@
     extra_ref[width:] = degree.astype(BF16)
 
 
-def place_tiles(idx_ref, cnt_ref, values_ref, out_ref, transposed, bits):
+def block_kernel(transposed, n_rows, n_cols, idx_ref, used_ref, values_ref, *rest):
+    out_ref = rest[-1]
     row_me, col_me = lax.axis_index("rows"), lax.axis_index("cols")
-    used = cnt_ref[0, 0]
+    used = jnp.broadcast_to(used_ref[:1, :], (TILE, TILE))
+    bits = n_rows.bit_length() - 1
     out_ref[...] = jnp.zeros_like(out_ref)
     for slot in range(values_ref.shape[2]):
-        live = slot < used
-        row = jnp.where(live, idx_ref[0, 0, 0, slot], 0) ^ col_me
-        col = jnp.where(live, idx_ref[0, 0, 1, slot], 0) ^ row_me
-        row = jnp.where(live, row, 0)
-        col = jnp.where(live, col, 0)
-        tile = jnp.where(live, values_ref[0, 0, slot], jnp.zeros((TILE, TILE), BF16))
+        row = jnp.clip(idx_ref[0, 0, 0, slot], 0, n_cols - 1) ^ col_me
+        col = jnp.clip(idx_ref[0, 0, 1, slot], 0, n_rows - 1) ^ row_me
+        tile = jnp.where(slot < used, values_ref[0, 0, slot].astype(F32), 0.0)
         at = (row, col)
         if transposed:
             tile = tile.T
             at = (reverse_bits(col, bits), row)
         here = (rows_at(at[0]), rows_at(at[1]))
-        out_ref[here] = (out_ref[here].astype(F32) + tile.astype(F32)).astype(BF16)
-
-
-def block_kernel(transposed, bits, idx_ref, cnt_ref, values_ref, *rest):
-    place_tiles(idx_ref, cnt_ref, values_ref, rest[-1], transposed, bits)
+        out_ref[here] = (out_ref[here].astype(F32) + tile).astype(BF16)
 
 
 def forward_kernel(n_rows, n_cols, matrix_ref, *rest):
@@ -184,14 +184,17 @@
 
     block_shape = shape((TILE, width), BF16)
     slow = pl.CostEstimate(flops=10**10, bytes_accessed=10**6, transcendentals=0)
-    scaled = call(scale_kernel, block_shape, [vmem] * 2, cost=slow)(degree, features)
+    count_shape = shape((8, TILE), jnp.int32)
+    zero = call(zero_kernel, count_shape, [], cost=slow)()
+    scaled, used = call(
+        scale_kernel, (block_shape, count_shape), [smem] + [vmem] * 3, cost=slow
+    )(tile_count, zero, degree, features)
     extra = call(extra_kernel, shape((width + DEG_ROWS, TILE), BF16), [vmem] * 2)(degree, cotangent)
-    bits = n_rows.bit_length() - 1
     matrix = call(
-        functools.partial(block_kernel, False, bits),
+        functools.partial(block_kernel, False, n_rows, n_cols),
         shape((n_cols * TILE, n_rows * TILE), BF16),
-        [smem, smem, vmem],
-    )(tile_index, tile_count, tile_values)
+        [smem, vmem, vmem],
+    )(tile_index, used, tile_values)
     blocks = shifted(scaled, "rows", n_rows)
     def sent(block, shift):
         return lax.ppermute(block, "cols", [(j, j ^ shift) for j in range(n_cols)])
@@ -209,16 +212,16 @@
         slow,
     )(matrix, *blocks)
     back_matrix = call(
-        functools.partial(block_kernel, True, bits),
+        functools.partial(block_kernel, True, n_rows, n_cols),
         shape((n_rows * TILE, n_cols * TILE), BF16),
-        [smem, smem, vmem] + [pl.ANY],
-    )(tile_index, tile_count, tile_values, parts[0])
-    parts, tied = lax.optimization_barrier((parts, extra))
+        [smem, vmem, vmem, pl.ANY],
+    )(tile_index, used, tile_values, parts[0])
+    sums = shifted(parts, "cols", n_cols)
+    back_matrix, tied = lax.optimization_barrier((back_matrix, extra))
     for shift in reversed(late):
         extras[shift] = sent(tied, shift)
-    sums = shifted(parts, "cols", n_cols)
     held = [extras[shift] for shift in early]
-    sums, held = lax.optimization_barrier((sums[::-1], held))
+    sums, held, back_matrix = lax.optimization_barrier((sums[::-1], held, back_matrix))
     for shift, block in zip(early, held):
         extras[shift] = block
     aggregated = call(own_rows_kernel, block_shape, [vmem] * (1 + n_cols))(degree, *sums)

time: 38.5 us -> 37.4 us (0.971)
  local copies, waits for them, and re-layouts: 1.55 us -> 0.16 us
  starting transfers between devices: 20.6 us -> 21 us
    unnamed x14 -> x12, local copies, waits for them, and re-layouts: 1.55 us -> 0.16 us
    pallas_call x3 -> x4, Pallas kernels: 1.52 us -> 1.55 us  [the longest x1 0.75 us: shards(): call(functools.partial(block_kernel, True, n_rows, n_cols), shape((n_rows...]
  transfers between devices with their start and end apart: 16 -> 16, of which waited for: 6 -> 8; matrix products, arithmetic and copies ran while one was open for 0% -> 0% of each run, Pallas kernels for 5% -> 5%
where the time goes in v6:
time: 37.4 us; the launch traced here: 37.2 us
  starting transfers between devices  21 us (56%)
  waiting for transfers between devices  11 us (29%)
  Pallas kernels  3.63 us (10%)
  between operations  1.43 us (4%)
    ppermute x9, starting transfers between devices, shifted(): lax.ppermute(source, axis, [(i, i ^ shift) for i in range(size)])  12.1 us
    ppermute x3, starting transfers between devices, sent(): return lax.ppermute(block, 'cols', [(j, j ^ shift) for j in range(n_cols)])  6.72 us
    ppermute x9, waiting for transfers between devices, shifted(): lax.ppermute(source, axis, [(i, i ^ shift) for i in range(size)])  5.63 us
    ppermute x4, waiting for transfers between devices, partner(): return lax.ppermute(block, 'rows', [(i, i ^ mask) for i in range(n_rows)])  5.35 us
    ppermute x4, starting transfers between devices, partner(): return lax.ppermute(block, 'rows', [(i, i ^ mask) for i in range(n_rows)])  2.23 us
    pallas_call x1, Pallas kernels, shards(): call(last_kernel, (block_shape, block_shape, shape((width, width), F32)),...  0.85 us
    pallas_call x1, Pallas kernels, shards(): call(functools.partial(block_kernel, True, n_rows, n_cols), shape((n_rows...  0.75 us
  transfers between devices with their start and end apart: 16, of which 8 were waited for; matrix products, arithmetic and copies ran while one was open for 0% of the time, Pallas kernels for 5%

profile of v6, /device:TPU:0, one launch (start us, length us, event | category | flops | bytes accessed | tf_op | source)
XLA Modules:
  0.0 37.2 jit_solution(9441365259693441826)
XLA Ops:
  1.3 0.1 copy-done.5
  1.6 2.4 %collective-permute-start.2 = (bf16[128,256]{1,0:T(8,128)(2,1)S(1)}, bf16[128,256]{1,0:T(8,128)(2,1)S(1)}, u32[]{:S(2)}, u32[]{:S(2)}) collective-permute-start(bf16[128,256]{1,0:T(8,128)(2,1)S(1)} %get-tuple-element.28.rest_0_), channel_id=1, source_target_pairs={{0,12},{4,8},{8,4},{12,0},{1,13},{5,9},{9,5},{13,1},{2,14},{6,10},... | collective-permute-start | bytes 196616 | tf_op jit(solution)/shard_map/ppermute | solution.py:180
  4.0 0.6 %collective-permute-start.1 = (bf16[128,256]{1,0:T(8,128)(2,1)S(1)}, bf16[128,256]{1,0:T(8,128)(2,1)S(1)}, u32[]{:S(2)}, u32[]{:S(2)}) collective-permute-start(bf16[128,256]{1,0:T(8,128)(2,1)S(1)} %get-tuple-element.28.rest_0_), channel_id=1, source_target_pairs={{0,8},{4,12},{8,0},{12,4},{1,9},{5,13},{9,1},{13,5},{2,10},{6,14},... | collective-permute-start | bytes 196616 | tf_op jit(solution)/shard_map/ppermute | solution.py:180
  4.7 2.9 %collective-permute-start.6 = (bf16[272,128]{1,0:T(8,128)(2,1)S(1)}, bf16[272,128]{1,0:T(8,128)(2,1)S(1)}, u32[]{:S(2)}, u32[]{:S(2)}) collective-permute-start(bf16[272,128]{1,0:T(8,128)(2,1)S(1)} %shard_map.98.rest_4_), channel_id=1, source_target_pairs={{0,2},{1,3},{2,0},{3,1},{4,6},{5,7},{6,4},{7,5},{8,10},{9,11},{10,... | collective-permute-start | bytes 208904 | tf_op jit(solution)/shard_map/ppermute | solution.py:200
  7.7 0.7 %shard_map.96.matrix_ref = bf16[512,512]{1,0:T(8,128)(2,1)S(1)} custom-call(s32[1,1,2,8]{3,2,1,0:T(2,128)S(1)} %copy-done.4, s32[8,128]{1,0:T(8,128)S(1)} %get-tuple-element.27.used_ref, bf16[1,1,8,128,128]{4,3,2,1,0:T(8,128)(2,1)S(1)} %copy-done), custom_call_target="tpu_custom_call" | custom-call | tf_op jit(solution)/shard_map/pallas_call | solution.py:193
  8.4 0.3 collective-permute-done.1.rest_2_
  8.7 0.3 shard_map.97
  9.0 3.9 %collective-permute-start.3 = (bf16[128,256]{1,0:T(8,128)(2,1)S(1)}, bf16[128,256]{1,0:T(8,128)(2,1)S(1)}, u32[]{:S(2)}, u32[]{:S(2)}) collective-permute-start(bf16[128,256]{1,0:T(8,128)(2,1)S(1)} %get-tuple-element.29), channel_id=1, source_target_pairs={{0,3},{1,2},{2,1},{3,0},{4,7},{5,6},{6,5},{7,4},{8,11},{9,10},{10,... | collective-permute-start | bytes 196616 | tf_op jit(solution)/shard_map/ppermute | solution.py:180
  12.9 0.6 %collective-permute-start.5 = (bf16[128,256]{1,0:T(8,128)(2,1)S(1)}, bf16[128,256]{1,0:T(8,128)(2,1)S(1)}, u32[]{:S(2)}, u32[]{:S(2)}) collective-permute-start(bf16[128,256]{1,0:T(8,128)(2,1)S(1)} %get-tuple-element.31), channel_id=1, source_target_pairs={{0,1},{1,0},{2,3},{3,2},{4,5},{5,4},{6,7},{7,6},{8,9},{9,8},{10,11... | collective-permute-start | bytes 196616 | tf_op jit(solution)/shard_map/ppermute | solution.py:180
  13.5 0.8 %shard_map.99.matrix_ref = bf16[512,512]{1,0:T(8,128)(2,1)S(1)} custom-call(s32[1,1,2,8]{3,2,1,0:T(2,128)S(1)} %copy-done.4, s32[8,128]{1,0:T(8,128)S(1)} %get-tuple-element.27.used_ref, bf16[1,1,8,128,128]{4,3,2,1,0:T(8,128)(2,1)S(1)} %copy-done, bf16[128,256]{1,0:T(8,128)(2,1)S(1)} %get-tuple-element.38.rest_0_.rest_3_), custom_call_target="tpu_custom_call" | custom-call | tf_op jit(solution)/shard_map/pallas_call | solution.py:214
  14.3 3.8 %collective-permute-start.11 = (bf16[272,128]{1,0:T(8,128)(2,1)S(1)}, bf16[272,128]{1,0:T(8,128)(2,1)S(1)}, u32[]{:S(2)}, u32[]{:S(2)}) collective-permute-start(bf16[272,128]{1,0:T(8,128)(2,1)S(1)} %shard_map.98.rest_4_), channel_id=1, source_target_pairs={{0,3},{1,2},{2,1},{3,0},{4,7},{5,6},{6,5},{7,4},{8,11},{9,10},{10,... | collective-permute-start | bytes 208904 | tf_op jit(solution)/shard_map/ppermute | solution.py:200
  18.1 1.7 %collective-permute-done.4.rest_1_ = bf16[128,256]{1,0:T(8,128)(2,1)S(1)} collective-permute-done((bf16[128,256]{1,0:T(8,128)(2,1)S(1)}, bf16[128,256]{1,0:T(8,128)(2,1)S(1)}, u32[]{:S(2)}, u32[]{:S(2)}) %collective-permute-start.4) | collective-permute-done | bytes 65568 | tf_op jit(solution)/shard_map/ppermute | solution.py:180
  19.9 2.9 %collective-permute-start.9 = (bf16[128,256]{1,0:T(8,128)(2,1)S(1)}, bf16[128,256]{1,0:T(8,128)(2,1)S(1)}, u32[]{:S(2)}, u32[]{:S(2)}) collective-permute-start(bf16[128,256]{1,0:T(8,128)(2,1)S(1)} %shard_map.100.rest_0_), channel_id=1, source_target_pairs={{0,3},{1,2},{2,1},{3,0},{4,7},{5,6},{6,5},{7,4},{8,11},{9,10},{10,... | collective-permute-start | bytes 196616 | tf_op jit(solution)/shard_map/ppermute | solution.py:180
  22.8 1.5 %collective-permute-start.7 = (bf16[128,256]{1,0:T(8,128)(2,1)S(1)}, bf16[128,256]{1,0:T(8,128)(2,1)S(1)}, u32[]{:S(2)}, u32[]{:S(2)}) collective-permute-start(bf16[128,256]{1,0:T(8,128)(2,1)S(1)} %shard_map.100.rest_0_), channel_id=1, source_target_pairs={{0,1},{1,0},{2,3},{3,2},{4,5},{5,4},{6,7},{7,6},{8,9},{9,8},{10,11... | collective-permute-start | bytes 196616 | tf_op jit(solution)/shard_map/ppermute | solution.py:180
  24.4 1.9 %collective-permute-done.9.rest_3_ = bf16[128,256]{1,0:T(8,128)(2,1)S(1)} collective-permute-done((bf16[128,256]{1,0:T(8,128)(2,1)S(1)}, bf16[128,256]{1,0:T(8,128)(2,1)S(1)}, u32[]{:S(2)}, u32[]{:S(2)}) %collective-permute-start.9) | collective-permute-done | bytes 65568 | tf_op jit(solution)/shard_map/ppermute | solution.py:180
  26.3 1.7 %collective-permute-done.8.rest_2_ = bf16[128,256]{1,0:T(8,128)(2,1)S(1)} collective-permute-done((bf16[128,256]{1,0:T(8,128)(2,1)S(1)}, bf16[128,256]{1,0:T(8,128)(2,1)S(1)}, u32[]{:S(2)}, u32[]{:S(2)}) %collective-permute-start.8) | collective-permute-done | bytes 65568 | tf_op jit(solution)/shard_map/ppermute | solution.py:180
  28.0 0.7 %shard_map.101 = (bf16[128,256]{1,0:T(8,128)(2,1)S(1)}, f32[256,256]{1,0:T(8,128)S(1)}, f32[128,256]{1,0:T(8,128)S(1)}, bf16[384,256]{1,0:T(8,128)(2,1)S(1)}) custom-call(bf16[256,256]{1,0:T(8,128)(2,1)S(1)} %copy-done.1, bf16[512,512]{1,0:T(8,128)(2,1)S(1)} %shard_map.99.matrix_ref, bf16[128,256]{1,0:T(8,128)(2,1)S(1)} %shard_map.100.rest_0_, ...), custom_call_target="tpu_custom_call" | custom-call | tf_op jit(solution)/shard_map/pallas_call | solution.py:231
  28.8 1.4 %collective-permute-done.12.got_ref.term_got_ref = bf16[384,256]{1,0:T(8,128)(2,1)S(1)} collective-permute-done((bf16[384,256]{1,0:T(8,128)(2,1)S(1)}, bf16[384,256]{1,0:T(8,128)(2,1)S(1)}, u32[]{:S(2)}, u32[]{:S(2)}) %collective-permute-start.12) | collective-permute-done | bytes 196640 | tf_op jit(solution)/shard_map/ppermute | solution.py:244
  30.3 1.5 %collective-permute-start.14 = (bf16[128,256]{1,0:T(8,128)(2,1)S(1)}, bf16[128,256]{1,0:T(8,128)(2,1)S(1)}, u32[]{:S(2)}, u32[]{:S(2)}) collective-permute-start(bf16[128,256]{1,0:T(8,128)(2,1)S(1)} %get-tuple-element.47.own_ref), channel_id=1, source_target_pairs={{0,8},{4,12},{8,0},{12,4},{1,9},{5,13},{9,1},{13,5},{2,10},{6,14},... | collective-permute-start | bytes 196616 | tf_op jit(solution)/shard_map/ppermute | solution.py:244
  31.8 0.6 %collective-permute-start.13 = (bf16[128,256]{1,0:T(8,128)(2,1)S(1)}, bf16[128,256]{1,0:T(8,128)(2,1)S(1)}, u32[]{:S(2)}, u32[]{:S(2)}) collective-permute-start(bf16[128,256]{1,0:T(8,128)(2,1)S(1)} %get-tuple-element.45), channel_id=1, source_target_pairs={{0,8},{4,12},{8,0},{12,4},{1,9},{5,13},{9,1},{13,5},{2,10},{6,14},... | collective-permute-start | bytes 196616 | tf_op jit(solution)/shard_map/ppermute | solution.py:244
  32.4 2.7 %collective-permute-done.14.got_ref = bf16[128,256]{1,0:T(8,128)(2,1)S(1)} collective-permute-done((bf16[128,256]{1,0:T(8,128)(2,1)S(1)}, bf16[128,256]{1,0:T(8,128)(2,1)S(1)}, u32[]{:S(2)}, u32[]{:S(2)}) %collective-permute-start.14) | collective-permute-done | bytes 65568 | tf_op jit(solution)/shard_map/ppermute | solution.py:244
  35.2 0.9 %collective-permute-done.13.got_ref = bf16[128,256]{1,0:T(8,128)(2,1)S(1)} collective-permute-done((bf16[128,256]{1,0:T(8,128)(2,1)S(1)}, bf16[128,256]{1,0:T(8,128)(2,1)S(1)}, u32[]{:S(2)}, u32[]{:S(2)}) %collective-permute-start.13) | collective-permute-done | bytes 65568 | tf_op jit(solution)/shard_map/ppermute | solution.py:244
  36.1 0.3 collective-permute-done.15.other_ref
  36.4 0.8 %shard_map.104 = (bf16[128,256]{1,0:T(8,128)(2,1)}, bf16[128,256]{1,0:T(8,128)(2,1)}, f32[256,256]{1,0:T(8,128)}) custom-call(s32[128]{0:T(128)S(1)} %copy-done.3, bf16[256,256]{1,0:T(8,128)(2,1)S(1)} %copy-done.1, f32[128,256]{1,0:T(8,128)S(1)} %get-tuple-element.44.keep_ref, bf16[128,256]{1,0:T(8,128)(2,1)S(1)} %collective-permute-done.13.got_ref, ...), custom_call_target="tpu_custom_call" | custom-call | tf_op jit(solution)/shard_map/pallas_call | solution.py:268
  (31 shorter events, 0.5 us)
Async XLA Ops:
  0.6 0.8 %copy-start.5 = (bf16[128,256]{1,0:T(8,128)(2,1)S(1)}, bf16[128,256]{1,0:T(8,128)(2,1)}, u32[]{:S(2)}) copy-start(bf16[128,256]{1,0:T(8,128)(2,1)} %x_ref.1) | copy-start | bytes 196612
  0.6 0.8 %copy-start.3 = (s32[128]{0:T(128)S(1)}, s32[128]{0:T(128)}, u32[]{:S(2)}) copy-start(s32[128]{0:T(128)} %deg_ref.7) | copy-start | bytes 1540
  1.5 3.2 %copy-start.2 = (bf16[128,256]{1,0:T(8,128)(2,1)S(1)}, bf16[128,256]{1,0:T(8,128)(2,1)}, u32[]{:S(2)}) copy-start(bf16[128,256]{1,0:T(8,128)(2,1)} %cot_ref.1) | copy-start | bytes 196612
  1.5 6.2 %copy-start = (bf16[1,1,8,128,128]{4,3,2,1,0:T(8,128)(2,1)S(1)}, bf16[1,1,8,128,128]{4,3,2,1,0:T(8,128)(2,1)}, u32[]{:S(2)}) copy-start(bf16[1,1,8,128,128]{4,3,2,1,0:T(8,128)(2,1)} %values_ref.3) | copy-start | bytes 786436
  1.6 6.8 %collective-permute-start.2 = (bf16[128,256]{1,0:T(8,128)(2,1)S(1)}, bf16[128,256]{1,0:T(8,128)(2,1)S(1)}, u32[]{:S(2)}, u32[]{:S(2)}) collective-permute-start(bf16[128,256]{1,0:T(8,128)(2,1)S(1)} %get-tuple-element.28.rest_0_), channel_id=1, source_target_pairs={{0,12},{4,8},{8,4},{12,0},{1,13},{5,9},{9,5},{13,1},{2,14},{6,10},... | collective-permute-start | bytes 196616 | tf_op jit(solution)/shard_map/ppermute | solution.py:180
  4.0 4.7 %collective-permute-start.1 = (bf16[128,256]{1,0:T(8,128)(2,1)S(1)}, bf16[128,256]{1,0:T(8,128)(2,1)S(1)}, u32[]{:S(2)}, u32[]{:S(2)}) collective-permute-start(bf16[128,256]{1,0:T(8,128)(2,1)S(1)} %get-tuple-element.28.rest_0_), channel_id=1, source_target_pairs={{0,8},{4,12},{8,0},{12,4},{1,9},{5,13},{9,1},{13,5},{2,10},{6,14},... | collective-permute-start | bytes 196616 | tf_op jit(solution)/shard_map/ppermute | solution.py:180
  4.7 4.0 %collective-permute-start = (bf16[128,256]{1,0:T(8,128)(2,1)S(1)}, bf16[128,256]{1,0:T(8,128)(2,1)S(1)}, u32[]{:S(2)}, u32[]{:S(2)}) collective-permute-start(bf16[128,256]{1,0:T(8,128)(2,1)S(1)} %get-tuple-element.28.rest_0_), channel_id=1, source_target_pairs={{0,4},{4,0},{8,12},{12,8},{1,5},{5,1},{9,13},{13,9},{2,6},{6,2},{1... | collective-permute-start | bytes 196616 | tf_op jit(solution)/shard_map/ppermute | solution.py:180
  4.7 2.9 %copy-start.4 = (s32[1,1,2,8]{3,2,1,0:T(2,128)S(1)}, s32[1,1,2,8]{3,2,1,0:T(2,128)}, u32[]{:S(2)}) copy-start(s32[1,1,2,8]{3,2,1,0:T(2,128)} %idx_ref.3) | copy-start | bytes 196
  4.7 13.4 %collective-permute-start.6 = (bf16[272,128]{1,0:T(8,128)(2,1)S(1)}, bf16[272,128]{1,0:T(8,128)(2,1)S(1)}, u32[]{:S(2)}, u32[]{:S(2)}) collective-permute-start(bf16[272,128]{1,0:T(8,128)(2,1)S(1)} %shard_map.98.rest_4_), channel_id=1, source_target_pairs={{0,2},{1,3},{2,0},{3,1},{4,6},{5,7},{6,4},{7,5},{8,10},{9,11},{10,... | collective-permute-start | bytes 208904 | tf_op jit(solution)/shard_map/ppermute | solution.py:200
  9.0 9.1 %collective-permute-start.3 = (bf16[128,256]{1,0:T(8,128)(2,1)S(1)}, bf16[128,256]{1,0:T(8,128)(2,1)S(1)}, u32[]{:S(2)}, u32[]{:S(2)}) collective-permute-start(bf16[128,256]{1,0:T(8,128)(2,1)S(1)} %get-tuple-element.29), channel_id=1, source_target_pairs={{0,3},{1,2},{2,1},{3,0},{4,7},{5,6},{6,5},{7,4},{8,11},{9,10},{10,... | collective-permute-start | bytes 196616 | tf_op jit(solution)/shard_map/ppermute | solution.py:180
  12.9 6.9 %collective-permute-start.4 = (bf16[128,256]{1,0:T(8,128)(2,1)S(1)}, bf16[128,256]{1,0:T(8,128)(2,1)S(1)}, u32[]{:S(2)}, u32[]{:S(2)}) collective-permute-start(bf16[128,256]{1,0:T(8,128)(2,1)S(1)} %get-tuple-element.30), channel_id=1, source_target_pairs={{0,2},{1,3},{2,0},{3,1},{4,6},{5,7},{6,4},{7,5},{8,10},{9,11},{10,... | collective-permute-start | bytes 196616 | tf_op jit(solution)/shard_map/ppermute | solution.py:180
  12.9 6.9 %collective-permute-start.5 = (bf16[128,256]{1,0:T(8,128)(2,1)S(1)}, bf16[128,256]{1,0:T(8,128)(2,1)S(1)}, u32[]{:S(2)}, u32[]{:S(2)}) collective-permute-start(bf16[128,256]{1,0:T(8,128)(2,1)S(1)} %get-tuple-element.31), channel_id=1, source_target_pairs={{0,1},{1,0},{2,3},{3,2},{4,5},{5,4},{6,7},{7,6},{8,9},{9,8},{10,11... | collective-permute-start | bytes 196616 | tf_op jit(solution)/shard_map/ppermute | solution.py:180
  14.3 13.7 %copy-start.1 = (bf16[256,256]{1,0:T(8,128)(2,1)S(1)}, bf16[256,256]{1,0:T(8,128)(2,1)}, u32[]{:S(2)}) copy-start(bf16[256,256]{1,0:T(8,128)(2,1)} %weight_ref.3) | copy-start | bytes 393220
  14.3 10.1 %collective-permute-start.11 = (bf16[272,128]{1,0:T(8,128)(2,1)S(1)}, bf16[272,128]{1,0:T(8,128)(2,1)S(1)}, u32[]{:S(2)}, u32[]{:S(2)}) collective-permute-start(bf16[272,128]{1,0:T(8,128)(2,1)S(1)} %shard_map.98.rest_4_), channel_id=1, source_target_pairs={{0,3},{1,2},{2,1},{3,0},{4,7},{5,6},{6,5},{7,4},{8,11},{9,10},{10,... | collective-permute-start | bytes 208904 | tf_op jit(solution)/shard_map/ppermute | solution.py:200
  18.1 6.3 %collective-permute-start.10 = (bf16[272,128]{1,0:T(8,128)(2,1)S(1)}, bf16[272,128]{1,0:T(8,128)(2,1)S(1)}, u32[]{:S(2)}, u32[]{:S(2)}) collective-permute-start(bf16[272,128]{1,0:T(8,128)(2,1)S(1)} %shard_map.98.rest_4_), channel_id=1, source_target_pairs={{0,1},{1,0},{2,3},{3,2},{4,5},{5,4},{6,7},{7,6},{8,9},{9,8},{10,11... | collective-permute-start | bytes 208904 | tf_op jit(solution)/shard_map/ppermute | solution.py:200
  19.9 6.4 %collective-permute-start.9 = (bf16[128,256]{1,0:T(8,128)(2,1)S(1)}, bf16[128,256]{1,0:T(8,128)(2,1)S(1)}, u32[]{:S(2)}, u32[]{:S(2)}) collective-permute-start(bf16[128,256]{1,0:T(8,128)(2,1)S(1)} %shard_map.100.rest_0_), channel_id=1, source_target_pairs={{0,3},{1,2},{2,1},{3,0},{4,7},{5,6},{6,5},{7,4},{8,11},{9,10},{10,... | collective-permute-start | bytes 196616 | tf_op jit(solution)/shard_map/ppermute | solution.py:180
  22.8 5.2 %collective-permute-start.8 = (bf16[128,256]{1,0:T(8,128)(2,1)S(1)}, bf16[128,256]{1,0:T(8,128)(2,1)S(1)}, u32[]{:S(2)}, u32[]{:S(2)}) collective-permute-start(bf16[128,256]{1,0:T(8,128)(2,1)S(1)} %shard_map.100.rest_0_), channel_id=1, source_target_pairs={{0,2},{1,3},{2,0},{3,1},{4,6},{5,7},{6,4},{7,5},{8,10},{9,11},{10,... | collective-permute-start | bytes 196616 | tf_op jit(solution)/shard_map/ppermute | solution.py:180
  22.8 5.2 %collective-permute-start.7 = (bf16[128,256]{1,0:T(8,128)(2,1)S(1)}, bf16[128,256]{1,0:T(8,128)(2,1)S(1)}, u32[]{:S(2)}, u32[]{:S(2)}) collective-permute-start(bf16[128,256]{1,0:T(8,128)(2,1)S(1)} %shard_map.100.rest_0_), channel_id=1, source_target_pairs={{0,1},{1,0},{2,3},{3,2},{4,5},{5,4},{6,7},{7,6},{8,9},{9,8},{10,11... | collective-permute-start | bytes 196616 | tf_op jit(solution)/shard_map/ppermute | solution.py:180
  28.7 1.5 %collective-permute-start.12 = (bf16[384,256]{1,0:T(8,128)(2,1)S(1)}, bf16[384,256]{1,0:T(8,128)(2,1)S(1)}, u32[]{:S(2)}, u32[]{:S(2)}) collective-permute-start(bf16[384,256]{1,0:T(8,128)(2,1)S(1)} %get-tuple-element.43), channel_id=1, source_target_pairs={{0,4},{4,0},{8,12},{12,8},{1,5},{5,1},{9,13},{13,9},{2,6},{6,2},{1... | collective-permute-start | bytes 589832 | tf_op jit(solution)/shard_map/ppermute | solution.py:244
  30.3 4.8 %collective-permute-start.14 = (bf16[128,256]{1,0:T(8,128)(2,1)S(1)}, bf16[128,256]{1,0:T(8,128)(2,1)S(1)}, u32[]{:S(2)}, u32[]{:S(2)}) collective-permute-start(bf16[128,256]{1,0:T(8,128)(2,1)S(1)} %get-tuple-element.47.own_ref), channel_id=1, source_target_pairs={{0,8},{4,12},{8,0},{12,4},{1,9},{5,13},{9,1},{13,5},{2,10},{6,14},... | collective-permute-start | bytes 196616 | tf_op jit(solution)/shard_map/ppermute | solution.py:244
  31.8 4.3 %collective-permute-start.13 = (bf16[128,256]{1,0:T(8,128)(2,1)S(1)}, bf16[128,256]{1,0:T(8,128)(2,1)S(1)}, u32[]{:S(2)}, u32[]{:S(2)}) collective-permute-start(bf16[128,256]{1,0:T(8,128)(2,1)S(1)} %get-tuple-element.45), channel_id=1, source_target_pairs={{0,8},{4,12},{8,0},{12,4},{1,9},{5,13},{9,1},{13,5},{2,10},{6,14},... | collective-permute-start | bytes 196616 | tf_op jit(solution)/shard_map/ppermute | solution.py:244
  35.1 1.3 %collective-permute-start.15 = (bf16[128,256]{1,0:T(8,128)(2,1)S(1)}, bf16[128,256]{1,0:T(8,128)(2,1)S(1)}, u32[]{:S(2)}, u32[]{:S(2)}) collective-permute-start(bf16[128,256]{1,0:T(8,128)(2,1)S(1)} %shard_map.103.own_ref), channel_id=1, source_target_pairs={{0,4},{4,0},{8,12},{12,8},{1,5},{5,1},{9,13},{13,9},{2,6},{6,2},{1... | collective-permute-start | bytes 196616 | tf_op jit(solution)/shard_map/ppermute | solution.py:244

commit v7 on v6

--- a/solution.py
+++ b/solution.py
@@ -91,38 +91,58 @@
     out_ref[...] = (scale * sums).astype(BF16)
 
 
-def middle_kernel(n_rows, n_cols, weight_ref, matrix_ref, *rest):
-    panels, extras = rest[:n_cols], rest[n_cols : 2 * n_cols]
-    act_ref, keep_ref, term_ref, send_ref, spread, term = rest[2 * n_cols :]
-    width = weight_ref.shape[0]
+def gradient_rows(panel, extra, weight):
+    width = weight.shape[0]
+    scale = wide(row_scale(extra[width : width + 1, :]), width)
+    aggregated = panel[...]
+    pre_act = jnp.dot(aggregated, weight, preferred_element_type=F32)
+    sig = 1.0 / (1.0 + jnp.exp(-pre_act))
+    cot = jnp.concatenate([extra[at : at + TILE] for at in range(0, width, TILE)], axis=1)
+    grad = cot.astype(F32) * sig * (1.0 + pre_act * (1.0 - sig))
+    term = lax.dot_general(
+        aggregated, grad.astype(BF16), (((0,), (0,)), ((), ())), preferred_element_type=F32
+    )
+    return (pre_act * sig).astype(BF16), (scale * grad).astype(BF16), term
+
+
+def middle_kernel(shifts, weight_ref, matrix_ref, *rest):
+    panels, extras = rest[: len(shifts)], rest[len(shifts) : 2 * len(shifts)]
+    act_ref, hidden_ref, term_ref, spread = rest[2 * len(shifts) :]
     weight = weight_ref[...]
-    term[...] = jnp.zeros_like(term)
-    for shift in range(n_cols):
-        extra = extras[shift]
-        scale = wide(row_scale(extra[width : width + 1, :]), width)
-        aggregated = panels[shift][...]
-        pre_act = jnp.dot(aggregated, weight, preferred_element_type=F32)
-        sig = 1.0 / (1.0 + jnp.exp(-pre_act))
+    spread[...] = jnp.zeros_like(spread)
+    term_ref[...] = jnp.zeros_like(term_ref)
+    for shift, panel, extra in zip(shifts, panels, extras):
+        activated, rows, term = gradient_rows(panel, extra, weight)
         if shift == 0:
-            act_ref[...] = (pre_act * sig).astype(BF16)
-        cot = jnp.concatenate([extra[at : at + TILE] for at in range(0, width, TILE)], axis=1)
-        grad = cot.astype(F32) * sig * (1.0 + pre_act * (1.0 - sig))
-        spread[shift * TILE : (shift + 1) * TILE] = (scale * grad).astype(BF16)
-        term[...] += lax.dot_general(
-            aggregated, grad.astype(BF16), (((0,), (0,)), ((), ())), preferred_element_type=F32
+            act_ref[...] = activated
+        spread[shift * TILE : (shift + 1) * TILE] = rows
+        term_ref[...] += term
+    for at in range(0, hidden_ref.shape[0], TILE):
+        hidden_ref[at : at + TILE] = jnp.dot(
+            matrix_ref[at : at + TILE, :], spread[...], preferred_element_type=F32
         )
-    half_rows = n_rows // 2 * TILE
-    for place in range(n_rows):
-        here = slice(place * TILE, (place + 1) * TILE)
-        hidden = jnp.dot(matrix_ref[here, :], spread[...], preferred_element_type=F32)
-        if place < n_rows // 2:
-            keep_ref[here] = hidden
+
+
+def finish_kernel(
+    shift, weight_ref, matrix_ref, panel, extra, hidden_ref, sum_ref, keep_ref, term_ref, send_ref, total
+):
+    activated, rows, term = gradient_rows(panel, extra, weight_ref[...])
+    half_rows = keep_ref.shape[0]
+    for at in range(0, hidden_ref.shape[0], TILE):
+        hidden = hidden_ref[at : at + TILE] + jnp.dot(
+            matrix_ref[at : at + TILE, shift * TILE : (shift + 1) * TILE],
+            rows,
+            preferred_element_type=F32,
+        )
+        if at < half_rows:
+            keep_ref[at : at + TILE] = hidden
         else:
-            send_ref[place * TILE - half_rows : (place + 1) * TILE - half_rows] = hidden.astype(BF16)
+            send_ref[at - half_rows : at - half_rows + TILE] = hidden.astype(BF16)
+    total[...] = sum_ref[...] + term
     side = lax.rem(lax.axis_index("rows"), 2)
-    half = width // 2
-    term_ref[...] = term[rows_at(side, half), :]
-    send_ref[half_rows:] = term[rows_at(1 - side, half), :].astype(BF16)
+    half = total.shape[0] // 2
+    term_ref[...] = total[rows_at(side, half), :]
+    send_ref[half_rows:] = total[rows_at(1 - side, half), :].astype(BF16)
 
 
 def fold_kernel(keep_ref, term_ref, got_ref, term_got_ref, keep_out, term_out, send_out):
@@ -228,17 +248,29 @@
     panels = shifted(aggregated, "cols", n_cols)
     half = n_rows // 2 * TILE
     side_rows = width // 2
-    kept_act, keep, term, send = call(
-        functools.partial(middle_kernel, n_rows, n_cols),
+    last = n_cols // 2
+    shifts = [shift for shift in range(n_cols) if shift != last]
+    kept_act, hidden, total = call(
+        functools.partial(middle_kernel, shifts),
+        (block_shape, shape((n_rows * TILE, width), F32), shape((width, width), F32)),
+        [vmem] * (2 + 2 * len(shifts)),
+        [vmem((n_cols * TILE, width), BF16)],
+    )(
+        weight,
+        back_matrix,
+        *[panels[shift] for shift in shifts],
+        *[extras[shift] for shift in shifts],
+    )
+    keep, term, send = call(
+        functools.partial(finish_kernel, last),
         (
-            block_shape,
             shape((half, width), F32),
             shape((side_rows, width), F32),
             shape((half + side_rows, width), BF16),
         ),
-        [vmem] * (2 + 2 * n_cols),
-        [vmem((n_cols * TILE, width), BF16), vmem((width, width), F32)],
-    )(weight, back_matrix, *panels, *extras)
+        [vmem] * 6,
+        [vmem((width, width), F32)],
+    )(weight, back_matrix, panels[last], extras[last], hidden, total)
 
     def partner(block, mask):
         return lax.ppermute(block, "rows", [(i, i ^ mask) for i in range(n_rows)])

time: 37.4 us -> 37.2 us (level)
  waiting for transfers between devices: 11 us -> 10.3 us
  Pallas kernels: 3.63 us -> 4.07 us
    ppermute x9, waiting for transfers between devices: 5.63 us -> 4.94 us  [shifted(): lax.ppermute(source, axis, [(i, i ^ shift) for i in range(size)])]
    pallas_call x1 -> x2, Pallas kernels: 0.75 us -> 1.17 us  [the longest x1 0.68 us: shards(): call(functools.partial(middle_kernel, shifts), (block_shape, shape((n_row...]
  transfers between devices with their start and end apart: 16 -> 16, of which waited for: 8 -> 8; matrix products, arithmetic and copies ran while one was open for 0% -> 0% of each run, Pallas kernels for 5% -> 7%
where the time goes in v7:
time: 37.2 us; the launch traced here: 37 us
  starting transfers between devices  21 us (56%)
  waiting for transfers between devices  10.3 us (28%)
  Pallas kernels  4.07 us (11%)
  between operations  1.45 us (4%)
    ppermute x9, starting transfers between devices, shifted(): lax.ppermute(source, axis, [(i, i ^ shift) for i in range(size)])  12.1 us
    ppermute x3, starting transfers between devices, sent(): return lax.ppermute(block, 'cols', [(j, j ^ shift) for j in range(n_cols)])  6.72 us
    ppermute x4, waiting for transfers between devices, partner(): return lax.ppermute(block, 'rows', [(i, i ^ mask) for i in range(n_rows)])  5.36 us
    ppermute x9, waiting for transfers between devices, shifted(): lax.ppermute(source, axis, [(i, i ^ shift) for i in range(size)])  4.94 us
    ppermute x4, starting transfers between devices, partner(): return lax.ppermute(block, 'rows', [(i, i ^ mask) for i in range(n_rows)])  2.23 us
    pallas_call x1, Pallas kernels, shards(): call(last_kernel, (block_shape, block_shape, shape((width, width), F32)),...  0.85 us
    pallas_call x1, Pallas kernels, shards(): call(functools.partial(block_kernel, True, n_rows, n_cols), shape((n_rows...  0.75 us
  transfers between devices with their start and end apart: 16, of which 8 were waited for; matrix products, arithmetic and copies ran while one was open for 0% of the time, Pallas kernels for 7%

profile of v7, /device:TPU:0, one launch (start us, length us, event | category | flops | bytes accessed | tf_op | source)
XLA Modules:
  0.0 37.0 jit_solution(8263647353331104693)
XLA Ops:
  1.6 2.4 %collective-permute-start.2 = (bf16[128,256]{1,0:T(8,128)(2,1)S(1)}, bf16[128,256]{1,0:T(8,128)(2,1)S(1)}, u32[]{:S(2)}, u32[]{:S(2)}) collective-permute-start(bf16[128,256]{1,0:T(8,128)(2,1)S(1)} %get-tuple-element.30.rest_0_), channel_id=1, source_target_pairs={{0,12},{4,8},{8,4},{12,0},{1,13},{5,9},{9,5},{13,1},{2,14},{6,10},... | collective-permute-start | bytes 196616 | tf_op jit(solution)/shard_map/ppermute | solution.py:200
  4.0 0.6 %collective-permute-start.1 = (bf16[128,256]{1,0:T(8,128)(2,1)S(1)}, bf16[128,256]{1,0:T(8,128)(2,1)S(1)}, u32[]{:S(2)}, u32[]{:S(2)}) collective-permute-start(bf16[128,256]{1,0:T(8,128)(2,1)S(1)} %get-tuple-element.30.rest_0_), channel_id=1, source_target_pairs={{0,8},{4,12},{8,0},{12,4},{1,9},{5,13},{9,1},{13,5},{2,10},{6,14},... | collective-permute-start | bytes 196616 | tf_op jit(solution)/shard_map/ppermute | solution.py:200
  4.7 2.9 %collective-permute-start.6 = (bf16[272,128]{1,0:T(8,128)(2,1)S(1)}, bf16[272,128]{1,0:T(8,128)(2,1)S(1)}, u32[]{:S(2)}, u32[]{:S(2)}) collective-permute-start(bf16[272,128]{1,0:T(8,128)(2,1)S(1)} %shard_map.98.rest_3_), channel_id=1, source_target_pairs={{0,2},{1,3},{2,0},{3,1},{4,6},{5,7},{6,4},{7,5},{8,10},{9,11},{10,... | collective-permute-start | bytes 208904 | tf_op jit(solution)/shard_map/ppermute | solution.py:220
  7.7 0.7 %shard_map.96.matrix_ref = bf16[512,512]{1,0:T(8,128)(2,1)S(1)} custom-call(s32[1,1,2,8]{3,2,1,0:T(2,128)S(1)} %copy-done.4, s32[8,128]{1,0:T(8,128)S(1)} %get-tuple-element.29.used_ref, bf16[1,1,8,128,128]{4,3,2,1,0:T(8,128)(2,1)S(1)} %copy-done.1), custom_call_target="tpu_custom_call" | custom-call | tf_op jit(solution)/shard_map/pallas_call | solution.py:213
  8.4 0.3 collective-permute-done.1.rest_2_
  8.7 0.3 shard_map.97
  9.0 3.9 %collective-permute-start.3 = (bf16[128,256]{1,0:T(8,128)(2,1)S(1)}, bf16[128,256]{1,0:T(8,128)(2,1)S(1)}, u32[]{:S(2)}, u32[]{:S(2)}) collective-permute-start(bf16[128,256]{1,0:T(8,128)(2,1)S(1)} %get-tuple-element.31), channel_id=1, source_target_pairs={{0,3},{1,2},{2,1},{3,0},{4,7},{5,6},{6,5},{7,4},{8,11},{9,10},{10,... | collective-permute-start | bytes 196616 | tf_op jit(solution)/shard_map/ppermute | solution.py:200
  12.9 0.6 %collective-permute-start.5 = (bf16[128,256]{1,0:T(8,128)(2,1)S(1)}, bf16[128,256]{1,0:T(8,128)(2,1)S(1)}, u32[]{:S(2)}, u32[]{:S(2)}) collective-permute-start(bf16[128,256]{1,0:T(8,128)(2,1)S(1)} %get-tuple-element.33), channel_id=1, source_target_pairs={{0,1},{1,0},{2,3},{3,2},{4,5},{5,4},{6,7},{7,6},{8,9},{9,8},{10,11... | collective-permute-start | bytes 196616 | tf_op jit(solution)/shard_map/ppermute | solution.py:200
  13.5 0.8 %shard_map.99.matrix_ref = bf16[512,512]{1,0:T(8,128)(2,1)S(1)} custom-call(s32[1,1,2,8]{3,2,1,0:T(2,128)S(1)} %copy-done.4, s32[8,128]{1,0:T(8,128)S(1)} %get-tuple-element.29.used_ref, bf16[1,1,8,128,128]{4,3,2,1,0:T(8,128)(2,1)S(1)} %copy-done.1, bf16[128,256]{1,0:T(8,128)(2,1)S(1)} %get-tuple-element.40.rest_0_.rest_3_), custom_call_target="tpu_custom_call" | custom-call | tf_op jit(solution)/shard_map/pallas_call | solution.py:234
  14.3 3.8 %collective-permute-start.11 = (bf16[272,128]{1,0:T(8,128)(2,1)S(1)}, bf16[272,128]{1,0:T(8,128)(2,1)S(1)}, u32[]{:S(2)}, u32[]{:S(2)}) collective-permute-start(bf16[272,128]{1,0:T(8,128)(2,1)S(1)} %shard_map.98.rest_3_), channel_id=1, source_target_pairs={{0,3},{1,2},{2,1},{3,0},{4,7},{5,6},{6,5},{7,4},{8,11},{9,10},{10,... | collective-permute-start | bytes 208904 | tf_op jit(solution)/shard_map/ppermute | solution.py:220
  18.1 1.7 %collective-permute-done.4.rest_1_ = bf16[128,256]{1,0:T(8,128)(2,1)S(1)} collective-permute-done((bf16[128,256]{1,0:T(8,128)(2,1)S(1)}, bf16[128,256]{1,0:T(8,128)(2,1)S(1)}, u32[]{:S(2)}, u32[]{:S(2)}) %collective-permute-start.4) | collective-permute-done | bytes 65568 | tf_op jit(solution)/shard_map/ppermute | solution.py:200
  19.9 2.9 %collective-permute-start.9 = (bf16[128,256]{1,0:T(8,128)(2,1)S(1)}, bf16[128,256]{1,0:T(8,128)(2,1)S(1)}, u32[]{:S(2)}, u32[]{:S(2)}) collective-permute-start(bf16[128,256]{1,0:T(8,128)(2,1)S(1)} %shard_map.100.rest_0_), channel_id=1, source_target_pairs={{0,3},{1,2},{2,1},{3,0},{4,7},{5,6},{6,5},{7,4},{8,11},{9,10},{10,... | collective-permute-start | bytes 196616 | tf_op jit(solution)/shard_map/ppermute | solution.py:200
  22.8 1.5 %collective-permute-start.7 = (bf16[128,256]{1,0:T(8,128)(2,1)S(1)}, bf16[128,256]{1,0:T(8,128)(2,1)S(1)}, u32[]{:S(2)}, u32[]{:S(2)}) collective-permute-start(bf16[128,256]{1,0:T(8,128)(2,1)S(1)} %shard_map.100.rest_0_), channel_id=1, source_target_pairs={{0,2},{1,3},{2,0},{3,1},{4,6},{5,7},{6,4},{7,5},{8,10},{9,11},{10,... | collective-permute-start | bytes 196616 | tf_op jit(solution)/shard_map/ppermute | solution.py:200
  24.4 2.0 %collective-permute-done.9.rest_2_ = bf16[128,256]{1,0:T(8,128)(2,1)S(1)} collective-permute-done((bf16[128,256]{1,0:T(8,128)(2,1)S(1)}, bf16[128,256]{1,0:T(8,128)(2,1)S(1)}, u32[]{:S(2)}, u32[]{:S(2)}) %collective-permute-start.9) | collective-permute-done | bytes 65568 | tf_op jit(solution)/shard_map/ppermute | solution.py:200
  26.3 0.7 %collective-permute-done.8.rest_1_ = bf16[128,256]{1,0:T(8,128)(2,1)S(1)} collective-permute-done((bf16[128,256]{1,0:T(8,128)(2,1)S(1)}, bf16[128,256]{1,0:T(8,128)(2,1)S(1)}, u32[]{:S(2)}, u32[]{:S(2)}) %collective-permute-start.8) | collective-permute-done | bytes 65568 | tf_op jit(solution)/shard_map/ppermute | solution.py:200
  27.1 0.7 %shard_map.101 = (bf16[128,256]{1,0:T(8,128)(2,1)S(1)}, f32[512,256]{1,0:T(8,128)S(1)}, f32[256,256]{1,0:T(8,128)S(1)}) custom-call(bf16[256,256]{1,0:T(8,128)(2,1)S(1)} %copy-done, bf16[512,512]{1,0:T(8,128)(2,1)S(1)} %shard_map.99.matrix_ref, bf16[128,256]{1,0:T(8,128)(2,1)S(1)} %shard_map.100.rest_0_, ...), custom_call_target="tpu_custom_call" | custom-call | tf_op jit(solution)/shard_map/pallas_call | solution.py:253
  27.8 0.2 collective-permute-done.7.panel
  28.0 0.5 %shard_map.102 = (f32[256,256]{1,0:T(8,128)S(1)}, f32[128,256]{1,0:T(8,128)S(1)}, bf16[384,256]{1,0:T(8,128)(2,1)S(1)}) custom-call(bf16[256,256]{1,0:T(8,128)(2,1)S(1)} %copy-done, bf16[512,512]{1,0:T(8,128)(2,1)S(1)} %shard_map.99.matrix_ref, bf16[128,256]{1,0:T(8,128)(2,1)S(1)} %collective-permute-done.7.panel, ...), custom_call_target="tpu_custom_call" | custom-call | tf_op jit(solution)/shard_map/pallas_call | solution.py:264
  28.6 1.4 %collective-permute-done.12.got_ref.term_got_ref = bf16[384,256]{1,0:T(8,128)(2,1)S(1)} collective-permute-done((bf16[384,256]{1,0:T(8,128)(2,1)S(1)}, bf16[384,256]{1,0:T(8,128)(2,1)S(1)}, u32[]{:S(2)}, u32[]{:S(2)}) %collective-permute-start.12) | collective-permute-done | bytes 196640 | tf_op jit(solution)/shard_map/ppermute | solution.py:276
  30.0 1.9 %collective-permute-start.14 = (bf16[128,256]{1,0:T(8,128)(2,1)S(1)}, bf16[128,256]{1,0:T(8,128)(2,1)S(1)}, u32[]{:S(2)}, u32[]{:S(2)}) collective-permute-start(bf16[128,256]{1,0:T(8,128)(2,1)S(1)} %get-tuple-element.51.own_ref), channel_id=1, source_target_pairs={{0,8},{4,12},{8,0},{12,4},{1,9},{5,13},{9,1},{13,5},{2,10},{6,14},... | collective-permute-start | bytes 196616 | tf_op jit(solution)/shard_map/ppermute | solution.py:276
  31.9 0.2 collective-permute-start.13
  32.1 2.3 %collective-permute-done.14.got_ref = bf16[128,256]{1,0:T(8,128)(2,1)S(1)} collective-permute-done((bf16[128,256]{1,0:T(8,128)(2,1)S(1)}, bf16[128,256]{1,0:T(8,128)(2,1)S(1)}, u32[]{:S(2)}, u32[]{:S(2)}) %collective-permute-start.14) | collective-permute-done | bytes 65568 | tf_op jit(solution)/shard_map/ppermute | solution.py:276
  34.5 1.6 %collective-permute-done.13.got_ref = bf16[128,256]{1,0:T(8,128)(2,1)S(1)} collective-permute-done((bf16[128,256]{1,0:T(8,128)(2,1)S(1)}, bf16[128,256]{1,0:T(8,128)(2,1)S(1)}, u32[]{:S(2)}, u32[]{:S(2)}) %collective-permute-start.13) | collective-permute-done | bytes 65568 | tf_op jit(solution)/shard_map/ppermute | solution.py:276
  36.2 0.8 %shard_map.105 = (bf16[128,256]{1,0:T(8,128)(2,1)}, bf16[128,256]{1,0:T(8,128)(2,1)}, f32[256,256]{1,0:T(8,128)}) custom-call(s32[128]{0:T(128)S(1)} %copy-done.3, bf16[256,256]{1,0:T(8,128)(2,1)S(1)} %copy-done, f32[128,256]{1,0:T(8,128)S(1)} %get-tuple-element.48.keep_ref, bf16[128,256]{1,0:T(8,128)(2,1)S(1)} %collective-permute-done.13.got_ref, ...), custom_call_target="tpu_custom_call" | custom-call | tf_op jit(solution)/shard_map/pallas_call | solution.py:300
  (32 shorter events, 0.7 us)
Async XLA Ops:
  0.6 0.8 %copy-start.5 = (bf16[128,256]{1,0:T(8,128)(2,1)S(1)}, bf16[128,256]{1,0:T(8,128)(2,1)}, u32[]{:S(2)}) copy-start(bf16[128,256]{1,0:T(8,128)(2,1)} %x_ref.1) | copy-start | bytes 196612
  0.6 0.8 %copy-start.3 = (s32[128]{0:T(128)S(1)}, s32[128]{0:T(128)}, u32[]{:S(2)}) copy-start(s32[128]{0:T(128)} %deg_ref.7) | copy-start | bytes 1540
  1.5 3.2 %copy-start.2 = (bf16[128,256]{1,0:T(8,128)(2,1)S(1)}, bf16[128,256]{1,0:T(8,128)(2,1)}, u32[]{:S(2)}) copy-start(bf16[128,256]{1,0:T(8,128)(2,1)} %cot_ref.1) | copy-start | bytes 196612
  1.5 6.2 %copy-start.1 = (bf16[1,1,8,128,128]{4,3,2,1,0:T(8,128)(2,1)S(1)}, bf16[1,1,8,128,128]{4,3,2,1,0:T(8,128)(2,1)}, u32[]{:S(2)}) copy-start(bf16[1,1,8,128,128]{4,3,2,1,0:T(8,128)(2,1)} %values_ref.3) | copy-start | bytes 786436
  1.6 6.8 %collective-permute-start.2 = (bf16[128,256]{1,0:T(8,128)(2,1)S(1)}, bf16[128,256]{1,0:T(8,128)(2,1)S(1)}, u32[]{:S(2)}, u32[]{:S(2)}) collective-permute-start(bf16[128,256]{1,0:T(8,128)(2,1)S(1)} %get-tuple-element.30.rest_0_), channel_id=1, source_target_pairs={{0,12},{4,8},{8,4},{12,0},{1,13},{5,9},{9,5},{13,1},{2,14},{6,10},... | collective-permute-start | bytes 196616 | tf_op jit(solution)/shard_map/ppermute | solution.py:200
  4.0 4.7 %collective-permute-start.1 = (bf16[128,256]{1,0:T(8,128)(2,1)S(1)}, bf16[128,256]{1,0:T(8,128)(2,1)S(1)}, u32[]{:S(2)}, u32[]{:S(2)}) collective-permute-start(bf16[128,256]{1,0:T(8,128)(2,1)S(1)} %get-tuple-element.30.rest_0_), channel_id=1, source_target_pairs={{0,8},{4,12},{8,0},{12,4},{1,9},{5,13},{9,1},{13,5},{2,10},{6,14},... | collective-permute-start | bytes 196616 | tf_op jit(solution)/shard_map/ppermute | solution.py:200
  4.7 4.0 %collective-permute-start = (bf16[128,256]{1,0:T(8,128)(2,1)S(1)}, bf16[128,256]{1,0:T(8,128)(2,1)S(1)}, u32[]{:S(2)}, u32[]{:S(2)}) collective-permute-start(bf16[128,256]{1,0:T(8,128)(2,1)S(1)} %get-tuple-element.30.rest_0_), channel_id=1, source_target_pairs={{0,4},{4,0},{8,12},{12,8},{1,5},{5,1},{9,13},{13,9},{2,6},{6,2},{1... | collective-permute-start | bytes 196616 | tf_op jit(solution)/shard_map/ppermute | solution.py:200
  4.7 2.9 %copy-start.4 = (s32[1,1,2,8]{3,2,1,0:T(2,128)S(1)}, s32[1,1,2,8]{3,2,1,0:T(2,128)}, u32[]{:S(2)}) copy-start(s32[1,1,2,8]{3,2,1,0:T(2,128)} %idx_ref.3) | copy-start | bytes 196
  4.7 13.4 %collective-permute-start.6 = (bf16[272,128]{1,0:T(8,128)(2,1)S(1)}, bf16[272,128]{1,0:T(8,128)(2,1)S(1)}, u32[]{:S(2)}, u32[]{:S(2)}) collective-permute-start(bf16[272,128]{1,0:T(8,128)(2,1)S(1)} %shard_map.98.rest_3_), channel_id=1, source_target_pairs={{0,2},{1,3},{2,0},{3,1},{4,6},{5,7},{6,4},{7,5},{8,10},{9,11},{10,... | collective-permute-start | bytes 208904 | tf_op jit(solution)/shard_map/ppermute | solution.py:220
  9.0 9.1 %collective-permute-start.3 = (bf16[128,256]{1,0:T(8,128)(2,1)S(1)}, bf16[128,256]{1,0:T(8,128)(2,1)S(1)}, u32[]{:S(2)}, u32[]{:S(2)}) collective-permute-start(bf16[128,256]{1,0:T(8,128)(2,1)S(1)} %get-tuple-element.31), channel_id=1, source_target_pairs={{0,3},{1,2},{2,1},{3,0},{4,7},{5,6},{6,5},{7,4},{8,11},{9,10},{10,... | collective-permute-start | bytes 196616 | tf_op jit(solution)/shard_map/ppermute | solution.py:200
  12.9 6.9 %collective-permute-start.4 = (bf16[128,256]{1,0:T(8,128)(2,1)S(1)}, bf16[128,256]{1,0:T(8,128)(2,1)S(1)}, u32[]{:S(2)}, u32[]{:S(2)}) collective-permute-start(bf16[128,256]{1,0:T(8,128)(2,1)S(1)} %get-tuple-element.32), channel_id=1, source_target_pairs={{0,2},{1,3},{2,0},{3,1},{4,6},{5,7},{6,4},{7,5},{8,10},{9,11},{10,... | collective-permute-start | bytes 196616 | tf_op jit(solution)/shard_map/ppermute | solution.py:200
  12.9 6.9 %collective-permute-start.5 = (bf16[128,256]{1,0:T(8,128)(2,1)S(1)}, bf16[128,256]{1,0:T(8,128)(2,1)S(1)}, u32[]{:S(2)}, u32[]{:S(2)}) collective-permute-start(bf16[128,256]{1,0:T(8,128)(2,1)S(1)} %get-tuple-element.33), channel_id=1, source_target_pairs={{0,1},{1,0},{2,3},{3,2},{4,5},{5,4},{6,7},{7,6},{8,9},{9,8},{10,11... | collective-permute-start | bytes 196616 | tf_op jit(solution)/shard_map/ppermute | solution.py:200
  14.3 12.8 %copy-start = (bf16[256,256]{1,0:T(8,128)(2,1)S(1)}, bf16[256,256]{1,0:T(8,128)(2,1)}, u32[]{:S(2)}) copy-start(bf16[256,256]{1,0:T(8,128)(2,1)} %weight_ref.5) | copy-start | bytes 393220
  14.3 10.1 %collective-permute-start.11 = (bf16[272,128]{1,0:T(8,128)(2,1)S(1)}, bf16[272,128]{1,0:T(8,128)(2,1)S(1)}, u32[]{:S(2)}, u32[]{:S(2)}) collective-permute-start(bf16[272,128]{1,0:T(8,128)(2,1)S(1)} %shard_map.98.rest_3_), channel_id=1, source_target_pairs={{0,3},{1,2},{2,1},{3,0},{4,7},{5,6},{6,5},{7,4},{8,11},{9,10},{10,... | collective-permute-start | bytes 208904 | tf_op jit(solution)/shard_map/ppermute | solution.py:220
  18.1 6.2 %collective-permute-start.10 = (bf16[272,128]{1,0:T(8,128)(2,1)S(1)}, bf16[272,128]{1,0:T(8,128)(2,1)S(1)}, u32[]{:S(2)}, u32[]{:S(2)}) collective-permute-start(bf16[272,128]{1,0:T(8,128)(2,1)S(1)} %shard_map.98.rest_3_), channel_id=1, source_target_pairs={{0,1},{1,0},{2,3},{3,2},{4,5},{5,4},{6,7},{7,6},{8,9},{9,8},{10,11... | collective-permute-start | bytes 208904 | tf_op jit(solution)/shard_map/ppermute | solution.py:220
  19.9 6.4 %collective-permute-start.9 = (bf16[128,256]{1,0:T(8,128)(2,1)S(1)}, bf16[128,256]{1,0:T(8,128)(2,1)S(1)}, u32[]{:S(2)}, u32[]{:S(2)}) collective-permute-start(bf16[128,256]{1,0:T(8,128)(2,1)S(1)} %shard_map.100.rest_0_), channel_id=1, source_target_pairs={{0,3},{1,2},{2,1},{3,0},{4,7},{5,6},{6,5},{7,4},{8,11},{9,10},{10,... | collective-permute-start | bytes 196616 | tf_op jit(solution)/shard_map/ppermute | solution.py:200
  22.8 4.3 %collective-permute-start.8 = (bf16[128,256]{1,0:T(8,128)(2,1)S(1)}, bf16[128,256]{1,0:T(8,128)(2,1)S(1)}, u32[]{:S(2)}, u32[]{:S(2)}) collective-permute-start(bf16[128,256]{1,0:T(8,128)(2,1)S(1)} %shard_map.100.rest_0_), channel_id=1, source_target_pairs={{0,1},{1,0},{2,3},{3,2},{4,5},{5,4},{6,7},{7,6},{8,9},{9,8},{10,11... | collective-permute-start | bytes 196616 | tf_op jit(solution)/shard_map/ppermute | solution.py:200
  22.8 5.2 %collective-permute-start.7 = (bf16[128,256]{1,0:T(8,128)(2,1)S(1)}, bf16[128,256]{1,0:T(8,128)(2,1)S(1)}, u32[]{:S(2)}, u32[]{:S(2)}) collective-permute-start(bf16[128,256]{1,0:T(8,128)(2,1)S(1)} %shard_map.100.rest_0_), channel_id=1, source_target_pairs={{0,2},{1,3},{2,0},{3,1},{4,6},{5,7},{6,4},{7,5},{8,10},{9,11},{10,... | collective-permute-start | bytes 196616 | tf_op jit(solution)/shard_map/ppermute | solution.py:200
  28.5 1.5 %collective-permute-start.12 = (bf16[384,256]{1,0:T(8,128)(2,1)S(1)}, bf16[384,256]{1,0:T(8,128)(2,1)S(1)}, u32[]{:S(2)}, u32[]{:S(2)}) collective-permute-start(bf16[384,256]{1,0:T(8,128)(2,1)S(1)} %get-tuple-element.47), channel_id=1, source_target_pairs={{0,4},{4,0},{8,12},{12,8},{1,5},{5,1},{9,13},{13,9},{2,6},{6,2},{1... | collective-permute-start | bytes 589832 | tf_op jit(solution)/shard_map/ppermute | solution.py:276
  30.0 4.4 %collective-permute-start.14 = (bf16[128,256]{1,0:T(8,128)(2,1)S(1)}, bf16[128,256]{1,0:T(8,128)(2,1)S(1)}, u32[]{:S(2)}, u32[]{:S(2)}) collective-permute-start(bf16[128,256]{1,0:T(8,128)(2,1)S(1)} %get-tuple-element.51.own_ref), channel_id=1, source_target_pairs={{0,8},{4,12},{8,0},{12,4},{1,9},{5,13},{9,1},{13,5},{2,10},{6,14},... | collective-permute-start | bytes 196616 | tf_op jit(solution)/shard_map/ppermute | solution.py:276
  31.9 4.3 %collective-permute-start.13 = (bf16[128,256]{1,0:T(8,128)(2,1)S(1)}, bf16[128,256]{1,0:T(8,128)(2,1)S(1)}, u32[]{:S(2)}, u32[]{:S(2)}) collective-permute-start(bf16[128,256]{1,0:T(8,128)(2,1)S(1)} %get-tuple-element.49), channel_id=1, source_target_pairs={{0,8},{4,12},{8,0},{12,4},{1,9},{5,13},{9,1},{13,5},{2,10},{6,14},... | collective-permute-start | bytes 196616 | tf_op jit(solution)/shard_map/ppermute | solution.py:276
  34.5 1.7 %collective-permute-start.15 = (bf16[128,256]{1,0:T(8,128)(2,1)S(1)}, bf16[128,256]{1,0:T(8,128)(2,1)S(1)}, u32[]{:S(2)}, u32[]{:S(2)}) collective-permute-start(bf16[128,256]{1,0:T(8,128)(2,1)S(1)} %shard_map.104.own_ref), channel_id=1, source_target_pairs={{0,4},{4,0},{8,12},{12,8},{1,5},{5,1},{9,13},{13,9},{2,6},{6,2},{1... | collective-permute-start | bytes 196616 | tf_op jit(solution)/shard_map/ppermute | solution.py:276

commit v8 on v7

--- a/solution.py
+++ b/solution.py
@@ -93,7 +93,7 @@
 
 def gradient_rows(panel, extra, weight):
     width = weight.shape[0]
-    scale = wide(row_scale(extra[width : width + 1, :]), width)
+    scale = wide(row_scale(extra[width : width + 16, :][:1]), width)
     aggregated = panel[...]
     pre_act = jnp.dot(aggregated, weight, preferred_element_type=F32)
     sig = 1.0 / (1.0 + jnp.exp(-pre_act))
@@ -215,14 +215,15 @@
         shape((n_cols * TILE, n_rows * TILE), BF16),
         [smem, vmem, vmem],
     )(tile_index, used, tile_values)
-    blocks = shifted(scaled, "rows", n_rows)
+    blocks = [scaled] + [
+        lax.ppermute(scaled, "rows", [(i, i ^ shift) for i in range(n_rows)])
+        for shift in range(1, n_rows)
+    ]
     def sent(block, shift):
         return lax.ppermute(block, "cols", [(j, j ^ shift) for j in range(n_cols)])
 
-    late = [shift for shift in range(1, n_cols) if shift != 2]
-    early = [shift for shift in range(1, n_cols) if shift == 2]
     extras = [extra] + [None] * (n_cols - 1)
-    for shift in reversed(early):
+    for shift in range(2, n_cols, 2):
         extras[shift] = sent(extra, shift)
     parts = call(
         functools.partial(forward_kernel, n_rows, n_cols),
@@ -237,10 +238,13 @@
         [smem, vmem, vmem, pl.ANY],
     )(tile_index, used, tile_values, parts[0])
     sums = shifted(parts, "cols", n_cols)
-    back_matrix, tied = lax.optimization_barrier((back_matrix, extra))
-    for shift in reversed(late):
-        extras[shift] = sent(tied, shift)
-    held = [extras[shift] for shift in early]
+    early = list(range(2, n_cols, 2))
+    back_matrix, tied, held = lax.optimization_barrier(
+        (back_matrix, extra, [extras[shift] for shift in early])
+    )
+    extras[1] = sent(tied, 1)
+    for shift, block in zip(early, held):
+        extras[shift + 1] = sent(block, 1)
     sums, held, back_matrix = lax.optimization_barrier((sums[::-1], held, back_matrix))
     for shift, block in zip(early, held):
         extras[shift] = block

time: 37.2 us -> 36.3 us (0.976)
  starting transfers between devices: 21 us -> 19.3 us
  waiting for transfers between devices: 10.3 us -> 11.1 us
    ppermute x9 -> x6, starting transfers between devices: 12.1 us -> 8.96 us  [shifted(): lax.ppermute(source, axis, [(i, i ^ shift) for i in range(size)])]
    ppermute x0 -> x3, starting transfers between devices: none -> 3.12 us  [shards(): lax.ppermute(scaled, 'rows', [(i, i ^ shift) for i in range(n_rows)])]
    ppermute x3, starting transfers between devices: 6.72 us -> 5 us  [sent(): return lax.ppermute(block, 'cols', [(j, j ^ shift) for j in range(n_cols)])]
    ppermute x9 -> x6, waiting for transfers between devices: 4.94 us -> 5.5 us  [shifted(): lax.ppermute(source, axis, [(i, i ^ shift) for i in range(size)])]
  transfers between devices with their start and end apart: 16 -> 16, of which waited for: 8 -> 9; matrix products, arithmetic and copies ran while one was open for 0% -> 0% of each run, Pallas kernels for 7% -> 7%
where the time goes in v8:
time: 36.3 us; the launch traced here: 36.1 us
  starting transfers between devices  19.3 us (53%)
  waiting for transfers between devices  11.1 us (31%)
  Pallas kernels  4.08 us (11%)
  between operations  1.45 us (4%)
    ppermute x6, starting transfers between devices, shifted(): lax.ppermute(source, axis, [(i, i ^ shift) for i in range(size)])  8.96 us
    ppermute x6, waiting for transfers between devices, shifted(): lax.ppermute(source, axis, [(i, i ^ shift) for i in range(size)])  5.5 us
    ppermute x4, waiting for transfers between devices, partner(): return lax.ppermute(block, 'rows', [(i, i ^ mask) for i in range(n_rows)])  5.26 us
    ppermute x3, starting transfers between devices, sent(): return lax.ppermute(block, 'cols', [(j, j ^ shift) for j in range(n_cols)])  5 us
    ppermute x3, starting transfers between devices, shards(): lax.ppermute(scaled, 'rows', [(i, i ^ shift) for i in range(n_rows)])  3.12 us
    ppermute x4, starting transfers between devices, partner(): return lax.ppermute(block, 'rows', [(i, i ^ mask) for i in range(n_rows)])  2.23 us
    pallas_call x1, Pallas kernels, shards(): call(last_kernel, (block_shape, block_shape, shape((width, width), F32)),...  0.85 us
    pallas_call x1, Pallas kernels, shards(): call(functools.partial(block_kernel, True, n_rows, n_cols), shape((n_rows...  0.75 us
  transfers between devices with their start and end apart: 16, of which 9 were waited for; matrix products, arithmetic and copies ran while one was open for 0% of the time, Pallas kernels for 7%

profile of v8, /device:TPU:0, one launch (start us, length us, event | category | flops | bytes accessed | tf_op | source)
XLA Modules:
  0.0 36.1 jit_solution(10057508974833127082)
XLA Ops:
  1.6 2.4 %collective-permute-start.2 = (bf16[128,256]{1,0:T(8,128)(2,1)S(1)}, bf16[128,256]{1,0:T(8,128)(2,1)S(1)}, u32[]{:S(2)}, u32[]{:S(2)}) collective-permute-start(bf16[128,256]{1,0:T(8,128)(2,1)S(1)} %get-tuple-element.31.rest_0_), channel_id=1, source_target_pairs={{0,12},{4,8},{8,4},{12,0},{1,13},{5,9},{9,5},{13,1},{2,14},{6,10},... | collective-permute-start | bytes 196616 | tf_op jit(solution)/shard_map/ppermute | solution.py:219
  4.0 0.6 %collective-permute-start.1 = (bf16[128,256]{1,0:T(8,128)(2,1)S(1)}, bf16[128,256]{1,0:T(8,128)(2,1)S(1)}, u32[]{:S(2)}, u32[]{:S(2)}) collective-permute-start(bf16[128,256]{1,0:T(8,128)(2,1)S(1)} %get-tuple-element.31.rest_0_), channel_id=1, source_target_pairs={{0,8},{4,12},{8,0},{12,4},{1,9},{5,13},{9,1},{13,5},{2,10},{6,14},... | collective-permute-start | bytes 196616 | tf_op jit(solution)/shard_map/ppermute | solution.py:219
  4.7 2.9 %collective-permute-start.6 = (bf16[272,128]{1,0:T(8,128)(2,1)S(1)}, bf16[272,128]{1,0:T(8,128)(2,1)S(1)}, u32[]{:S(2)}, u32[]{:S(2)}) collective-permute-start(bf16[272,128]{1,0:T(8,128)(2,1)S(1)} %shard_map.99.rest_3_), channel_id=1, source_target_pairs={{0,2},{1,3},{2,0},{3,1},{4,6},{5,7},{6,4},{7,5},{8,10},{9,11},{10,... | collective-permute-start | bytes 208904 | tf_op jit(solution)/shard_map/ppermute | solution.py:223
  7.7 0.7 %shard_map.96.matrix_ref = bf16[512,512]{1,0:T(8,128)(2,1)S(1)} custom-call(s32[1,1,2,8]{3,2,1,0:T(2,128)S(1)} %copy-done.4, s32[8,128]{1,0:T(8,128)S(1)} %get-tuple-element.30.used_ref, bf16[1,1,8,128,128]{4,3,2,1,0:T(8,128)(2,1)S(1)} %copy-done.1), custom_call_target="tpu_custom_call" | custom-call | tf_op jit(solution)/shard_map/pallas_call | solution.py:213
  8.4 0.3 collective-permute-done.1.rest_2_
  9.0 3.9 %collective-permute-start.3 = (bf16[128,256]{1,0:T(8,128)(2,1)S(1)}, bf16[128,256]{1,0:T(8,128)(2,1)S(1)}, u32[]{:S(2)}, u32[]{:S(2)}) collective-permute-start(bf16[128,256]{1,0:T(8,128)(2,1)S(1)} %get-tuple-element.32), channel_id=1, source_target_pairs={{0,3},{1,2},{2,1},{3,0},{4,7},{5,6},{6,5},{7,4},{8,11},{9,10},{10,... | collective-permute-start | bytes 196616 | tf_op jit(solution)/shard_map/ppermute | solution.py:200
  12.9 0.6 %collective-permute-start.5 = (bf16[128,256]{1,0:T(8,128)(2,1)S(1)}, bf16[128,256]{1,0:T(8,128)(2,1)S(1)}, u32[]{:S(2)}, u32[]{:S(2)}) collective-permute-start(bf16[128,256]{1,0:T(8,128)(2,1)S(1)} %get-tuple-element.34), channel_id=1, source_target_pairs={{0,1},{1,0},{2,3},{3,2},{4,5},{5,4},{6,7},{7,6},{8,9},{9,8},{10,11... | collective-permute-start | bytes 196616 | tf_op jit(solution)/shard_map/ppermute | solution.py:200
  13.5 0.8 %shard_map.98.matrix_ref = bf16[512,512]{1,0:T(8,128)(2,1)S(1)} custom-call(s32[1,1,2,8]{3,2,1,0:T(2,128)S(1)} %copy-done.4, s32[8,128]{1,0:T(8,128)S(1)} %get-tuple-element.30.used_ref, bf16[1,1,8,128,128]{4,3,2,1,0:T(8,128)(2,1)S(1)} %copy-done.1, bf16[128,256]{1,0:T(8,128)(2,1)S(1)} %get-tuple-element.42.rest_0_.rest_3_), custom_call_target="tpu_custom_call" | custom-call | tf_op jit(solution)/shard_map/pallas_call | solution.py:235
  14.3 1.5 %collective-permute-start.10 = (bf16[272,128]{1,0:T(8,128)(2,1)S(1)}, bf16[272,128]{1,0:T(8,128)(2,1)S(1)}, u32[]{:S(2)}, u32[]{:S(2)}) collective-permute-start(bf16[272,128]{1,0:T(8,128)(2,1)S(1)} %shard_map.99.rest_3_), channel_id=1, source_target_pairs={{0,1},{1,0},{2,3},{3,2},{4,5},{5,4},{6,7},{7,6},{8,9},{9,8},{10,11... | collective-permute-start | bytes 208904 | tf_op jit(solution)/shard_map/ppermute | solution.py:223
  15.8 0.6 %collective-permute-start.11 = (bf16[272,128]{1,0:T(8,128)(2,1)S(1)}, bf16[272,128]{1,0:T(8,128)(2,1)S(1)}, u32[]{:S(2)}, u32[]{:S(2)}) collective-permute-start(bf16[272,128]{1,0:T(8,128)(2,1)S(1)} %collective-permute-done.6.extra), channel_id=1, source_target_pairs={{0,1},{1,0},{2,3},{3,2},{4,5},{5,4},{6,7},{7,6},{8,9},{9,8},{10,11... | collective-permute-start | bytes 208904 | tf_op jit(solution)/shard_map/ppermute | solution.py:223
  16.4 2.3 %collective-permute-done.4.rest_1_ = bf16[128,256]{1,0:T(8,128)(2,1)S(1)} collective-permute-done((bf16[128,256]{1,0:T(8,128)(2,1)S(1)}, bf16[128,256]{1,0:T(8,128)(2,1)S(1)}, u32[]{:S(2)}, u32[]{:S(2)}) %collective-permute-start.4) | collective-permute-done | bytes 65568 | tf_op jit(solution)/shard_map/ppermute | solution.py:200
  18.7 0.4 %collective-permute-done.5.rest_2_ = bf16[128,256]{1,0:T(8,128)(2,1)S(1)} collective-permute-done((bf16[128,256]{1,0:T(8,128)(2,1)S(1)}, bf16[128,256]{1,0:T(8,128)(2,1)S(1)}, u32[]{:S(2)}, u32[]{:S(2)}) %collective-permute-start.5) | collective-permute-done | bytes 65568 | tf_op jit(solution)/shard_map/ppermute | solution.py:200
  19.2 2.5 %collective-permute-start.9 = (bf16[128,256]{1,0:T(8,128)(2,1)S(1)}, bf16[128,256]{1,0:T(8,128)(2,1)S(1)}, u32[]{:S(2)}, u32[]{:S(2)}) collective-permute-start(bf16[128,256]{1,0:T(8,128)(2,1)S(1)} %shard_map.100.rest_0_), channel_id=1, source_target_pairs={{0,3},{1,2},{2,1},{3,0},{4,7},{5,6},{6,5},{7,4},{8,11},{9,10},{10,... | collective-permute-start | bytes 196616 | tf_op jit(solution)/shard_map/ppermute | solution.py:200
  21.7 2.0 %collective-permute-start.7 = (bf16[128,256]{1,0:T(8,128)(2,1)S(1)}, bf16[128,256]{1,0:T(8,128)(2,1)S(1)}, u32[]{:S(2)}, u32[]{:S(2)}) collective-permute-start(bf16[128,256]{1,0:T(8,128)(2,1)S(1)} %shard_map.100.rest_0_), channel_id=1, source_target_pairs={{0,2},{1,3},{2,0},{3,1},{4,6},{5,7},{6,4},{7,5},{8,10},{9,11},{10,... | collective-permute-start | bytes 196616 | tf_op jit(solution)/shard_map/ppermute | solution.py:200
  23.7 2.3 %collective-permute-done.9.rest_2_ = bf16[128,256]{1,0:T(8,128)(2,1)S(1)} collective-permute-done((bf16[128,256]{1,0:T(8,128)(2,1)S(1)}, bf16[128,256]{1,0:T(8,128)(2,1)S(1)}, u32[]{:S(2)}, u32[]{:S(2)}) %collective-permute-start.9) | collective-permute-done | bytes 65568 | tf_op jit(solution)/shard_map/ppermute | solution.py:200
  26.0 0.4 %collective-permute-done.8.rest_1_ = bf16[128,256]{1,0:T(8,128)(2,1)S(1)} collective-permute-done((bf16[128,256]{1,0:T(8,128)(2,1)S(1)}, bf16[128,256]{1,0:T(8,128)(2,1)S(1)}, u32[]{:S(2)}, u32[]{:S(2)}) %collective-permute-start.8) | collective-permute-done | bytes 65568 | tf_op jit(solution)/shard_map/ppermute | solution.py:200
  26.4 0.7 %shard_map.101 = (bf16[128,256]{1,0:T(8,128)(2,1)S(1)}, f32[512,256]{1,0:T(8,128)S(1)}, f32[256,256]{1,0:T(8,128)S(1)}) custom-call(bf16[256,256]{1,0:T(8,128)(2,1)S(1)} %copy-done, bf16[512,512]{1,0:T(8,128)(2,1)S(1)} %shard_map.98.matrix_ref, bf16[128,256]{1,0:T(8,128)(2,1)S(1)} %shard_map.100.rest_0_, ...), custom_call_target="tpu_custom_call" | custom-call | tf_op jit(solution)/shard_map/pallas_call | solution.py:257
  27.2 0.5 %shard_map.102 = (f32[256,256]{1,0:T(8,128)S(1)}, f32[128,256]{1,0:T(8,128)S(1)}, bf16[384,256]{1,0:T(8,128)(2,1)S(1)}) custom-call(bf16[256,256]{1,0:T(8,128)(2,1)S(1)} %copy-done, bf16[512,512]{1,0:T(8,128)(2,1)S(1)} %shard_map.98.matrix_ref, bf16[128,256]{1,0:T(8,128)(2,1)S(1)} %collective-permute-done.7.panel, ...), custom_call_target="tpu_custom_call" | custom-call | tf_op jit(solution)/shard_map/pallas_call | solution.py:268
  27.8 1.4 %collective-permute-done.12.got_ref.term_got_ref = bf16[384,256]{1,0:T(8,128)(2,1)S(1)} collective-permute-done((bf16[384,256]{1,0:T(8,128)(2,1)S(1)}, bf16[384,256]{1,0:T(8,128)(2,1)S(1)}, u32[]{:S(2)}, u32[]{:S(2)}) %collective-permute-start.12) | collective-permute-done | bytes 196640 | tf_op jit(solution)/shard_map/ppermute | solution.py:280
  29.2 1.8 %collective-permute-start.14 = (bf16[128,256]{1,0:T(8,128)(2,1)S(1)}, bf16[128,256]{1,0:T(8,128)(2,1)S(1)}, u32[]{:S(2)}, u32[]{:S(2)}) collective-permute-start(bf16[128,256]{1,0:T(8,128)(2,1)S(1)} %get-tuple-element.53.own_ref), channel_id=1, source_target_pairs={{0,8},{4,12},{8,0},{12,4},{1,9},{5,13},{9,1},{13,5},{2,10},{6,14},... | collective-permute-start | bytes 196616 | tf_op jit(solution)/shard_map/ppermute | solution.py:280
  31.0 0.3 collective-permute-start.13
  31.3 2.4 %collective-permute-done.14.got_ref = bf16[128,256]{1,0:T(8,128)(2,1)S(1)} collective-permute-done((bf16[128,256]{1,0:T(8,128)(2,1)S(1)}, bf16[128,256]{1,0:T(8,128)(2,1)S(1)}, u32[]{:S(2)}, u32[]{:S(2)}) %collective-permute-start.14) | collective-permute-done | bytes 65568 | tf_op jit(solution)/shard_map/ppermute | solution.py:280
  33.9 1.4 %collective-permute-done.13.got_ref = bf16[128,256]{1,0:T(8,128)(2,1)S(1)} collective-permute-done((bf16[128,256]{1,0:T(8,128)(2,1)S(1)}, bf16[128,256]{1,0:T(8,128)(2,1)S(1)}, u32[]{:S(2)}, u32[]{:S(2)}) %collective-permute-start.13) | collective-permute-done | bytes 65568 | tf_op jit(solution)/shard_map/ppermute | solution.py:280
  35.3 0.8 %shard_map.105 = (bf16[128,256]{1,0:T(8,128)(2,1)}, bf16[128,256]{1,0:T(8,128)(2,1)}, f32[256,256]{1,0:T(8,128)}) custom-call(s32[128]{0:T(128)S(1)} %copy-done.3, bf16[256,256]{1,0:T(8,128)(2,1)S(1)} %copy-done, f32[128,256]{1,0:T(8,128)S(1)} %get-tuple-element.50.keep_ref, bf16[128,256]{1,0:T(8,128)(2,1)S(1)} %collective-permute-done.13.got_ref, ...), custom_call_target="tpu_custom_call" | custom-call | tf_op jit(solution)/shard_map/pallas_call | solution.py:304
  (32 shorter events, 1.1 us)
Async XLA Ops:
  0.6 0.8 %copy-start.5 = (bf16[128,256]{1,0:T(8,128)(2,1)S(1)}, bf16[128,256]{1,0:T(8,128)(2,1)}, u32[]{:S(2)}) copy-start(bf16[128,256]{1,0:T(8,128)(2,1)} %x_ref.1) | copy-start | bytes 196612
  0.6 0.8 %copy-start.3 = (s32[128]{0:T(128)S(1)}, s32[128]{0:T(128)}, u32[]{:S(2)}) copy-start(s32[128]{0:T(128)} %deg_ref.7) | copy-start | bytes 1540
  1.5 3.2 %copy-start.2 = (bf16[128,256]{1,0:T(8,128)(2,1)S(1)}, bf16[128,256]{1,0:T(8,128)(2,1)}, u32[]{:S(2)}) copy-start(bf16[128,256]{1,0:T(8,128)(2,1)} %cot_ref.1) | copy-start | bytes 196612
  1.5 6.2 %copy-start.1 = (bf16[1,1,8,128,128]{4,3,2,1,0:T(8,128)(2,1)S(1)}, bf16[1,1,8,128,128]{4,3,2,1,0:T(8,128)(2,1)}, u32[]{:S(2)}) copy-start(bf16[1,1,8,128,128]{4,3,2,1,0:T(8,128)(2,1)} %values_ref.3) | copy-start | bytes 786436
  1.6 6.8 %collective-permute-start.2 = (bf16[128,256]{1,0:T(8,128)(2,1)S(1)}, bf16[128,256]{1,0:T(8,128)(2,1)S(1)}, u32[]{:S(2)}, u32[]{:S(2)}) collective-permute-start(bf16[128,256]{1,0:T(8,128)(2,1)S(1)} %get-tuple-element.31.rest_0_), channel_id=1, source_target_pairs={{0,12},{4,8},{8,4},{12,0},{1,13},{5,9},{9,5},{13,1},{2,14},{6,10},... | collective-permute-start | bytes 196616 | tf_op jit(solution)/shard_map/ppermute | solution.py:219
  4.0 4.7 %collective-permute-start.1 = (bf16[128,256]{1,0:T(8,128)(2,1)S(1)}, bf16[128,256]{1,0:T(8,128)(2,1)S(1)}, u32[]{:S(2)}, u32[]{:S(2)}) collective-permute-start(bf16[128,256]{1,0:T(8,128)(2,1)S(1)} %get-tuple-element.31.rest_0_), channel_id=1, source_target_pairs={{0,8},{4,12},{8,0},{12,4},{1,9},{5,13},{9,1},{13,5},{2,10},{6,14},... | collective-permute-start | bytes 196616 | tf_op jit(solution)/shard_map/ppermute | solution.py:219
  4.7 4.0 %collective-permute-start = (bf16[128,256]{1,0:T(8,128)(2,1)S(1)}, bf16[128,256]{1,0:T(8,128)(2,1)S(1)}, u32[]{:S(2)}, u32[]{:S(2)}) collective-permute-start(bf16[128,256]{1,0:T(8,128)(2,1)S(1)} %get-tuple-element.31.rest_0_), channel_id=1, source_target_pairs={{0,4},{4,0},{8,12},{12,8},{1,5},{5,1},{9,13},{13,9},{2,6},{6,2},{1... | collective-permute-start | bytes 196616 | tf_op jit(solution)/shard_map/ppermute | solution.py:219
  4.7 2.9 %copy-start.4 = (s32[1,1,2,8]{3,2,1,0:T(2,128)S(1)}, s32[1,1,2,8]{3,2,1,0:T(2,128)}, u32[]{:S(2)}) copy-start(s32[1,1,2,8]{3,2,1,0:T(2,128)} %idx_ref.3) | copy-start | bytes 196
  4.7 9.6 %collective-permute-start.6 = (bf16[272,128]{1,0:T(8,128)(2,1)S(1)}, bf16[272,128]{1,0:T(8,128)(2,1)S(1)}, u32[]{:S(2)}, u32[]{:S(2)}) collective-permute-start(bf16[272,128]{1,0:T(8,128)(2,1)S(1)} %shard_map.99.rest_3_), channel_id=1, source_target_pairs={{0,2},{1,3},{2,0},{3,1},{4,6},{5,7},{6,4},{7,5},{8,10},{9,11},{10,... | collective-permute-start | bytes 208904 | tf_op jit(solution)/shard_map/ppermute | solution.py:223
  9.0 7.4 %collective-permute-start.3 = (bf16[128,256]{1,0:T(8,128)(2,1)S(1)}, bf16[128,256]{1,0:T(8,128)(2,1)S(1)}, u32[]{:S(2)}, u32[]{:S(2)}) collective-permute-start(bf16[128,256]{1,0:T(8,128)(2,1)S(1)} %get-tuple-element.32), channel_id=1, source_target_pairs={{0,3},{1,2},{2,1},{3,0},{4,7},{5,6},{6,5},{7,4},{8,11},{9,10},{10,... | collective-permute-start | bytes 196616 | tf_op jit(solution)/shard_map/ppermute | solution.py:200
  12.9 5.8 %collective-permute-start.4 = (bf16[128,256]{1,0:T(8,128)(2,1)S(1)}, bf16[128,256]{1,0:T(8,128)(2,1)S(1)}, u32[]{:S(2)}, u32[]{:S(2)}) collective-permute-start(bf16[128,256]{1,0:T(8,128)(2,1)S(1)} %get-tuple-element.33), channel_id=1, source_target_pairs={{0,2},{1,3},{2,0},{3,1},{4,6},{5,7},{6,4},{7,5},{8,10},{9,11},{10,... | collective-permute-start | bytes 196616 | tf_op jit(solution)/shard_map/ppermute | solution.py:200
  12.9 6.2 %collective-permute-start.5 = (bf16[128,256]{1,0:T(8,128)(2,1)S(1)}, bf16[128,256]{1,0:T(8,128)(2,1)S(1)}, u32[]{:S(2)}, u32[]{:S(2)}) collective-permute-start(bf16[128,256]{1,0:T(8,128)(2,1)S(1)} %get-tuple-element.34), channel_id=1, source_target_pairs={{0,1},{1,0},{2,3},{3,2},{4,5},{5,4},{6,7},{7,6},{8,9},{9,8},{10,11... | collective-permute-start | bytes 196616 | tf_op jit(solution)/shard_map/ppermute | solution.py:200
  14.3 12.1 %copy-start = (bf16[256,256]{1,0:T(8,128)(2,1)S(1)}, bf16[256,256]{1,0:T(8,128)(2,1)}, u32[]{:S(2)}) copy-start(bf16[256,256]{1,0:T(8,128)(2,1)} %weight_ref.5) | copy-start | bytes 393220
  14.3 9.4 %collective-permute-start.10 = (bf16[272,128]{1,0:T(8,128)(2,1)S(1)}, bf16[272,128]{1,0:T(8,128)(2,1)S(1)}, u32[]{:S(2)}, u32[]{:S(2)}) collective-permute-start(bf16[272,128]{1,0:T(8,128)(2,1)S(1)} %shard_map.99.rest_3_), channel_id=1, source_target_pairs={{0,1},{1,0},{2,3},{3,2},{4,5},{5,4},{6,7},{7,6},{8,9},{9,8},{10,11... | collective-permute-start | bytes 208904 | tf_op jit(solution)/shard_map/ppermute | solution.py:223
  15.8 7.9 %collective-permute-start.11 = (bf16[272,128]{1,0:T(8,128)(2,1)S(1)}, bf16[272,128]{1,0:T(8,128)(2,1)S(1)}, u32[]{:S(2)}, u32[]{:S(2)}) collective-permute-start(bf16[272,128]{1,0:T(8,128)(2,1)S(1)} %collective-permute-done.6.extra), channel_id=1, source_target_pairs={{0,1},{1,0},{2,3},{3,2},{4,5},{5,4},{6,7},{7,6},{8,9},{9,8},{10,11... | collective-permute-start | bytes 208904 | tf_op jit(solution)/shard_map/ppermute | solution.py:223
  19.2 6.7 %collective-permute-start.9 = (bf16[128,256]{1,0:T(8,128)(2,1)S(1)}, bf16[128,256]{1,0:T(8,128)(2,1)S(1)}, u32[]{:S(2)}, u32[]{:S(2)}) collective-permute-start(bf16[128,256]{1,0:T(8,128)(2,1)S(1)} %shard_map.100.rest_0_), channel_id=1, source_target_pairs={{0,3},{1,2},{2,1},{3,0},{4,7},{5,6},{6,5},{7,4},{8,11},{9,10},{10,... | collective-permute-start | bytes 196616 | tf_op jit(solution)/shard_map/ppermute | solution.py:200
  21.7 4.7 %collective-permute-start.8 = (bf16[128,256]{1,0:T(8,128)(2,1)S(1)}, bf16[128,256]{1,0:T(8,128)(2,1)S(1)}, u32[]{:S(2)}, u32[]{:S(2)}) collective-permute-start(bf16[128,256]{1,0:T(8,128)(2,1)S(1)} %shard_map.100.rest_0_), channel_id=1, source_target_pairs={{0,1},{1,0},{2,3},{3,2},{4,5},{5,4},{6,7},{7,6},{8,9},{9,8},{10,11... | collective-permute-start | bytes 196616 | tf_op jit(solution)/shard_map/ppermute | solution.py:200
  21.7 5.5 %collective-permute-start.7 = (bf16[128,256]{1,0:T(8,128)(2,1)S(1)}, bf16[128,256]{1,0:T(8,128)(2,1)S(1)}, u32[]{:S(2)}, u32[]{:S(2)}) collective-permute-start(bf16[128,256]{1,0:T(8,128)(2,1)S(1)} %shard_map.100.rest_0_), channel_id=1, source_target_pairs={{0,2},{1,3},{2,0},{3,1},{4,6},{5,7},{6,4},{7,5},{8,10},{9,11},{10,... | collective-permute-start | bytes 196616 | tf_op jit(solution)/shard_map/ppermute | solution.py:200
  27.7 1.5 %collective-permute-start.12 = (bf16[384,256]{1,0:T(8,128)(2,1)S(1)}, bf16[384,256]{1,0:T(8,128)(2,1)S(1)}, u32[]{:S(2)}, u32[]{:S(2)}) collective-permute-start(bf16[384,256]{1,0:T(8,128)(2,1)S(1)} %get-tuple-element.49), channel_id=1, source_target_pairs={{0,4},{4,0},{8,12},{12,8},{1,5},{5,1},{9,13},{13,9},{2,6},{6,2},{1... | collective-permute-start | bytes 589832 | tf_op jit(solution)/shard_map/ppermute | solution.py:280
  29.2 4.5 %collective-permute-start.14 = (bf16[128,256]{1,0:T(8,128)(2,1)S(1)}, bf16[128,256]{1,0:T(8,128)(2,1)S(1)}, u32[]{:S(2)}, u32[]{:S(2)}) collective-permute-start(bf16[128,256]{1,0:T(8,128)(2,1)S(1)} %get-tuple-element.53.own_ref), channel_id=1, source_target_pairs={{0,8},{4,12},{8,0},{12,4},{1,9},{5,13},{9,1},{13,5},{2,10},{6,14},... | collective-permute-start | bytes 196616 | tf_op jit(solution)/shard_map/ppermute | solution.py:280
  31.0 4.3 %collective-permute-start.13 = (bf16[128,256]{1,0:T(8,128)(2,1)S(1)}, bf16[128,256]{1,0:T(8,128)(2,1)S(1)}, u32[]{:S(2)}, u32[]{:S(2)}) collective-permute-start(bf16[128,256]{1,0:T(8,128)(2,1)S(1)} %get-tuple-element.51), channel_id=1, source_target_pairs={{0,8},{4,12},{8,0},{12,4},{1,9},{5,13},{9,1},{13,5},{2,10},{6,14},... | collective-permute-start | bytes 196616 | tf_op jit(solution)/shard_map/ppermute | solution.py:280
  33.8 1.5 %collective-permute-start.15 = (bf16[128,256]{1,0:T(8,128)(2,1)S(1)}, bf16[128,256]{1,0:T(8,128)(2,1)S(1)}, u32[]{:S(2)}, u32[]{:S(2)}) collective-permute-start(bf16[128,256]{1,0:T(8,128)(2,1)S(1)} %shard_map.104.own_ref), channel_id=1, source_target_pairs={{0,4},{4,0},{8,12},{12,8},{1,5},{5,1},{9,13},{13,9},{2,6},{6,2},{1... | collective-permute-start | bytes 196616 | tf_op jit(solution)/shard_map/ppermute | solution.py:280
